TPU v7x, 256 devices: a whole 4x4x8 slice. The times are simulated.
256 devices in a mesh: panel: 2 (over x_lo), lat: 16 (over z, core), lon: 8 (over y, x_hi).
Axes of the slice: x: 4 (x_hi: 2, x_lo: 2; x = x_hi * 2 + x_lo), y: 4, z: 8, core: 2. Of those that a mesh axis runs over, the one named last changes fastest.
Arguments:
- state: float32 [2, 7, 2, 384, 4608], P('panel', None, None, 'lat', 'lon'), may hold values from -4 to 4
- pack_cell: int32 [2, 16, 8, 48], P('panel', 'lat', 'lon'), may hold values from 0 to 13224, as said below
- pack_frac: float32 [2, 2, 16, 8, 48], P('panel', None, 'lat', 'lon'), may hold values from 0 to 1
- ns_source: int32 [2, 2, 4608], P(None, None, 'lon'), may hold values from 0 to 6143
- we_source: int32 [2, 2, 384], P(None, None, 'lat'), may hold values from 0 to 6143
- ns_turn: float32 [2, 2, 4608], P(None, None, 'lon'), may hold values from -3.140625 to 3.140625
- we_turn: float32 [2, 2, 384], P(None, None, 'lat'), may hold values from -3.140625 to 3.140625
Outputs:
- new_state: float32 [2, 7, 2, 384, 4608], P('panel', None, None, 'lat', 'lon')
Inputs may be any that keep to these rules, and one draw needn't show every extreme that they name: `pack_cell`: donor offsets leave room for the next row and column inside the tile.
All inputs are finite; a program needn't handle non-finite values.
Results may differ from a plain program's by a relative error of at most 0.00002.
Values sent between devices are 32-bit elements; how exact they have to be, the bound alone decides.
No kernel may reach another device: no remote copies, remote signals or barrier semaphores. Data moves between devices by JAX's collectives and lax.ppermute only.
A program may use at most 128 MiB of HBM per device.

v0:
```python
import math

import jax
import jax.numpy as jnp
from jax import lax
from jax.sharding import PartitionSpec as P

time_step = 0.25
viscosity = 0.1
resistivity = 0.08
conduction = 0.12
buoyancy = 0.5
gradient = 0.5


def swapped(value, axis, distance):
    mask = 2**distance
    pairs = [(source, source ^ mask) for source in range(lax.axis_size(axis))]
    return lax.ppermute(value, axis, pairs)


def with_halo(block, sides, width):
    for axis, dim in sides:
        count = lax.axis_size(axis)
        forward = [(i, i + 1) for i in range(count - 1)]
        backward = [(target, source) for source, target in forward]
        low = lax.ppermute(
            lax.slice_in_dim(block, block.shape[dim] - width, None, axis=dim), axis, forward
        )
        high = lax.ppermute(lax.slice_in_dim(block, 0, width, axis=dim), axis, backward)
        block = jnp.concatenate([low, block, high], axis=dim)
    return block


def tendency(ghosted, inv_sine):
    padded = jnp.pad(ghosted, ((0, 0), (1, 1), (0, 0), (0, 0)))
    centre = padded[:, 1:-1, 1:-1, 1:-1]
    above_r = padded[:, 2:, 1:-1, 1:-1]
    below_r = padded[:, :-2, 1:-1, 1:-1]
    north_side = padded[:, 1:-1, :-2, 1:-1]
    south_side = padded[:, 1:-1, 2:, 1:-1]
    west_side = padded[:, 1:-1, 1:-1, :-2]
    east_side = padded[:, 1:-1, 1:-1, 2:]
    metric = inv_sine[None, None, :, None]
    grad_r = 0.5 * (above_r - below_r)
    grad_t = 0.5 * (south_side - north_side)
    grad_p = 0.5 * metric * (east_side - west_side)
    laplace = (
        above_r
        + below_r
        - 2.0 * centre
        + (south_side + north_side - 2.0 * centre)
        + metric * metric * (east_side + west_side - 2.0 * centre)
    )
    by_flow = centre[0:1] * grad_r + centre[1:2] * grad_t + centre[2:3] * grad_p
    by_field = centre[3:4] * grad_r + centre[4:5] * grad_t + centre[5:6] * grad_p
    velocity = -by_flow[0:3] + by_field[3:6] + viscosity * laplace[0:3]
    velocity = velocity.at[0].add(buoyancy * centre[6])
    magnetic = -by_flow[3:6] + by_field[0:3] + resistivity * laplace[3:6]
    thermal = -by_flow[6:7] + conduction * laplace[6:7] + gradient * centre[0:1]
    return jnp.concatenate([velocity, magnetic, thermal], 0)


def rotate(values, angle):
    cosine = jnp.cos(angle)
    sine = jnp.sin(angle)
    return jnp.stack(
        [
            values[0],
            cosine * values[1] - sine * values[2],
            sine * values[1] + cosine * values[2],
            values[3],
            cosine * values[4] - sine * values[5],
            sine * values[4] + cosine * values[5],
            values[6],
        ]
    )


def pick_rim(donated, source, angle, layers):
    taken = jnp.take(donated, source.reshape(-1), axis=1)
    taken = taken.reshape(7, layers, source.shape[0], source.shape[1])
    return rotate(taken, angle)


def make_packet(tile, donor_cell, fractions):
    layers = tile.shape[1]
    rows = tile.shape[2]
    cols = tile.shape[3]
    flat = tile.reshape(7 * layers, rows * cols)
    lat_off = donor_cell // (cols - 1)
    lon_off = donor_cell % (cols - 1)
    start = lat_off * cols + lon_off
    frac_a = fractions[0]
    frac_b = fractions[1]
    return (
        (1.0 - frac_a) * (1.0 - frac_b) * jnp.take(flat, start, axis=1)
        + (1.0 - frac_a) * frac_b * jnp.take(flat, start + 1, axis=1)
        + frac_a * (1.0 - frac_b) * jnp.take(flat, start + cols, axis=1)
        + frac_a * frac_b * jnp.take(flat, start + cols + 1, axis=1)
    )


def on_device(state, pack_cell, pack_frac, ns_source, we_source, ns_turn, we_turn):
    tile = state[0]
    layers = tile.shape[1]
    rows = tile.shape[2]
    donor_cell = pack_cell.reshape(-1)
    fractions = pack_frac.reshape(2, -1)
    lat_index = lax.axis_index("lat")
    lon_index = lax.axis_index("lon")
    panel_index = lax.axis_index("panel")
    lat_count = lax.axis_size("lat")
    lon_count = lax.axis_size("lon")
    row_global = (lat_index * rows + jnp.arange(rows, dtype=jnp.int32)).astype(jnp.float32)
    theta = math.pi / 4 + (row_global + 0.5) * (math.pi / 2) / (rows * lat_count)
    inv_sine = 1.0 / jnp.sin(theta)
    at_north = lat_index == 0
    at_south = lat_index == lat_count - 1
    at_west = lon_index == 0
    at_east = lon_index == lon_count - 1

    def rim_values(section):
        packet = make_packet(section, donor_cell, fractions)
        donated = lax.all_gather(packet, ("lat", "lon"), axis=1, tiled=True)
        other_index = 1 - panel_index
        other_ns = lax.dynamic_index_in_dim(ns_source, other_index, 0, keepdims=False)
        other_we = lax.dynamic_index_in_dim(we_source, other_index, 0, keepdims=False)
        turn_ns = lax.dynamic_index_in_dim(ns_turn, other_index, 0, keepdims=False)
        turn_we = lax.dynamic_index_in_dim(we_turn, other_index, 0, keepdims=False)
        send_ns = pick_rim(donated, other_ns, turn_ns, layers)
        send_we = pick_rim(donated, other_we, turn_we, layers)
        cycle_ns, cycle_we = swapped((send_ns, send_we), "panel", 0)
        return (cycle_ns, cycle_we)

    def evaluate(section):
        cycle_ns, cycle_we = rim_values(section)
        ghosted = with_halo(section, (("lat", 2), ("lon", 3)), 1)
        top_row = jnp.where(at_north, cycle_ns[:, :, 0], ghosted[:, :, 0, 1:-1])
        bottom_row = jnp.where(at_south, cycle_ns[:, :, 1], ghosted[:, :, -1, 1:-1])
        left_col = jnp.where(at_west, cycle_we[:, :, 0], ghosted[:, :, 1:-1, 0])
        right_col = jnp.where(at_east, cycle_we[:, :, 1], ghosted[:, :, 1:-1, -1])
        ghosted = ghosted.at[:, :, 0, 1:-1].set(top_row)
        ghosted = ghosted.at[:, :, -1, 1:-1].set(bottom_row)
        ghosted = ghosted.at[:, :, 1:-1, 0].set(left_col)
        ghosted = ghosted.at[:, :, 1:-1, -1].set(right_col)
        return tendency(ghosted, inv_sine)

    first = evaluate(tile)
    second = evaluate(tile + time_step / 2 * first)
    third = evaluate(tile + time_step / 2 * second)
    fourth = evaluate(tile + time_step * third)
    result = tile + time_step / 6 * (first + 2.0 * second + 2.0 * third + fourth)
    return result[None]


def solution(mesh):
    return jax.shard_map(
        on_device,
        mesh=mesh,
        in_specs=(
            P("panel", None, None, "lat", "lon"),
            P("panel", "lat", "lon", None),
            P("panel", None, "lat", "lon", None),
            P(None, None, "lon"),
            P(None, None, "lat"),
            P(None, None, "lon"),
            P(None, None, "lat"),
        ),
        out_specs=P("panel", None, None, "lat", "lon"),
        check_vma=False,
    )
```

profile of v0, /device:TPU:1, one launch (start us, length us, event | category | flops | bytes accessed | tf_op | source)
XLA Modules:
  0.0 1683.7 jit_solution(14738990233796656321)
XLA Ops:
  3.1 4.3 copy.588
  7.4 3.6 gather_fusion.1
  11.0 3.6 gather_fusion.2
  14.6 3.6 gather_fusion.3
  18.2 3.6 gather_fusion
  22.5 325.2 %all-gather = f32[128,48,14]{1,2,0:T(8,128)S(1)} all-gather(f32[1,48,14]{1,2,0:T(8,128)S(1)} %copy.592), channel_id=1, replica_groups=mesh['panel'=2,'lat'=16,'lon'=8] {'lat','lon'}, dimensions={0}, use_global_device_ids=true | all-gather | bytes 346752 | tf_op jit(solution)/shard_map/all_gather | solution.py:125
  347.8 2.4 copy.593
  350.2 2.5 gather_fusion.5
  356.4 12.9 collective-permute-start.1
  369.5 4.3 gather_fusion.4
  374.1 2.6 fusion.86
  392.2 5.7 collective-permute-start.2
  402.4 3.9 scatter.54
  406.3 2.7 scatter.55
  409.5 2.5 scatter.59
  419.1 4.3 copy.637
  423.4 8.5 add.650
  431.9 3.7 gather_fusion.7
  435.6 3.7 gather_fusion.8
  439.3 3.7 gather_fusion.6
  443.0 3.7 gather_fusion.9
  447.0 318.0 %all-gather.1 = f32[128,48,14]{1,2,0:T(8,128)S(1)} all-gather(f32[1,48,14]{1,2,0:T(8,128)S(1)} %copy.638), channel_id=1, replica_groups=mesh['panel'=2,'lat'=16,'lon'=8] {'lat','lon'}, dimensions={0}, use_global_device_ids=true | all-gather | bytes 346752 | tf_op jit(solution)/shard_map/all_gather | solution.py:125
  765.1 2.4 copy.639
  767.5 2.6 gather_fusion.11
  770.1 4.3 gather_fusion.10
  781.5 12.9 collective-permute-start.7
  794.7 2.7 fusion.85
  817.7 2.5 collective-permute-done.9
  826.7 3.9 scatter.60
  830.6 2.7 scatter.61
  833.8 2.5 scatter.65
  842.1 4.3 copy.681
  846.4 8.5 add.676
  855.0 3.7 gather_fusion.13
  858.7 3.7 gather_fusion.14
  862.4 3.7 gather_fusion.12
  866.1 3.7 gather_fusion.15
  870.1 315.6 %all-gather.2 = f32[128,48,14]{1,2,0:T(8,128)S(1)} all-gather(f32[1,48,14]{1,2,0:T(8,128)S(1)} %copy.682), channel_id=1, replica_groups=mesh['panel'=2,'lat'=16,'lon'=8] {'lat','lon'}, dimensions={0}, use_global_device_ids=true | all-gather | bytes 346752 | tf_op jit(solution)/shard_map/all_gather | solution.py:125
  1185.7 2.4 copy.683
  1188.1 2.7 gather_fusion.17
  1190.7 4.3 gather_fusion.16
  1203.3 13.1 collective-permute-start.13
  1216.7 2.7 fusion.84
  1232.5 3.5 collective-permute-start.14
  1239.2 2.9 collective-permute-done.15
  1248.6 3.9 scatter.66
  1252.5 2.7 scatter.69
  1255.7 2.5 scatter.71
  1264.1 4.3 copy.725
  1268.4 8.6 add.702
  1277.0 3.7 gather_fusion.19
  1280.7 3.7 gather_fusion.20
  1284.4 3.7 gather_fusion.18
  1288.1 3.7 gather_fusion.21
  1292.1 315.3 %all-gather.3 = f32[128,48,14]{1,2,0:T(8,128)S(1)} all-gather(f32[1,48,14]{1,2,0:T(8,128)S(1)} %copy.726), channel_id=1, replica_groups=mesh['panel'=2,'lat'=16,'lon'=8] {'lat','lon'}, dimensions={0}, use_global_device_ids=true | all-gather | bytes 346752 | tf_op jit(solution)/shard_map/all_gather | solution.py:125
  1609.9 2.7 gather_fusion.23
  1612.6 4.3 gather_fusion.22
  1623.9 13.2 collective-permute-start.19
  1637.3 2.7 fusion.83
  1652.5 5.0 collective-permute-start.20
  1660.7 2.9 collective-permute-done.21
  1668.1 3.9 scatter.74
  1672.0 2.7 scatter.75
  1675.2 2.5 scatter.79
  (459 shorter events, 149.3 us)
Async XLA Ops:
  0.0 369.4 %copy-start = (s32[2,2,576]{2,1,0:T(2,128)S(1)}, s32[2,2,576]{2,1,0:T(2,128)}, u32[]{:S(2)}) copy-start(s32[2,2,576]{2,1,0:T(2,128)} %param.56) | copy-start | bytes 27652
  1.5 20.5 %copy-start.78 = (pred[48]{0:T(512)(128)(4,1)}, pred[48]{0:T(512)(128)(4,1)S(1)}, u32[]{:S(2)}) copy-start(pred[48]{0:T(512)(128)(4,1)S(1)} %get-tuple-element.248) | copy-start | bytes 148
  1.5 20.4 %copy-start.37 = (pred[48]{0:T(512)(128)(4,1)}, pred[48]{0:T(512)(128)(4,1)S(1)}, u32[]{:S(2)}) copy-start(pred[48]{0:T(512)(128)(4,1)S(1)} %get-tuple-element.250) | copy-start | bytes 148
  1.5 20.4 %copy-start.41 = (pred[48]{0:T(512)(128)(4,1)}, pred[48]{0:T(512)(128)(4,1)S(1)}, u32[]{:S(2)}) copy-start(pred[48]{0:T(512)(128)(4,1)S(1)} %get-tuple-element.412) | copy-start | bytes 148
  1.5 20.4 %copy-start.45 = (pred[48]{0:T(512)(128)(4,1)}, pred[48]{0:T(512)(128)(4,1)S(1)}, u32[]{:S(2)}) copy-start(pred[48]{0:T(512)(128)(4,1)S(1)} %get-tuple-element.414) | copy-start | bytes 148
  1.5 351.1 %copy-start.33 = (pred[48]{0:T(512)(128)(4,1)}, pred[48]{0:T(512)(128)(4,1)S(1)}, u32[]{:S(2)}) copy-start(pred[48]{0:T(512)(128)(4,1)S(1)} %get-tuple-element.416) | copy-start | bytes 148
  3.0 18.8 %copy-start.83 = (f32[1,2,1,1,48]{4,3,2,1,0:T(1,128)S(1)}, f32[1,2,1,1,48]{4,3,2,1,0:T(1,128)}, u32[]{:S(2)}) copy-start(f32[1,2,1,1,48]{4,3,2,1,0:T(1,128)} %param.55) | copy-start | bytes 1156
  7.4 14.5 copy-start.66
  353.3 16.2 copy-start.21
  353.6 44.2 %collective-permute-start.5 = (f32[7,2,2,24]{3,2,1,0:T(2,128)S(1)}, f32[7,2,2,24]{3,2,1,0:T(2,128)S(1)}, u32[]{:S(2)}, u32[]{:S(2)}) collective-permute-start(f32[7,2,2,24]{3,2,1,0:T(2,128)S(1)} %constant_dynamic-update-slice_fusion.7), channel_id=1, source_target_pairs={{0,128},{128,0},{1,129},{129,1},{2,130},{130,2},{3,131},{131,3},{4... | collective-permute-start | bytes 8072 | tf_op jit(solution)/shard_map/ppermute | solution.py:19
  354.5 35.3 %collective-permute-start = (f32[7,2,1,576]{3,1,2,0:T(2,128)S(1)}, f32[7,2,1,576]{3,1,2,0:T(2,128)S(1)}, u32[]{:S(2)}, u32[]{:S(2)}) collective-permute-start(f32[7,2,1,576]{3,1,2,0:T(2,128)S(1)} %get-tuple-element.322), channel_id=1, source_target_pairs={{0,8},{8,16},{16,24},{24,32},{32,40},{40,48},{48,56},{56,64},{64,7... | collective-permute-start | bytes 96776 | tf_op jit(solution)/shard_map/ppermute | solution.py:27
  356.4 33.4 %collective-permute-start.1 = (f32[7,2,1,576]{3,1,2,0:T(2,128)S(1)}, f32[7,2,1,576]{3,1,2,0:T(2,128)S(1)}, u32[]{:S(2)}, u32[]{:S(2)}) collective-permute-start(f32[7,2,1,576]{3,1,2,0:T(2,128)S(1)} %get-tuple-element.323), channel_id=1, source_target_pairs={{8,0},{16,8},{24,16},{32,24},{40,32},{48,40},{56,48},{64,56},{72,6... | collective-permute-start | bytes 96776 | tf_op jit(solution)/shard_map/ppermute | solution.py:30
  388.0 13.4 collective-permute-start.4
  389.8 22.5 %copy-start.74 = (f32[24]{0:T(128)}, f32[24]{0:T(128)S(1)}, u32[]{:S(2)}) copy-start(f32[24]{0:T(128)S(1)} %get-tuple-element.418) | copy-start | bytes 292
  389.8 23.8 %copy-start.70 = (f32[24]{0:T(128)}, f32[24]{0:T(128)S(1)}, u32[]{:S(2)}) copy-start(f32[24]{0:T(128)S(1)} %get-tuple-element.417) | copy-start | bytes 292
  390.7 7.9 collective-permute-start.3
  392.2 6.3 collective-permute-start.2
  423.3 23.4 %copy-start.38 = (pred[48]{0:T(512)(128)(4,1)S(1)}, pred[48]{0:T(512)(128)(4,1)}, u32[]{:S(2)}) copy-start(pred[48]{0:T(512)(128)(4,1)} %copy-done.37) | copy-start | bytes 148
  423.3 23.4 %copy-start.42 = (pred[48]{0:T(512)(128)(4,1)S(1)}, pred[48]{0:T(512)(128)(4,1)}, u32[]{:S(2)}) copy-start(pred[48]{0:T(512)(128)(4,1)} %copy-done.41) | copy-start | bytes 148
  423.3 23.4 %copy-start.46 = (pred[48]{0:T(512)(128)(4,1)S(1)}, pred[48]{0:T(512)(128)(4,1)}, u32[]{:S(2)}) copy-start(pred[48]{0:T(512)(128)(4,1)} %copy-done.45) | copy-start | bytes 148
  423.3 23.4 %copy-start.50 = (f32[48]{0:T(128)S(1)}, f32[48]{0:T(128)}, u32[]{:S(2)}) copy-start(f32[48]{0:T(128)} %copy-done.49) | copy-start | bytes 580
  423.4 23.4 %copy-start.54 = (f32[48]{0:T(128)S(1)}, f32[48]{0:T(128)}, u32[]{:S(2)}) copy-start(f32[48]{0:T(128)} %copy-done.53) | copy-start | bytes 580
  423.4 23.4 %copy-start.58 = (f32[48]{0:T(128)S(1)}, f32[48]{0:T(128)}, u32[]{:S(2)}) copy-start(f32[48]{0:T(128)} %copy-done.57) | copy-start | bytes 580
  423.4 23.4 %copy-start.62 = (f32[48]{0:T(128)S(1)}, f32[48]{0:T(128)}, u32[]{:S(2)}) copy-start(f32[48]{0:T(128)} %copy-done.61) | copy-start | bytes 580
  423.4 23.4 %copy-start.79 = (pred[48]{0:T(512)(128)(4,1)S(1)}, pred[48]{0:T(512)(128)(4,1)}, u32[]{:S(2)}) copy-start(pred[48]{0:T(512)(128)(4,1)} %copy-done.78) | copy-start | bytes 148
  767.5 27.1 %copy-start.30 = (pred[1152]{0:T(1024)(128)(4,1)S(1)}, pred[1152]{0:T(1024)(128)(4,1)}, u32[]{:S(2)}) copy-start(pred[1152]{0:T(1024)(128)(4,1)} %copy-done.29) | copy-start | bytes 3460
  779.3 41.7 %collective-permute-start.11 = (f32[7,2,2,24]{3,1,0,2:T(2,128)}, f32[7,2,2,24]{3,1,0,2:T(2,128)}, u32[]{:S(2)}, u32[]{:S(2)}) collective-permute-start(f32[7,2,2,24]{3,1,0,2:T(2,128)} %constant_dynamic-update-slice_fusion.21), channel_id=1, source_target_pairs={{0,128},{128,0},{1,129},{129,1},{2,130},{130,2},{3,131},{131,3},{4... | collective-permute-start | bytes 8072 | tf_op jit(solution)/shard_map/ppermute | solution.py:19
  779.6 29.5 %collective-permute-start.6 = (f32[7,2,1,576]{3,1,2,0:T(2,128)S(1)}, f32[7,2,1,576]{3,1,2,0:T(2,128)S(1)}, u32[]{:S(2)}, u32[]{:S(2)}) collective-permute-start(f32[7,2,1,576]{3,1,2,0:T(2,128)S(1)} %get-tuple-element.320), channel_id=1, source_target_pairs={{0,8},{8,16},{16,24},{24,32},{32,40},{40,48},{48,56},{56,64},{64,7... | collective-permute-start | bytes 96776 | tf_op jit(solution)/shard_map/ppermute | solution.py:27
  781.5 27.5 %collective-permute-start.7 = (f32[7,2,1,576]{3,1,2,0:T(2,128)S(1)}, f32[7,2,1,576]{3,1,2,0:T(2,128)S(1)}, u32[]{:S(2)}, u32[]{:S(2)}) collective-permute-start(f32[7,2,1,576]{3,1,2,0:T(2,128)S(1)} %get-tuple-element.321), channel_id=1, source_target_pairs={{8,0},{16,8},{24,16},{32,24},{40,32},{48,40},{56,48},{64,56},{72,6... | collective-permute-start | bytes 96776 | tf_op jit(solution)/shard_map/ppermute | solution.py:30
  811.8 5.0 collective-permute-start.8
  814.2 5.9 collective-permute-start.9
  816.1 9.4 collective-permute-start.10
  846.4 23.4 %copy-start.39 = (pred[48]{0:T(512)(128)(4,1)S(1)}, pred[48]{0:T(512)(128)(4,1)}, u32[]{:S(2)}) copy-start(pred[48]{0:T(512)(128)(4,1)} %copy-done.37) | copy-start | bytes 148
  846.4 23.4 %copy-start.43 = (pred[48]{0:T(512)(128)(4,1)S(1)}, pred[48]{0:T(512)(128)(4,1)}, u32[]{:S(2)}) copy-start(pred[48]{0:T(512)(128)(4,1)} %copy-done.41) | copy-start | bytes 148
  846.4 23.4 %copy-start.47 = (pred[48]{0:T(512)(128)(4,1)S(1)}, pred[48]{0:T(512)(128)(4,1)}, u32[]{:S(2)}) copy-start(pred[48]{0:T(512)(128)(4,1)} %copy-done.45) | copy-start | bytes 148
  846.4 23.4 %copy-start.51 = (f32[48]{0:T(128)S(1)}, f32[48]{0:T(128)}, u32[]{:S(2)}) copy-start(f32[48]{0:T(128)} %copy-done.49) | copy-start | bytes 580
  846.4 23.4 %copy-start.55 = (f32[48]{0:T(128)S(1)}, f32[48]{0:T(128)}, u32[]{:S(2)}) copy-start(f32[48]{0:T(128)} %copy-done.53) | copy-start | bytes 580
  846.4 23.4 %copy-start.59 = (f32[48]{0:T(128)S(1)}, f32[48]{0:T(128)}, u32[]{:S(2)}) copy-start(f32[48]{0:T(128)} %copy-done.57) | copy-start | bytes 580
  846.4 23.4 %copy-start.63 = (f32[48]{0:T(128)S(1)}, f32[48]{0:T(128)}, u32[]{:S(2)}) copy-start(f32[48]{0:T(128)} %copy-done.61) | copy-start | bytes 580
  846.4 23.4 %copy-start.80 = (pred[48]{0:T(512)(128)(4,1)S(1)}, pred[48]{0:T(512)(128)(4,1)}, u32[]{:S(2)}) copy-start(pred[48]{0:T(512)(128)(4,1)} %copy-done.78) | copy-start | bytes 148
  1188.1 13.3 copy-start.8
  1188.1 28.4 %copy-start.31 = (pred[1152]{0:T(1024)(128)(4,1)S(1)}, pred[1152]{0:T(1024)(128)(4,1)}, u32[]{:S(2)}) copy-start(pred[1152]{0:T(1024)(128)(4,1)} %copy-done.29) | copy-start | bytes 3460
  1200.0 43.0 %collective-permute-start.17 = (f32[7,2,2,24]{3,1,0,2:T(2,128)}, f32[7,2,2,24]{3,1,0,2:T(2,128)}, u32[]{:S(2)}, u32[]{:S(2)}) collective-permute-start(f32[7,2,2,24]{3,1,0,2:T(2,128)} %constant_dynamic-update-slice_fusion.35), channel_id=1, source_target_pairs={{0,128},{128,0},{1,129},{129,1},{2,130},{130,2},{3,131},{131,3},{4... | collective-permute-start | bytes 8072 | tf_op jit(solution)/shard_map/ppermute | solution.py:19
  1201.4 29.6 %collective-permute-start.12 = (f32[7,2,1,576]{3,1,2,0:T(2,128)S(1)}, f32[7,2,1,576]{3,1,2,0:T(2,128)S(1)}, u32[]{:S(2)}, u32[]{:S(2)}) collective-permute-start(f32[7,2,1,576]{3,1,2,0:T(2,128)S(1)} %get-tuple-element.316), channel_id=1, source_target_pairs={{0,8},{8,16},{16,24},{24,32},{32,40},{40,48},{48,56},{56,64},{64,7... | collective-permute-start | bytes 96776 | tf_op jit(solution)/shard_map/ppermute | solution.py:27
  1203.3 27.7 %collective-permute-start.13 = (f32[7,2,1,576]{3,1,2,0:T(2,128)S(1)}, f32[7,2,1,576]{3,1,2,0:T(2,128)S(1)}, u32[]{:S(2)}, u32[]{:S(2)}) collective-permute-start(f32[7,2,1,576]{3,1,2,0:T(2,128)S(1)} %get-tuple-element.317), channel_id=1, source_target_pairs={{8,0},{16,8},{24,16},{32,24},{40,32},{48,40},{56,48},{64,56},{72,6... | collective-permute-start | bytes 96776 | tf_op jit(solution)/shard_map/ppermute | solution.py:30
  1232.5 5.8 collective-permute-start.14
  1236.2 5.9 collective-permute-start.15
  1238.1 9.4 collective-permute-start.16
  1268.4 23.5 %copy-start.40 = (pred[48]{0:T(512)(128)(4,1)S(1)}, pred[48]{0:T(512)(128)(4,1)}, u32[]{:S(2)}) copy-start(pred[48]{0:T(512)(128)(4,1)} %copy-done.37) | copy-start | bytes 148
  1268.4 23.5 %copy-start.44 = (pred[48]{0:T(512)(128)(4,1)S(1)}, pred[48]{0:T(512)(128)(4,1)}, u32[]{:S(2)}) copy-start(pred[48]{0:T(512)(128)(4,1)} %copy-done.41) | copy-start | bytes 148
  1268.4 23.5 %copy-start.48 = (pred[48]{0:T(512)(128)(4,1)S(1)}, pred[48]{0:T(512)(128)(4,1)}, u32[]{:S(2)}) copy-start(pred[48]{0:T(512)(128)(4,1)} %copy-done.45) | copy-start | bytes 148
  1268.4 23.5 %copy-start.52 = (f32[48]{0:T(128)S(1)}, f32[48]{0:T(128)}, u32[]{:S(2)}) copy-start(f32[48]{0:T(128)} %copy-done.49) | copy-start | bytes 580
  1268.4 23.5 %copy-start.56 = (f32[48]{0:T(128)S(1)}, f32[48]{0:T(128)}, u32[]{:S(2)}) copy-start(f32[48]{0:T(128)} %copy-done.53) | copy-start | bytes 580
  1268.4 23.5 %copy-start.60 = (f32[48]{0:T(128)S(1)}, f32[48]{0:T(128)}, u32[]{:S(2)}) copy-start(f32[48]{0:T(128)} %copy-done.57) | copy-start | bytes 580
  1268.4 23.5 %copy-start.64 = (f32[48]{0:T(128)S(1)}, f32[48]{0:T(128)}, u32[]{:S(2)}) copy-start(f32[48]{0:T(128)} %copy-done.61) | copy-start | bytes 580
  1268.4 23.5 %copy-start.81 = (pred[48]{0:T(512)(128)(4,1)S(1)}, pred[48]{0:T(512)(128)(4,1)}, u32[]{:S(2)}) copy-start(pred[48]{0:T(512)(128)(4,1)} %copy-done.78) | copy-start | bytes 148
  1609.9 12.0 copy-start.7
  1609.9 27.1 %copy-start.32 = (pred[1152]{0:T(1024)(128)(4,1)S(1)}, pred[1152]{0:T(1024)(128)(4,1)}, u32[]{:S(2)}) copy-start(pred[1152]{0:T(1024)(128)(4,1)} %copy-done.29) | copy-start | bytes 3460
  1621.8 42.6 %collective-permute-start.23 = (f32[7,2,2,24]{3,1,0,2:T(2,128)}, f32[7,2,2,24]{3,1,0,2:T(2,128)}, u32[]{:S(2)}, u32[]{:S(2)}) collective-permute-start(f32[7,2,2,24]{3,1,0,2:T(2,128)} %constant_dynamic-update-slice_fusion.49), channel_id=1, source_target_pairs={{0,128},{128,0},{1,129},{129,1},{2,130},{130,2},{3,131},{131,3},{4... | collective-permute-start | bytes 8072 | tf_op jit(solution)/shard_map/ppermute | solution.py:19
  1621.9 29.7 %collective-permute-start.18 = (f32[7,2,1,576]{3,1,2,0:T(2,128)S(1)}, f32[7,2,1,576]{3,1,2,0:T(2,128)S(1)}, u32[]{:S(2)}, u32[]{:S(2)}) collective-permute-start(f32[7,2,1,576]{3,1,2,0:T(2,128)S(1)} %get-tuple-element.312), channel_id=1, source_target_pairs={{0,8},{8,16},{16,24},{24,32},{32,40},{40,48},{48,56},{56,64},{64,7... | collective-permute-start | bytes 96776 | tf_op jit(solution)/shard_map/ppermute | solution.py:27
  1623.9 27.8 %collective-permute-start.19 = (f32[7,2,1,576]{3,1,2,0:T(2,128)S(1)}, f32[7,2,1,576]{3,1,2,0:T(2,128)S(1)}, u32[]{:S(2)}, u32[]{:S(2)}) collective-permute-start(f32[7,2,1,576]{3,1,2,0:T(2,128)S(1)} %get-tuple-element.313), channel_id=1, source_target_pairs={{8,0},{16,8},{24,16},{32,24},{40,32},{48,40},{56,48},{64,56},{72,6... | collective-permute-start | bytes 96776 | tf_op jit(solution)/shard_map/ppermute | solution.py:30
  1652.5 7.3 collective-permute-start.20
  1657.7 5.9 collective-permute-start.21
  1659.6 7.5 collective-permute-start.22
  (45 other events, 142.0 us)
where the time goes:
time: 1700 us; the launch traced here: 1680 us
  blocking collectives  1270 us (75%)
  local copies, waits for them, and re-layouts  235 us (14%)
  starting transfers between devices  85.5 us (5%)
  other arithmetic  78.6 us (5%)
    all_gather x4, blocking collectives, rim_values(): donated = lax.all_gather(packet, ('lat', 'lon'), axis=1, tiled=True)  1270 us
    ppermute x8, starting transfers between devices, with_halo(): lax.ppermute(lax.slice_in_dim(block, 0, width, axis=dim), axis, backward)  57.3 us
  transfers between devices with their start and end apart: 24, of which 4 were waited for; matrix products, arithmetic and copies ran while one was open for 5% of the time, Pallas kernels for 0%

commit v1 on v0

v1 whole, which is shorter than its diff:
```python
import functools
import math

import jax
import jax.numpy as jnp
from jax import lax
from jax.experimental import pallas as pl
from jax.experimental.pallas import tpu as pltpu
from jax.sharding import Mesh, PartitionSpec as P

time_step = 0.25
viscosity = 0.1
resistivity = 0.08
conduction = 0.12
buoyancy = 0.5
gradient = 0.5

AXES = ("panel", "z", "core", "y", "xh")
SIZES = dict(zip(AXES, (2, 8, 2, 4, 2)))
LAT = ("z", "core")
LON = ("y", "xh")

FIELDS = 14
CT = 24
CP = 576
ROWS = 32
COLS = 640
HALO = 4
SLOTS = 48
NT = 384
LANES = 128
TILES = 128
LANE_TILES = COLS // LANES
LAST = COLS - LANES
VMEM_LIMIT = 24 * 1024 * 1024


def lane_of(shape):
    return lax.broadcasted_iota(jnp.int32, shape, len(shape) - 1)


def row_of(shape):
    return lax.broadcasted_iota(jnp.int32, shape, len(shape) - 2)


def lane_gather(block, index):
    return jnp.take_along_axis(block, index, axis=1, mode="promise_in_bounds")


def build_packet(block_of, index_ref, weight_ref):
    left = lane_of((1, LANES)) < 64
    sums = []
    for f in range(FIELDS):
        total = None
        for t in range(LANE_TILES):
            index = index_ref[t]
            for rb in range(CT // 8):
                term = weight_ref[rb * LANE_TILES + t] * lane_gather(block_of(f, rb, t), index)
                total = term if total is None else total + term
        row = jnp.sum(total, axis=0, keepdims=True)
        sums.append(row + pltpu.roll(row, 64, 1))
    zero = jnp.zeros((1, LANES), jnp.float32)
    rows = [jnp.where(left, sums[f], sums[f + 8] if f + 8 < FIELDS else zero) for f in range(8)]
    return jnp.concatenate(rows, axis=0)


def state_block(state_ref, f, rb, t):
    rows = slice(rb * 8, rb * 8 + 8)
    if t < LANE_TILES - 1:
        return state_ref[f, rows, t * LANES : (t + 1) * LANES]
    half = state_ref[f, rows, LAST:CP]
    return jnp.concatenate([half, jnp.zeros((8, LANES - 64), jnp.float32)], axis=1)


def open_kernel(state_ref, aux_ref, packet_ref, north_ref, south_ref, index_ref, weight_ref):
    shape = (8, LANES)
    lane = lane_of(shape)
    row = row_of(shape)
    cell = jnp.broadcast_to(aux_ref[4:5, 0:LANES], shape)
    frac_u = jnp.broadcast_to(aux_ref[5:6, 0:LANES], shape)
    frac_v = jnp.broadcast_to(aux_ref[6:7, 0:LANES], shape)
    lat_off = jnp.floor((cell + 0.5) * (1.0 / (CP - 1)))
    lon_off = cell - lat_off * (CP - 1)
    lat_off = lat_off.astype(jnp.int32)
    second = lane >= 64
    column = lon_off.astype(jnp.int32) + second.astype(jnp.int32)
    used = (lane & 63) < SLOTS
    along = jnp.where(second, frac_v, 1.0 - frac_v)
    for t in range(LANE_TILES):
        local = column - t * LANES
        inside = used & (local >= 0) & (local < LANES)
        index_ref[t] = jnp.where(inside, local, 0)
        for rb in range(CT // 8):
            here = row + rb * 8
            down = jnp.where(here == lat_off, 1.0 - frac_u, jnp.where(here == lat_off + 1, frac_u, 0.0))
            weight_ref[rb * LANE_TILES + t] = jnp.where(inside, down * along, 0.0)
    packet_ref[...] = build_packet(functools.partial(state_block, state_ref), index_ref, weight_ref)
    upper = row_of((8, COLS)) < HALO
    for c in range(7):
        for t in range(LANE_TILES):
            cols = slice(t * LANES, (t + 1) * LANES)
            top = [state_block(state_ref, 2 * c + k, 0, t) for k in range(2)]
            end = [state_block(state_ref, 2 * c + k, CT // 8 - 1, t) for k in range(2)]
            north_ref[c, :, cols] = jnp.where(row < HALO, top[0], pltpu.roll(top[1], HALO, 0))
            south_ref[c, :, cols] = jnp.where(row < HALO, pltpu.roll(end[0], HALO, 0), end[1])
    north_ref[7] = aux_ref[...]
    south_ref[7] = aux_ref[...]


def outer_rows(from_south, from_north, k, row):
    if k == 0:
        return jnp.where(row < HALO, from_south, pltpu.roll(from_north, HALO, 0))
    return jnp.where(row < HALO, pltpu.roll(from_south, HALO, 0), from_north)


def side_kernel(state_ref, from_south_ref, from_north_ref, aux_ref, west_ref, east_ref):
    shape = (8, LANES)
    lane = lane_of(shape)
    row = row_of(shape)
    for rb in range(ROWS // 8):
        west = jnp.zeros(shape, jnp.float32)
        east = jnp.zeros(shape, jnp.float32)
        for f in range(FIELDS):
            c, k = f // 2, f % 2
            if rb < CT // 8:
                first = state_block(state_ref, f, rb, 0)
                last = state_block(state_ref, f, rb, LANE_TILES - 1)
            else:
                first = outer_rows(from_south_ref[c, :, 0:LANES], from_north_ref[c, :, 0:LANES], k, row)
                last = outer_rows(from_south_ref[c, :, LAST:COLS], from_north_ref[c, :, LAST:COLS], k, row)
            here = (lane >= 8 * f) & (lane < 8 * f + HALO)
            west = jnp.where(here, pltpu.roll(first, 8 * f, 1) if f else first, west)
            east = jnp.where(here, pltpu.roll(last, (8 * f - 60) % LANES, 1), east)
        if rb == 0:
            here = (lane >= 112) & (lane < 112 + HALO)
            west = jnp.where(here, pltpu.roll(aux_ref[:, 0:LANES], 112, 1), west)
            east = jnp.where(here, pltpu.roll(aux_ref[:, LAST:COLS], 112 - 60, 1), east)
        west_ref[rb * 8 : rb * 8 + 8, :] = west
        east_ref[rb * 8 : rb * 8 + 8, :] = east


def frame_kernel(
    flags_ref, state_ref, from_south_ref, from_north_ref, from_east_ref, from_west_ref, aux_ref,
    full_ref, slot_ref, tile_ref, cos_ref, sin_ref, metric_ref,
):
    shape = (8, LANES)
    lane = lane_of(shape)
    row = row_of(shape)
    for rb in range(ROWS // 8):
        rows = slice(rb * 8, rb * 8 + 8)
        from_east = from_east_ref[rows, :]
        from_west = from_west_ref[rows, :]
        for f in range(FIELDS):
            c, k = f // 2, f % 2
            for t in range(LANE_TILES):
                cols = slice(t * LANES, (t + 1) * LANES)
                if rb < CT // 8:
                    block = state_block(state_ref, f, rb, t)
                else:
                    block = outer_rows(from_south_ref[c, :, cols], from_north_ref[c, :, cols], k, row)
                if t == LANE_TILES - 1:
                    block = jnp.where((lane >= 64) & (lane < 64 + HALO), pltpu.roll(from_east, (64 - 8 * f) % LANES, 1), block)
                    block = jnp.where(lane >= LANES - HALO, pltpu.roll(from_west, (124 - 8 * f) % LANES, 1), block)
                full_ref[f, rows, cols] = block
    mine = flags_ref[2]
    for t in range(LANE_TILES + 1):
        if t < LANE_TILES:
            block = aux_ref[:, t * LANES : (t + 1) * LANES]
            if t == LANE_TILES - 1:
                east = from_east_ref[0:8, :]
                west = from_west_ref[0:8, :]
                block = jnp.where((lane >= 64) & (lane < 64 + HALO), pltpu.roll(east, (64 - 112) % LANES, 1), block)
                block = jnp.where(lane >= LANES - HALO, pltpu.roll(west, 124 - 112, 1), block)
            source = jnp.broadcast_to(block[0:1, :], shape)
            angle = jnp.broadcast_to(block[1:2, :], shape)
        else:
            block = aux_ref[:, 0:LANES]
            block = jnp.where((lane >= CT) & (lane < CT + HALO), pltpu.roll(from_south_ref[7, :, 0:LANES], CT, 1), block)
            block = jnp.where((lane >= 28) & (lane < 32), pltpu.roll(from_north_ref[7, :, 0:LANES], 8, 1), block)
            source = jnp.broadcast_to(block[2:3, :], shape)
            angle = jnp.broadcast_to(block[3:4, :], shape)
        whole = jnp.floor((source + 0.5) * (1.0 / SLOTS))
        slot_ref[t] = (source - whole * SLOTS).astype(jnp.int32)
        tile_ref[t] = whole.astype(jnp.int32) ^ mine
        cos_ref[t] = jnp.cos(angle)
        sin_ref[t] = jnp.sin(angle)
    line = row_of((ROWS, LANES))
    line = jnp.where(line >= ROWS - HALO, line - ROWS, line) + flags_ref[0] * CT
    theta = math.pi / 4 + (line.astype(jnp.float32) + 0.5) * ((math.pi / 2) / NT)
    metric_ref[...] = 1.0 / jnp.sin(theta)


def pick_ghosts(donor_ref, slot_ref, tile_ref, cos_ref, sin_ref):
    shape = (8, LANES)
    row = row_of(shape)
    count = LANE_TILES + 1
    slots = [slot_ref[t] for t in range(count)]
    tiles = [tile_ref[t] for t in range(count)]
    low = [jnp.zeros(shape, jnp.float32) for _ in range(count)]
    high = [jnp.zeros(shape, jnp.float32) for _ in range(count)]
    for v in range(TILES):
        z, core, y, x = v // 16, v // 8 % 2, v // 2 % 4, v % 2
        block = donor_ref[core, z * 4 + y, x]
        for t in range(count):
            here = tiles[t] == v
            low[t] = jnp.where(here, lane_gather(block, slots[t]), low[t])
            high[t] = jnp.where(here, lane_gather(block, slots[t] + 64), high[t])
    ghosts = []
    for t in range(count):
        cosine, sine = cos_ref[t], sin_ref[t]
        first = (row == 2) | (row == 3)
        other = (row == 4) | (row == 5)
        mate = jnp.where(first, pltpu.roll(low[t], 6, 0), pltpu.roll(low[t], 2, 0))
        turn = jnp.where(first, -sine, sine)
        a = jnp.where(first | other, cosine * low[t] + turn * mate, low[t])
        first = row < 2
        mate = jnp.where(first, pltpu.roll(high[t], 6, 0), pltpu.roll(high[t], 2, 0))
        turn = jnp.where(first, -sine, sine)
        b = jnp.where(row < 4, cosine * high[t] + turn * mate, high[t])
        ghosts.append((a, b))
    return ghosts


def put_ghosts(flags_ref, work_ref, ghosts):
    lat, lon = flags_ref[0], flags_ref[1]

    def put_row(line):
        for f in range(FIELDS):
            for t in range(LANE_TILES):
                work_ref[f, line : line + 1, t * LANES : (t + 1) * LANES] = ghosts[t][f // 8][f % 8 : f % 8 + 1, :]

    def put_column(place):
        shape = (ROWS, LANES)
        lane = lane_of(shape)
        diagonal = lane == row_of(shape)
        for f in range(FIELDS):
            values = jnp.broadcast_to(ghosts[LANE_TILES][f // 8][f % 8 : f % 8 + 1, :], shape)
            column = jnp.sum(jnp.where(diagonal, values, 0.0), axis=1, keepdims=True)
            work_ref[f, :, LAST:COLS] = jnp.where(lane == place, jnp.broadcast_to(column, shape), work_ref[f, :, LAST:COLS])

    pl.when(lat == 0)(lambda: put_row(ROWS - 1))
    pl.when(lat == NT // CT - 1)(lambda: put_row(CT))
    pl.when(lon == 0)(lambda: put_column(LANES - 1))
    pl.when(lon == 7)(lambda: put_column(CP - LAST))


def tendency(work_ref, metric_ref, rb, k, emit):
    low = rb * 8
    rows = slice(low, low + 8)
    shape = (8, COLS)
    row = row_of(shape)
    metric = jnp.concatenate([metric_ref[rows, :]] * LANE_TILES, axis=1)
    square = metric * metric
    centre_weight = 4.0 + 2.0 * square
    radial = 0.5 if k == 0 else -0.5

    def value(c):
        return work_ref[2 * c + k, rows, :]

    def coefficients(c):
        return radial * value(c), 0.5 * value(c + 1), (0.5 * metric) * value(c + 2)

    flow_by = coefficients(0)
    field_by = coefficients(3)

    def parts(c):
        f = 2 * c + k
        centre = value(c)
        across = work_ref[2 * c + 1 - k, rows, :]
        before = (low - 1) % ROWS
        after = (low + 8) % ROWS
        north = jnp.where(row == 0, jnp.broadcast_to(work_ref[f, before : before + 1, :], shape), pltpu.roll(centre, 1, 0))
        south = jnp.where(row == 7, jnp.broadcast_to(work_ref[f, after : after + 1, :], shape), pltpu.roll(centre, 7, 0))
        west = pltpu.roll(centre, 1, 1)
        east = pltpu.roll(centre, COLS - 1, 1)
        grad_t = south - north
        grad_p = east - west
        laplace = across + (south + north) + square * (east + west) - centre_weight * centre
        return across, grad_t, grad_p, laplace

    def along(by, p):
        return by[0] * p[0] + by[1] * p[1] + by[2] * p[2]

    for c in range(3):
        p = parts(c)
        u_flow, u_field, u_laplace = along(flow_by, p), along(field_by, p), p[3]
        p = parts(c + 3)
        velocity = along(field_by, p) - u_flow + viscosity * u_laplace
        if c == 0:
            velocity = velocity + buoyancy * value(6)
        emit(c, velocity)
        emit(c + 3, u_field - along(flow_by, p) + resistivity * p[3])
    p = parts(6)
    emit(6, conduction * p[3] - along(flow_by, p) + gradient * value(0))


def stage_kernel(
    factor, flags_ref, donor_ref, slot_ref, tile_ref, cos_ref, sin_ref, metric_ref, index_ref, weight_ref, full_ref, now_ref,
    next_ref, packet_ref, work_ref,
):
    work_ref[...] = now_ref[...]
    put_ghosts(flags_ref, work_ref, pick_ghosts(donor_ref, slot_ref, tile_ref, cos_ref, sin_ref))
    for rb in range(ROWS // 8):
        rows = slice(rb * 8, rb * 8 + 8)
        for k in range(2):

            def emit(c, value):
                next_ref[2 * c + k, rows, :] = full_ref[2 * c + k, rows, :] + factor * value

            tendency(work_ref, metric_ref, rb, k, emit)

    def block_of(f, rb, t):
        return next_ref[f, rb * 8 : rb * 8 + 8, t * LANES : (t + 1) * LANES]

    packet_ref[...] = build_packet(block_of, index_ref, weight_ref)


def last_kernel(
    flags_ref, donor_ref, slot_ref, tile_ref, cos_ref, sin_ref, metric_ref, full_ref, second_ref, third_ref, fourth_ref,
    out_ref, work_ref,
):
    work_ref[...] = fourth_ref[...]
    put_ghosts(flags_ref, work_ref, pick_ghosts(donor_ref, slot_ref, tile_ref, cos_ref, sin_ref))
    for rb in range(CT // 8):
        rows = slice(rb * 8, rb * 8 + 8)
        for k in range(2):

            def emit(c, value):
                f = 2 * c + k
                base = second_ref[f, rows, :] + 2.0 * third_ref[f, rows, :] + fourth_ref[f, rows, :] - full_ref[f, rows, :]
                out_ref[f, rows, :] = ((1.0 / 3.0) * base + (time_step / 6) * value)[:, :CP]

            tendency(work_ref, metric_ref, rb, k, emit)


def call(kernel, ins, outs, scratch=(), flags=False):
    vmem = pl.BlockSpec(memory_space=pltpu.VMEM)
    specs = [vmem] * len(ins)
    if flags:
        specs[0] = pl.BlockSpec(memory_space=pltpu.SMEM)
    shapes = tuple(jax.ShapeDtypeStruct(s, d) for s, d in outs)
    return pl.pallas_call(
        kernel,
        out_shape=shapes,
        in_specs=specs,
        out_specs=(vmem,) * len(outs),
        scratch_shapes=list(scratch),
        compiler_params=pltpu.CompilerParams(vmem_limit_bytes=VMEM_LIMIT),
    )(*ins)


def coordinates(axes):
    points = [()]
    for a in axes:
        points = [q + (i,) for q in points for i in range(SIZES[a])]
    return points


def permute(value, axes, move):
    points = coordinates(axes)
    place = {q: i for i, q in enumerate(points)}
    pairs = []
    for q in points:
        to = move(q)
        if to is not None:
            pairs.append((place[q], place[to]))
    return lax.ppermute(value, axes if len(axes) > 1 else axes[0], pairs)


def shifted(value, axes, step):
    inner = SIZES[axes[1]]
    count = SIZES[axes[0]] * inner

    def move(q):
        to = q[0] * inner + q[1] + step
        return (to // inner, to % inner) if 0 <= to < count else None

    return permute(value, axes, move)


def gather_packets(packet):
    same = permute(packet, ("panel", "xh"), lambda q: (1 - q[0], q[1]))
    other = permute(packet, ("panel", "xh"), lambda q: (1 - q[0], 1 - q[1]))
    both = jnp.stack([same, other])
    count = SIZES["z"] * SIZES["y"]
    spread = lax.all_to_all(jnp.broadcast_to(both[None], (count,) + both.shape), ("z", "y"), 0, 0)
    return lax.all_gather(spread, "core")


def on_device(state, pack_cell, pack_frac, ns_source, we_source, ns_turn, we_turn):
    f32 = jnp.float32
    tile = state.reshape(FIELDS, CT, CP)
    lat = lax.axis_index(LAT)
    lon = lax.axis_index(LON)
    panel = lax.axis_index("panel")
    flags = jnp.stack([lat, lon, lax.axis_index("xh")]).astype(jnp.int32)
    side_ns = (lat == SIZES["z"] * SIZES["core"] - 1).astype(jnp.int32)
    side_we = (lon == SIZES["y"] * SIZES["xh"] - 1).astype(jnp.int32)

    def chosen(table, side):
        line = lax.dynamic_slice(table, (panel, side, 0), (1, 1, table.shape[2]))[0].astype(f32)
        return jnp.pad(line, ((0, 0), (0, COLS - line.shape[1])))

    def doubled(line):
        line = line.reshape(1, SLOTS).astype(f32)
        return jnp.pad(line, ((0, 0), (0, COLS - SLOTS))) + jnp.pad(line, ((0, 0), (64, COLS - 64 - SLOTS)))

    fractions = pack_frac.reshape(2, SLOTS)
    aux = jnp.concatenate(
        [
            chosen(ns_source, side_ns),
            chosen(ns_turn, side_ns),
            chosen(we_source, side_we),
            chosen(we_turn, side_we),
            doubled(pack_cell),
            doubled(fractions[0]),
            doubled(fractions[1]),
            jnp.zeros((1, COLS), f32),
        ],
        axis=0,
    )
    vreg = (8, LANES)
    full_shape = (FIELDS, ROWS, COLS)
    message = (8, 8, COLS)
    packet, to_north, to_south, index, weight = call(
        open_kernel,
        [tile, aux],
        [(vreg, f32), (message, f32), (message, f32), ((LANE_TILES,) + vreg, jnp.int32), ((3 * LANE_TILES,) + vreg, f32)],
    )
    from_south = shifted(to_north, LAT, -1)
    from_north = shifted(to_south, LAT, 1)
    donors = gather_packets(packet)
    to_west, to_east = call(side_kernel, [tile, from_south, from_north, aux], [((ROWS, LANES), f32)] * 2)
    from_east = shifted(to_west, LON, -1)
    from_west = shifted(to_east, LON, 1)
    points = (LANE_TILES + 1,) + vreg
    full, slot, where, cosine, sine, metric = call(
        frame_kernel,
        [flags, tile, from_south, from_north, from_east, from_west, aux],
        [(full_shape, f32), (points, jnp.int32), (points, jnp.int32), (points, f32), (points, f32), ((ROWS, LANES), f32)],
        flags=True,
    )
    ghost_tables = [slot, where, cosine, sine, metric]
    work = [pltpu.VMEM(full_shape, f32)]
    states = [full]
    for factor in (time_step / 2, time_step / 2, time_step):
        after, packet = call(
            functools.partial(stage_kernel, factor),
            [flags, donors] + ghost_tables + [index, weight, full, states[-1]],
            [(full_shape, f32), (vreg, f32)],
            work,
            flags=True,
        )
        states.append(after)
        donors = gather_packets(packet)
    (result,) = call(
        last_kernel, [flags, donors] + ghost_tables + states, [((FIELDS, CT, CP), f32)], work, flags=True
    )
    return result.reshape(state.shape)


def solution(mesh):
    fine = Mesh(mesh.devices.reshape(tuple(SIZES[a] for a in AXES)), AXES)
    return jax.shard_map(
        on_device,
        mesh=fine,
        in_specs=(
            P("panel", None, None, LAT, LON),
            P("panel", LAT, LON, None),
            P("panel", None, LAT, LON, None),
            P(None, None, LON),
            P(None, None, LAT),
            P(None, None, LON),
            P(None, None, LAT),
        ),
        out_specs=P("panel", None, None, LAT, LON),
        check_vma=False,
    )
```

time: 1700 us -> 156 us (0.09)
  blocking collectives: 1270 us -> 68.6 us
  local copies, waits for them, and re-layouts: 235 us -> 3.39 us
  other arithmetic: 78.6 us -> 2.29 us
  starting transfers between devices: 85.5 us -> 34.4 us
  Pallas kernels: 0 us -> 32.8 us
    all_gather x4, blocking collectives: 1270 us -> 18.8 us  [gather_packets(): return lax.all_gather(spread, 'core')]
    gather x24 -> x0, local copies, waits for them, and re-layouts: 86.7 us -> none  [the longest x8 27.7 us: pick_rim(): taken = jnp.take(donated, source.reshape(-1), axis=1)]
    ppermute x24 -> x12, starting transfers between devices: 85.5 us -> 23 us  [permute(): return lax.ppermute(value, axes if len(axes) > 1 else axes[0], pairs)]
    all_to_all x0 -> x3, blocking collectives: none -> 49.7 us  [gather_packets(): lax.all_to_all(jnp.broadcast_to(both[None], (count,) + both.shape), ('z',...]
    scatter x16 -> x0, local copies, waits for them, and re-layouts: 38.2 us -> none  [the longest x4 15.5 us: evaluate(): ghosted = ghosted.at[:, :, 0, 1:-1].set(top_row)]
    add x17 -> x2, other arithmetic: 37.4 us -> 0.15 us  [doubled(): jnp.pad(line, ((0, 0), (0, COLS - SLOTS)))]
    pallas_call x0 -> x7, Pallas kernels: none -> 32.8 us  [call(): pl.pallas_call(kernel, out_shape=shapes, in_specs=specs, out_specs=(vmem,...]
    slice x41 -> x1, local copies, waits for them, and re-layouts: 24.4 us -> 0.67 us  [on_device(): fractions[1]]
  transfers between devices with their start and end apart: 24 -> 13, of which waited for: 4 -> 9; matrix products, arithmetic and copies ran while one was open for 5% -> 0% of each run, Pallas kernels for 0% -> 1%
where the time goes in v1:
time: 156 us; the launch traced here: 155 us
  blocking collectives  68.6 us (44%)
  starting transfers between devices  34.4 us (22%)
  Pallas kernels  32.8 us (21%)
  waiting for transfers between devices  13.7 us (9%)
  local copies, waits for them, and re-layouts  3.39 us (2%)
  other arithmetic  2.29 us (1%)
    all_to_all x3, blocking collectives, gather_packets(): lax.all_to_all(jnp.broadcast_to(both[None], (count,) + both.shape), ('z',...  49.7 us
    pallas_call x7, Pallas kernels, call(): pl.pallas_call(kernel, out_shape=shapes, in_specs=specs, out_specs=(vmem,...  32.8 us
    ppermute x12, starting transfers between devices, permute(): return lax.ppermute(value, axes if len(axes) > 1 else axes[0], pairs)  23 us
    all_gather x4, blocking collectives, gather_packets(): return lax.all_gather(spread, 'core')  18.8 us
    ppermute x12, waiting for transfers between devices, permute(): return lax.ppermute(value, axes if len(axes) > 1 else axes[0], pairs)  13.7 us
    all_to_all x1, starting transfers between devices, gather_packets(): lax.all_to_all(jnp.broadcast_to(both[None], (count,) + both.shape), ('z',...  11.4 us
  transfers between devices with their start and end apart: 13, of which 9 were waited for; matrix products, arithmetic and copies ran while one was open for 0% of the time, Pallas kernels for 1%

profile of v1, /device:TPU:1, one launch (start us, length us, event | category | flops | bytes accessed | tf_op | source)
XLA Modules:
  0.0 155.3 jit_solution(11364124075747401872)
XLA Ops:
  0.0 0.0 copy-start
  0.0 0.7 convert_bitcast_fusion.1
  0.7 0.7 fusion.1
  1.4 0.7 fusion.2
  2.0 0.7 slice_bitcast_fusion
  2.7 0.1 pad_add_fusion.2
  2.8 0.7 convert_bitcast_fusion
  3.5 0.0 copy-done
  3.6 0.1 pad_add_fusion
  3.7 0.0 copy-start.1
  3.7 1.1 copy-done.1
  4.8 0.0 copy-start.2
  4.8 1.2 shard_map.73
  6.0 3.4 %collective-permute-start.1 = (f32[8,128]{1,0:T(8,128)S(1)}, f32[8,128]{1,0:T(8,128)S(1)}, u32[]{:S(2)}, u32[]{:S(2)}) collective-permute-start(f32[8,128]{1,0:T(8,128)S(1)} %get-tuple-element.24), channel_id=1, source_target_pairs={{0,129},{1,128},{128,1},{129,0},{2,131},{3,130},{130,3},{131,2},{4... | collective-permute-start | bytes 12296 | tf_op jit(solution)/shard_map/ppermute | solution.py:367
  9.4 0.0 collective-permute-start
  9.4 1.0 collective-permute-done.1
  10.4 1.5 collective-permute-done
  11.8 0.7 broadcast_in_dim.11
  12.6 11.4 %all-to-all-start = ((f32[32,2,8,128]{3,2,1,0:T(8,128)}), f32[32,2,8,128]{3,2,1,0:T(8,128)S(1)}, u32[]{:S(2)}, u32[]{:S(2)}) async-start(f32[32,2,8,128]{3,2,1,0:T(8,128)} %broadcast_in_dim.11), calls=%async_computation | async-start | bytes 524288 | tf_op jit(solution)/shard_map/all_to_all | solution.py:386
  23.9 4.1 %collective-permute-start.2 = (f32[8,8,640]{2,1,0:T(8,128)S(1)}, f32[8,8,640]{2,1,0:T(8,128)S(1)}, u32[]{:S(2)}, u32[]{:S(2)}) collective-permute-start(f32[8,8,640]{2,1,0:T(8,128)S(1)} %get-tuple-element.25), channel_id=1, source_target_pairs={{8,0},{16,8},{24,16},{32,24},{40,32},{48,40},{56,48},{64,56},{72,6... | collective-permute-start | bytes 491528 | tf_op jit(solution)/shard_map/ppermute | solution.py:367
  28.1 3.3 %collective-permute-start.3 = (f32[8,8,640]{2,1,0:T(8,128)S(1)}, f32[8,8,640]{2,1,0:T(8,128)S(1)}, u32[]{:S(2)}, u32[]{:S(2)}) collective-permute-start(f32[8,8,640]{2,1,0:T(8,128)S(1)} %get-tuple-element.26), channel_id=1, source_target_pairs={{0,8},{8,16},{16,24},{24,32},{32,40},{40,48},{48,56},{56,64},{64,7... | collective-permute-start | bytes 491528 | tf_op jit(solution)/shard_map/ppermute | solution.py:367
  31.4 2.7 %collective-permute-done.2.from_south_ref = f32[8,8,640]{2,1,0:T(8,128)S(1)} collective-permute-done((f32[8,8,640]{2,1,0:T(8,128)S(1)}, f32[8,8,640]{2,1,0:T(8,128)S(1)}, u32[]{:S(2)}, u32[]{:S(2)}) %collective-permute-start.2) | collective-permute-done | bytes 163872 | tf_op jit(solution)/shard_map/ppermute | solution.py:367
  34.1 0.0 collective-permute-done.3.from_north_ref
  34.1 0.0 copy-done.2
  34.1 0.2 shard_map.74
  34.3 1.3 collective-permute-start.4
  35.6 5.5 %collective-permute-start.5 = (f32[32,128]{1,0:T(8,128)S(1)}, f32[32,128]{1,0:T(8,128)S(1)}, u32[]{:S(2)}, u32[]{:S(2)}) collective-permute-start(f32[32,128]{1,0:T(8,128)S(1)} %get-tuple-element.28), channel_id=1, source_target_pairs={{0,1},{1,2},{2,3},{3,4},{4,5},{5,6},{6,7},{8,9},{9,10},{10,11},{11... | collective-permute-start | bytes 49160 | tf_op jit(solution)/shard_map/ppermute | solution.py:367
  41.1 0.1 pad_add_fusion.3.flags_ref
  41.2 0.0 collective-permute-done.4.from_east_ref
  41.2 0.8 collective-permute-done.5.from_west_ref
  41.9 0.8 shard_map.75
  42.7 0.0 all-to-all-done
  42.8 2.2 %all-gather = f32[64,2,8,128]{3,2,1,0:T(8,128)S(1)} all-gather(f32[32,2,8,128]{3,2,1,0:T(8,128)S(1)} %all-to-all-done), channel_id=2, replica_groups=mesh['panel'=2,'z'=8,'core'=2,'y'=4,'xh'=2] {'core'}, dimensions={0}, use_global_device_ids=true | all-gather | bytes 786432 | tf_op jit(solution)/shard_map/all_gather | solution.py:387
  44.9 7.8 %shard_map.76 = (f32[14,32,640]{2,1,0:T(8,128)S(1)}, f32[8,128]{1,0:T(8,128)S(1)}) custom-call(s32[3]{0:T(128)S(1)} %pad_add_fusion.3.flags_ref, f32[2,32,2,8,128]{4,3,2,1,0:T(8,128)S(1)} %bitcast.36, s32[6,8,128]{2,1,0:T(8,128)S(1)} %get-tuple-element.29.slot_ref, s32[6,8,128]{2,1,0:T(8,128)S(1)} %get-tuple-element.30.tile_ref, ...), custom_call_target="tpu_custom_call" | custom-call | tf_op jit(solution)/shard_map/pallas_call | solution.py:342
  52.7 2.5 %collective-permute-start.7 = (f32[8,128]{1,0:T(8,128)S(1)}, f32[8,128]{1,0:T(8,128)S(1)}, u32[]{:S(2)}, u32[]{:S(2)}) collective-permute-start(f32[8,128]{1,0:T(8,128)S(1)} %get-tuple-element.37), channel_id=1, source_target_pairs={{0,129},{1,128},{128,1},{129,0},{2,131},{3,130},{130,3},{131,2},{4... | collective-permute-start | bytes 12296 | tf_op jit(solution)/shard_map/ppermute | solution.py:367
  55.2 0.3 collective-permute-start.6
  55.5 0.9 collective-permute-done.7
  56.4 1.3 collective-permute-done.6
  57.7 22.9 %all_to_all.20 = f32[32,2,8,128]{3,2,1,0:T(8,128)S(1)} all-to-all(f32[32,2,8,128]{3,2,1,0:T(8,128)S(1)} %broadcast_in_dim.12), channel_id=1, replica_groups=mesh['panel'=2,'z'=8,'core'=2,'y'=4,'xh'=2] {'z','y'}, dimensions={0} | all-to-all | bytes 524288 | tf_op jit(solution)/shard_map/all_to_all | solution.py:386
  80.6 5.6 %all-gather.1 = f32[64,2,8,128]{3,2,1,0:T(8,128)S(1)} all-gather(f32[32,2,8,128]{3,2,1,0:T(8,128)S(1)} %all_to_all.20), channel_id=3, replica_groups=mesh['panel'=2,'z'=8,'core'=2,'y'=4,'xh'=2] {'core'}, dimensions={0}, use_global_device_ids=true | all-gather | bytes 786432 | tf_op jit(solution)/shard_map/all_gather | solution.py:387
  86.1 7.9 %shard_map.77 = (f32[14,32,640]{2,1,0:T(8,128)S(1)}, f32[8,128]{1,0:T(8,128)S(1)}) custom-call(s32[3]{0:T(128)S(1)} %pad_add_fusion.3.flags_ref, f32[2,32,2,8,128]{4,3,2,1,0:T(8,128)S(1)} %bitcast.37, s32[6,8,128]{2,1,0:T(8,128)S(1)} %get-tuple-element.29.slot_ref, s32[6,8,128]{2,1,0:T(8,128)S(1)} %get-tuple-element.30.tile_ref, ...), custom_call_target="tpu_custom_call" | custom-call | tf_op jit(solution)/shard_map/pallas_call | solution.py:342
  94.1 1.7 %collective-permute-start.9 = (f32[8,128]{1,0:T(8,128)S(1)}, f32[8,128]{1,0:T(8,128)S(1)}, u32[]{:S(2)}, u32[]{:S(2)}) collective-permute-start(f32[8,128]{1,0:T(8,128)S(1)} %get-tuple-element.39), channel_id=1, source_target_pairs={{0,129},{1,128},{128,1},{129,0},{2,131},{3,130},{130,3},{131,2},{4... | collective-permute-start | bytes 12296 | tf_op jit(solution)/shard_map/ppermute | solution.py:367
  95.8 0.0 collective-permute-start.8
  95.8 2.0 %collective-permute-done.9 = f32[8,128]{1,0:T(8,128)S(1)} collective-permute-done((f32[8,128]{1,0:T(8,128)S(1)}, f32[8,128]{1,0:T(8,128)S(1)}, u32[]{:S(2)}, u32[]{:S(2)}) %collective-permute-start.9) | collective-permute-done | bytes 4128 | tf_op jit(solution)/shard_map/ppermute | solution.py:367
  97.8 0.7 collective-permute-done.8
  98.6 13.5 %all_to_all.21 = f32[32,2,8,128]{3,2,1,0:T(8,128)S(1)} all-to-all(f32[32,2,8,128]{3,2,1,0:T(8,128)S(1)} %broadcast_in_dim.13), channel_id=1, replica_groups=mesh['panel'=2,'z'=8,'core'=2,'y'=4,'xh'=2] {'z','y'}, dimensions={0} | all-to-all | bytes 524288 | tf_op jit(solution)/shard_map/all_to_all | solution.py:386
  112.1 5.6 %all-gather.2 = f32[64,2,8,128]{3,2,1,0:T(8,128)S(1)} all-gather(f32[32,2,8,128]{3,2,1,0:T(8,128)S(1)} %all_to_all.21), channel_id=4, replica_groups=mesh['panel'=2,'z'=8,'core'=2,'y'=4,'xh'=2] {'core'}, dimensions={0}, use_global_device_ids=true | all-gather | bytes 786432 | tf_op jit(solution)/shard_map/all_gather | solution.py:387
  117.6 7.7 %shard_map.78 = (f32[14,32,640]{2,1,0:T(8,128)S(1)}, f32[8,128]{1,0:T(8,128)S(1)}) custom-call(s32[3]{0:T(128)S(1)} %pad_add_fusion.3.flags_ref, f32[2,32,2,8,128]{4,3,2,1,0:T(8,128)S(1)} %bitcast.35, s32[6,8,128]{2,1,0:T(8,128)S(1)} %get-tuple-element.29.slot_ref, s32[6,8,128]{2,1,0:T(8,128)S(1)} %get-tuple-element.30.tile_ref, ...), custom_call_target="tpu_custom_call" | custom-call | tf_op jit(solution)/shard_map/pallas_call | solution.py:342
  125.4 0.9 collective-permute-start.11
  126.2 0.0 collective-permute-start.10
  126.2 2.9 %collective-permute-done.11 = f32[8,128]{1,0:T(8,128)S(1)} collective-permute-done((f32[8,128]{1,0:T(8,128)S(1)}, f32[8,128]{1,0:T(8,128)S(1)}, u32[]{:S(2)}, u32[]{:S(2)}) %collective-permute-start.11) | collective-permute-done | bytes 4128 | tf_op jit(solution)/shard_map/ppermute | solution.py:367
  129.1 0.0 collective-permute-done.10
  129.1 13.4 %all_to_all.22 = f32[32,2,8,128]{3,2,1,0:T(8,128)S(1)} all-to-all(f32[32,2,8,128]{3,2,1,0:T(8,128)S(1)} %broadcast_in_dim.14), channel_id=1, replica_groups=mesh['panel'=2,'z'=8,'core'=2,'y'=4,'xh'=2] {'z','y'}, dimensions={0} | all-to-all | bytes 524288 | tf_op jit(solution)/shard_map/all_to_all | solution.py:386
  142.5 5.6 %all-gather.3 = f32[64,2,8,128]{3,2,1,0:T(8,128)S(1)} all-gather(f32[32,2,8,128]{3,2,1,0:T(8,128)S(1)} %all_to_all.22), channel_id=5, replica_groups=mesh['panel'=2,'z'=8,'core'=2,'y'=4,'xh'=2] {'core'}, dimensions={0}, use_global_device_ids=true | all-gather | bytes 786432 | tf_op jit(solution)/shard_map/all_gather | solution.py:387
  148.1 7.2 %shard_map.79 = f32[14,24,576]{2,1,0:T(8,128)} custom-call(s32[3]{0:T(128)S(1)} %pad_add_fusion.3.flags_ref, f32[2,32,2,8,128]{4,3,2,1,0:T(8,128)S(1)} %bitcast.34, s32[6,8,128]{2,1,0:T(8,128)S(1)} %get-tuple-element.29.slot_ref, s32[6,8,128]{2,1,0:T(8,128)S(1)} %get-tuple-element.30.tile_ref, f32[6,8,128]{2,1,0:T(8,128)S(1)} %get-tuple-element.31.cos_ref, ...), custom_call_target="tpu_custom_call" | custom-call | tf_op jit(solution)/shard_map/pallas_call | solution.py:342
  (14 shorter events, 0.2 us)
Async XLA Ops:
  0.0 3.5 %copy-start = (f32[2,2,576]{2,1,0:T(2,128)S(1)}, f32[2,2,576]{2,1,0:T(2,128)}, u32[]{:S(2)}) copy-start(f32[2,2,576]{2,1,0:T(2,128)} %param.12) | copy-start | bytes 27652
  3.7 1.2 copy-start.1
  4.8 29.3 %copy-start.2 = (f32[1,7,2,24,576]{4,3,2,1,0:T(8,128)S(1)}, f32[1,7,2,24,576]{4,3,2,1,0:T(8,128)}, u32[]{:S(2)}) copy-start(f32[1,7,2,24,576]{4,3,2,1,0:T(8,128)} %param.7) | copy-start | bytes 2322436
  6.0 4.4 %collective-permute-start.1 = (f32[8,128]{1,0:T(8,128)S(1)}, f32[8,128]{1,0:T(8,128)S(1)}, u32[]{:S(2)}, u32[]{:S(2)}) collective-permute-start(f32[8,128]{1,0:T(8,128)S(1)} %get-tuple-element.24), channel_id=1, source_target_pairs={{0,129},{1,128},{128,1},{129,0},{2,131},{3,130},{130,3},{131,2},{4... | collective-permute-start | bytes 12296 | tf_op jit(solution)/shard_map/ppermute | solution.py:367
  9.4 2.5 %collective-permute-start = (f32[8,128]{1,0:T(8,128)S(1)}, f32[8,128]{1,0:T(8,128)S(1)}, u32[]{:S(2)}, u32[]{:S(2)}) collective-permute-start(f32[8,128]{1,0:T(8,128)S(1)} %get-tuple-element.24), channel_id=1, source_target_pairs={{0,128},{1,129},{128,0},{129,1},{2,130},{3,131},{130,2},{131,3},{4... | collective-permute-start | bytes 12296 | tf_op jit(solution)/shard_map/ppermute | solution.py:367
  12.6 30.2 %all-to-all-start = ((f32[32,2,8,128]{3,2,1,0:T(8,128)}), f32[32,2,8,128]{3,2,1,0:T(8,128)S(1)}, u32[]{:S(2)}, u32[]{:S(2)}) async-start(f32[32,2,8,128]{3,2,1,0:T(8,128)} %broadcast_in_dim.11), calls=%async_computation | async-start | bytes 524288 | tf_op jit(solution)/shard_map/all_to_all | solution.py:386
  23.9 10.2 %collective-permute-start.2 = (f32[8,8,640]{2,1,0:T(8,128)S(1)}, f32[8,8,640]{2,1,0:T(8,128)S(1)}, u32[]{:S(2)}, u32[]{:S(2)}) collective-permute-start(f32[8,8,640]{2,1,0:T(8,128)S(1)} %get-tuple-element.25), channel_id=1, source_target_pairs={{8,0},{16,8},{24,16},{32,24},{40,32},{48,40},{56,48},{64,56},{72,6... | collective-permute-start | bytes 491528 | tf_op jit(solution)/shard_map/ppermute | solution.py:367
  28.1 6.0 %collective-permute-start.3 = (f32[8,8,640]{2,1,0:T(8,128)S(1)}, f32[8,8,640]{2,1,0:T(8,128)S(1)}, u32[]{:S(2)}, u32[]{:S(2)}) collective-permute-start(f32[8,8,640]{2,1,0:T(8,128)S(1)} %get-tuple-element.26), channel_id=1, source_target_pairs={{0,8},{8,16},{16,24},{24,32},{32,40},{40,48},{48,56},{56,64},{64,7... | collective-permute-start | bytes 491528 | tf_op jit(solution)/shard_map/ppermute | solution.py:367
  34.3 6.9 %collective-permute-start.4 = (f32[32,128]{1,0:T(8,128)S(1)}, f32[32,128]{1,0:T(8,128)S(1)}, u32[]{:S(2)}, u32[]{:S(2)}) collective-permute-start(f32[32,128]{1,0:T(8,128)S(1)} %get-tuple-element.27), channel_id=1, source_target_pairs={{1,0},{2,1},{3,2},{4,3},{5,4},{6,5},{7,6},{9,8},{10,9},{11,10},{12... | collective-permute-start | bytes 49160 | tf_op jit(solution)/shard_map/ppermute | solution.py:367
  35.6 6.4 %collective-permute-start.5 = (f32[32,128]{1,0:T(8,128)S(1)}, f32[32,128]{1,0:T(8,128)S(1)}, u32[]{:S(2)}, u32[]{:S(2)}) collective-permute-start(f32[32,128]{1,0:T(8,128)S(1)} %get-tuple-element.28), channel_id=1, source_target_pairs={{0,1},{1,2},{2,3},{3,4},{4,5},{5,6},{6,7},{8,9},{9,10},{10,11},{11... | collective-permute-start | bytes 49160 | tf_op jit(solution)/shard_map/ppermute | solution.py:367
  52.7 3.7 %collective-permute-start.7 = (f32[8,128]{1,0:T(8,128)S(1)}, f32[8,128]{1,0:T(8,128)S(1)}, u32[]{:S(2)}, u32[]{:S(2)}) collective-permute-start(f32[8,128]{1,0:T(8,128)S(1)} %get-tuple-element.37), channel_id=1, source_target_pairs={{0,129},{1,128},{128,1},{129,0},{2,131},{3,130},{130,3},{131,2},{4... | collective-permute-start | bytes 12296 | tf_op jit(solution)/shard_map/ppermute | solution.py:367
  55.2 2.5 %collective-permute-start.6 = (f32[8,128]{1,0:T(8,128)S(1)}, f32[8,128]{1,0:T(8,128)S(1)}, u32[]{:S(2)}, u32[]{:S(2)}) collective-permute-start(f32[8,128]{1,0:T(8,128)S(1)} %get-tuple-element.37), channel_id=1, source_target_pairs={{0,128},{1,129},{128,0},{129,1},{2,130},{3,131},{130,2},{131,3},{4... | collective-permute-start | bytes 12296 | tf_op jit(solution)/shard_map/ppermute | solution.py:367
  94.1 3.7 %collective-permute-start.9 = (f32[8,128]{1,0:T(8,128)S(1)}, f32[8,128]{1,0:T(8,128)S(1)}, u32[]{:S(2)}, u32[]{:S(2)}) collective-permute-start(f32[8,128]{1,0:T(8,128)S(1)} %get-tuple-element.39), channel_id=1, source_target_pairs={{0,129},{1,128},{128,1},{129,0},{2,131},{3,130},{130,3},{131,2},{4... | collective-permute-start | bytes 12296 | tf_op jit(solution)/shard_map/ppermute | solution.py:367
  95.8 2.8 %collective-permute-start.8 = (f32[8,128]{1,0:T(8,128)S(1)}, f32[8,128]{1,0:T(8,128)S(1)}, u32[]{:S(2)}, u32[]{:S(2)}) collective-permute-start(f32[8,128]{1,0:T(8,128)S(1)} %get-tuple-element.39), channel_id=1, source_target_pairs={{0,128},{1,129},{128,0},{129,1},{2,130},{3,131},{130,2},{131,3},{4... | collective-permute-start | bytes 12296 | tf_op jit(solution)/shard_map/ppermute | solution.py:367
  125.4 3.7 %collective-permute-start.11 = (f32[8,128]{1,0:T(8,128)S(1)}, f32[8,128]{1,0:T(8,128)S(1)}, u32[]{:S(2)}, u32[]{:S(2)}) collective-permute-start(f32[8,128]{1,0:T(8,128)S(1)} %get-tuple-element.41), channel_id=1, source_target_pairs={{0,129},{1,128},{128,1},{129,0},{2,131},{3,130},{130,3},{131,2},{4... | collective-permute-start | bytes 12296 | tf_op jit(solution)/shard_map/ppermute | solution.py:367
  126.2 2.9 %collective-permute-start.10 = (f32[8,128]{1,0:T(8,128)S(1)}, f32[8,128]{1,0:T(8,128)S(1)}, u32[]{:S(2)}, u32[]{:S(2)}) collective-permute-start(f32[8,128]{1,0:T(8,128)S(1)} %get-tuple-element.41), channel_id=1, source_target_pairs={{0,128},{1,129},{128,0},{129,1},{2,130},{3,131},{130,2},{131,3},{4... | collective-permute-start | bytes 12296 | tf_op jit(solution)/shard_map/ppermute | solution.py:367

commit v2 on v1

v2 whole, which is shorter than its diff:
```python
import functools
import math

import jax
import jax.numpy as jnp
from jax import lax
from jax.experimental import pallas as pl
from jax.experimental.pallas import tpu as pltpu
from jax.sharding import Mesh, PartitionSpec as P

time_step = 0.25
viscosity = 0.1
resistivity = 0.08
conduction = 0.12
buoyancy = 0.5
gradient = 0.5

AXES = ("panel", "z", "core", "y", "xh")
SIZES = dict(zip(AXES, (2, 8, 2, 4, 2)))
LAT = ("z", "core")
LON = ("y", "xh")

FIELDS = 14
CT = 24
CP = 576
ROWS = 32
COLS = 640
HALO = 4
SLOTS = 48
NT = 384
LANES = 128
TILES = 128
LANE_TILES = COLS // LANES
LAST = COLS - LANES
VMEM_LIMIT = 24 * 1024 * 1024


def lane_of(shape):
    return lax.broadcasted_iota(jnp.int32, shape, len(shape) - 1)


def row_of(shape):
    return lax.broadcasted_iota(jnp.int32, shape, len(shape) - 2)


def lane_gather(block, index):
    return jnp.take_along_axis(block, index, axis=1, mode="promise_in_bounds")


def build_packet(block_of, index_ref, weight_ref):
    totals = [None] * FIELDS
    for t in range(LANE_TILES):
        index = index_ref[t]
        for rb in range(CT // 8):
            weight = weight_ref[rb * LANE_TILES + t]
            for f in range(FIELDS):
                term = weight * lane_gather(block_of(f, rb, t), index)
                totals[f] = term if totals[f] is None else totals[f] + term
    rows = [jnp.sum(total, axis=0, keepdims=True) for total in totals]
    rows += [jnp.zeros((1, LANES), jnp.float32)] * (16 - FIELDS)
    packet = jnp.concatenate(rows, axis=0)
    return packet + pltpu.roll(packet, 64, 1)


def state_block(state_ref, f, rb, t):
    rows = slice(rb * 8, rb * 8 + 8)
    if t < LANE_TILES - 1:
        return state_ref[f, rows, t * LANES : (t + 1) * LANES]
    half = state_ref[f, rows, LAST:CP]
    return jnp.concatenate([half, jnp.zeros((8, LANES - 64), jnp.float32)], axis=1)


def place_of(aux_ref):
    return aux_ref[7, 0].astype(jnp.int32), aux_ref[7, LANES].astype(jnp.int32)


def open_kernel(
    flags_ref, state_hbm, cell_hbm, frac_hbm, ns_source_hbm, we_source_hbm, ns_turn_hbm, we_turn_hbm,
    state_ref, aux_ref, packet_ref, inner_ref, cross_ref, index_ref, weight_ref,
    cell_ref, frac_ref, ns_source_ref, we_source_ref, ns_turn_ref, we_turn_ref, semaphores,
):
    sources = (cell_hbm, frac_hbm, ns_source_hbm, we_source_hbm, ns_turn_hbm, we_turn_hbm, state_hbm)
    targets = (cell_ref, frac_ref, ns_source_ref, we_source_ref, ns_turn_ref, we_turn_ref, state_ref)
    copies = [pltpu.make_async_copy(sources[i], targets[i], semaphores.at[i]) for i in range(len(sources))]
    for copy in copies:
        copy.start()
    for copy in copies[:-1]:
        copy.wait()
    panel = flags_ref[2, 0]
    far_south = flags_ref[0, 0] == NT // CT - 1
    far_east = flags_ref[1, 0] == 7
    aux_ref[...] = jnp.zeros((8, COLS), jnp.float32)
    for i, (table, far) in enumerate(
        ((ns_source_ref, far_south), (ns_turn_ref, far_south), (we_source_ref, far_east), (we_turn_ref, far_east))
    ):
        both = table[panel].astype(jnp.float32)
        aux_ref[i : i + 1, 0 : both.shape[1]] = jnp.where(far, both[1:2, :], both[0:1, :])
    aux_ref[7:8, 0:LANES] = flags_ref[0:1, :].astype(jnp.float32)
    aux_ref[7:8, LANES : 2 * LANES] = flags_ref[1:2, :].astype(jnp.float32)
    shape = (8, LANES)
    lane = lane_of(shape)
    row = row_of(shape)
    copies[-1].wait()
    first_core = (flags_ref[0, 0] & 1) == 0
    for c in range(7):
        for t in range(LANE_TILES):
            cols = slice(t * LANES, (t + 1) * LANES)
            top = [state_block(state_ref, 2 * c + k, 0, t) for k in range(2)]
            end = [state_block(state_ref, 2 * c + k, CT // 8 - 1, t) for k in range(2)]
            north = jnp.where(row < HALO, top[0], pltpu.roll(top[1], HALO, 0))
            south = jnp.where(row < HALO, pltpu.roll(end[0], HALO, 0), end[1])
            inner_ref[c, :, cols] = jnp.where(first_core, south, north)
            cross_ref[c, :, cols] = jnp.where(first_core, north, south)

    def doubled(line):
        line = jnp.concatenate([line, jnp.zeros((1, LANES - SLOTS), jnp.float32)], axis=1)
        line = jnp.broadcast_to(line, shape)
        return jnp.where(lane < 64, line, pltpu.roll(line, 64, 1))

    cell = doubled(cell_ref[...].astype(jnp.float32))
    frac_u = doubled(frac_ref[0:1, :])
    frac_v = doubled(frac_ref[1:2, :])
    lat_off = jnp.floor((cell + 0.5) * (1.0 / (CP - 1)))
    lon_off = cell - lat_off * (CP - 1)
    lat_off = lat_off.astype(jnp.int32)
    second = lane >= 64
    column = lon_off.astype(jnp.int32) + second.astype(jnp.int32)
    used = (lane & 63) < SLOTS
    along = jnp.where(second, frac_v, 1.0 - frac_v)
    for t in range(LANE_TILES):
        local = column - t * LANES
        inside = used & (local >= 0) & (local < LANES)
        index_ref[t] = jnp.where(inside, local, 0)
        for rb in range(CT // 8):
            here = row + rb * 8
            down = jnp.where(here == lat_off, 1.0 - frac_u, jnp.where(here == lat_off + 1, frac_u, 0.0))
            weight_ref[rb * LANE_TILES + t] = jnp.where(inside, down * along, 0.0)
    packet_ref[...] = build_packet(functools.partial(state_block, state_ref), index_ref, weight_ref)

    inner_ref[7] = aux_ref[...]
    cross_ref[7] = aux_ref[...]


def ordered(flag, inner, cross):
    first = (flag & 1) == 0
    return jnp.where(first, inner, cross), jnp.where(first, cross, inner)


def outer_rows(from_south, from_north, k, row):
    if k == 0:
        return jnp.where(row < HALO, from_south, pltpu.roll(from_north, HALO, 0))
    return jnp.where(row < HALO, pltpu.roll(from_south, HALO, 0), from_north)


def side_kernel(aux_ref, state_ref, lat_inner_ref, lat_cross_ref, inner_ref, cross_ref):
    shape = (8, LANES)
    lat, lon = place_of(aux_ref)
    lane = lane_of(shape)
    row = row_of(shape)
    for rb in range(ROWS // 8):
        west = jnp.zeros(shape, jnp.float32)
        east = jnp.zeros(shape, jnp.float32)
        for f in range(FIELDS):
            c, k = f // 2, f % 2
            if rb < CT // 8:
                first = state_block(state_ref, f, rb, 0)
                last = state_block(state_ref, f, rb, LANE_TILES - 1)
            else:
                first = outer_rows(*ordered(lat, lat_inner_ref[c, :, 0:LANES], lat_cross_ref[c, :, 0:LANES]), k, row)
                last = outer_rows(*ordered(lat, lat_inner_ref[c, :, LAST:COLS], lat_cross_ref[c, :, LAST:COLS]), k, row)
            here = (lane >= 8 * f) & (lane < 8 * f + HALO)
            west = jnp.where(here, pltpu.roll(first, 8 * f, 1) if f else first, west)
            east = jnp.where(here, pltpu.roll(last, (8 * f - 60) % LANES, 1), east)
        if rb == 0:
            here = (lane >= 112) & (lane < 112 + HALO)
            west = jnp.where(here, pltpu.roll(aux_ref[:, 0:LANES], 112, 1), west)
            east = jnp.where(here, pltpu.roll(aux_ref[:, LAST:COLS], 112 - 60, 1), east)
        inner, cross = ordered(lon, east, west)
        inner_ref[rb * 8 : rb * 8 + 8, :] = inner
        cross_ref[rb * 8 : rb * 8 + 8, :] = cross


def with_columns(block, from_east, from_west, f, lane):
    block = jnp.where((lane >= 64) & (lane < 64 + HALO), pltpu.roll(from_east, (64 - 8 * f) % LANES, 1), block)
    return jnp.where(lane >= LANES - HALO, pltpu.roll(from_west, (124 - 8 * f) % LANES, 1), block)


def frame_kernel(
    aux_ref, state_ref, lat_inner_ref, lat_cross_ref, lon_inner_ref, lon_cross_ref,
    full_ref, slot_ref, tile_ref, cos_ref, sin_ref, metric_ref,
):
    shape = (8, LANES)
    lat, lon = place_of(aux_ref)
    lane = lane_of(shape)
    row = row_of(shape)
    for rb in range(ROWS // 8):
        rows = slice(rb * 8, rb * 8 + 8)
        east, west = ordered(lon, lon_inner_ref[rows, :], lon_cross_ref[rows, :])
        for f in range(FIELDS):
            c, k = f // 2, f % 2
            for t in range(LANE_TILES):
                cols = slice(t * LANES, (t + 1) * LANES)
                if rb < CT // 8:
                    block = state_block(state_ref, f, rb, t)
                else:
                    south, north = ordered(lat, lat_inner_ref[c, :, cols], lat_cross_ref[c, :, cols])
                    block = outer_rows(south, north, k, row)
                if t == LANE_TILES - 1:
                    block = with_columns(block, east, west, f, lane)
                full_ref[f, rows, cols] = block
    for t in range(LANE_TILES + 1):
        if t < LANE_TILES:
            block = aux_ref[:, t * LANES : (t + 1) * LANES]
            if t == LANE_TILES - 1:
                east, west = ordered(lon, lon_inner_ref[0:8, :], lon_cross_ref[0:8, :])
                block = jnp.where((lane >= 64) & (lane < 64 + HALO), pltpu.roll(east, (64 - 112) % LANES, 1), block)
                block = jnp.where(lane >= LANES - HALO, pltpu.roll(west, 124 - 112, 1), block)
            source = jnp.broadcast_to(block[0:1, :], shape)
            angle = jnp.broadcast_to(block[1:2, :], shape)
        else:
            block = aux_ref[:, 0:LANES]
            south, north = ordered(lat, lat_inner_ref[7, :, 0:LANES], lat_cross_ref[7, :, 0:LANES])
            block = jnp.where((lane >= CT) & (lane < CT + HALO), pltpu.roll(south, CT, 1), block)
            block = jnp.where((lane >= 28) & (lane < 32), pltpu.roll(north, 8, 1), block)
            source = jnp.broadcast_to(block[2:3, :], shape)
            angle = jnp.broadcast_to(block[3:4, :], shape)
        whole = jnp.floor((source + 0.5) * (1.0 / SLOTS))
        tile = whole.astype(jnp.int32)
        slot_ref[t] = (source - whole * SLOTS).astype(jnp.int32) + 64 * (tile & 1)
        tile_ref[t] = tile // 2
        cos_ref[t] = jnp.cos(angle)
        sin_ref[t] = jnp.sin(angle)
    line = row_of((ROWS, LANES))
    line = jnp.where(line >= ROWS - HALO, line - ROWS, line) + lat * CT
    theta = math.pi / 4 + (line.astype(jnp.float32) + 0.5) * ((math.pi / 2) / NT)
    metric_ref[...] = 1.0 / jnp.sin(theta)


def pick_ghosts(donor_ref, slot_ref, tile_ref, cos_ref, sin_ref):
    shape = (8, LANES)
    row = row_of(shape)
    count = LANE_TILES + 1
    low, high = [], []
    for t in range(count):
        slots, pairs = slot_ref[t], tile_ref[t]
        for half, out in ((0, low), (1, high)):
            total = jnp.zeros(shape, jnp.float32)
            for v in range(TILES // 2):
                z, core, y = v // 8, v // 4 % 2, v % 4
                block = donor_ref[core, z * 4 + y, half * 8 : half * 8 + 8, :]
                total = jnp.where(pairs == v, lane_gather(block, slots), total)
            out.append(total)
    ghosts = []
    for t in range(count):
        cosine, sine = cos_ref[t], sin_ref[t]
        first = (row == 2) | (row == 3)
        other = (row == 4) | (row == 5)
        mate = jnp.where(first, pltpu.roll(low[t], 6, 0), pltpu.roll(low[t], 2, 0))
        turn = jnp.where(first, -sine, sine)
        a = jnp.where(first | other, cosine * low[t] + turn * mate, low[t])
        first = row < 2
        mate = jnp.where(first, pltpu.roll(high[t], 6, 0), pltpu.roll(high[t], 2, 0))
        turn = jnp.where(first, -sine, sine)
        b = jnp.where(row < 4, cosine * high[t] + turn * mate, high[t])
        ghosts.append((a, b))
    return ghosts


def keep_ghosts(lon, ghosts, line_ref, column_ref):
    for t in range(LANE_TILES):
        cols = slice(t * LANES, (t + 1) * LANES)
        line_ref[0:8, cols], line_ref[8:16, cols] = ghosts[t]

    def put_column():
        shape = (ROWS, LANES)
        diagonal = lane_of(shape) == row_of(shape)
        for f in range(FIELDS):
            values = jnp.broadcast_to(ghosts[LANE_TILES][f // 8][f % 8 : f % 8 + 1, :], shape)
            column = jnp.sum(jnp.where(diagonal, values, 0.0), axis=1, keepdims=True)
            column_ref[f] = jnp.broadcast_to(column, shape)

    pl.when((lon == 0) | (lon == 7))(put_column)


def tendency(work_ref, metric_ref, rb, k, emit, tile=None, ghosts=None):
    low = rb * 8
    rows = slice(low, low + 8)
    whole = tile is None
    cols = slice(0, COLS) if whole else slice(tile * LANES, (tile + 1) * LANES)
    shape = (8, cols.stop - cols.start)
    row = row_of(shape)
    lane = lane_of(shape)
    metric = metric_ref[rows, :]
    if whole:
        metric = jnp.concatenate([metric] * LANE_TILES, axis=1)
    square = metric * metric
    centre_weight = 4.0 + 2.0 * square
    radial = 0.5 if k == 0 else -0.5

    def value(c):
        return work_ref[2 * c + k, rows, cols]

    def beside(f, step):
        start = (tile + step) % LANE_TILES * LANES
        return work_ref[f, rows, start : start + LANES]

    def coefficients(c):
        return radial * value(c), 0.5 * value(c + 1), (0.5 * metric) * value(c + 2)

    flow_by = coefficients(0)
    field_by = coefficients(3)

    def parts(c):
        f = 2 * c + k
        centre = value(c)
        across = work_ref[2 * c + 1 - k, rows, cols]
        before = work_ref[f, (low - 1) % ROWS : (low - 1) % ROWS + 1, cols]
        after = work_ref[f, (low + 8) % ROWS : (low + 8) % ROWS + 1, cols]
        if ghosts is not None:
            (lat, lon), line_ref, column_ref = ghosts
            if rb == 0:
                before = jnp.where(lat == 0, line_ref[f : f + 1, cols], before)
            if rb == CT // 8 - 1:
                after = jnp.where(lat == NT // CT - 1, line_ref[f : f + 1, cols], after)
        north = jnp.where(row == 0, jnp.broadcast_to(before, shape), pltpu.roll(centre, 1, 0))
        south = jnp.where(row == 7, jnp.broadcast_to(after, shape), pltpu.roll(centre, 7, 0))
        west = pltpu.roll(centre, 1, 1)
        east = pltpu.roll(centre, shape[1] - 1, 1)
        if tile == 0:
            west = jnp.where(lane == 0, jnp.where(lon == 0, column_ref[f, rows, :], pltpu.roll(beside(f, -1), 1, 1)), west)
            east = jnp.where(lane == LANES - 1, pltpu.roll(beside(f, 1), LANES - 1, 1), east)
        elif tile is not None:
            west = jnp.where(lane == 0, pltpu.roll(beside(f, -1), 1, 1), west)
            east = jnp.where(lane == LANES - 1, pltpu.roll(beside(f, 1), LANES - 1, 1), east)
            east = jnp.where((lane == CP - LAST - 1) & (lon == 7), column_ref[f, rows, :], east)
        grad_t = south - north
        grad_p = east - west
        laplace = across + (south + north) + square * (east + west) - centre_weight * centre
        return across, grad_t, grad_p, laplace

    def along(by, p):
        return by[0] * p[0] + by[1] * p[1] + by[2] * p[2]

    for c in range(3):
        p = parts(c)
        u_flow, u_field, u_laplace = along(flow_by, p), along(field_by, p), p[3]
        p = parts(c + 3)
        velocity = along(field_by, p) - u_flow + viscosity * u_laplace
        if c == 0:
            velocity = velocity + buoyancy * value(6)
        emit(c, velocity)
        emit(c + 3, u_field - along(flow_by, p) + resistivity * p[3])
    p = parts(6)
    emit(6, conduction * p[3] - along(flow_by, p) + gradient * value(0))


def inner_kernel(factor, metric_ref, *refs):
    full_ref, now_ref, next_ref = refs if len(refs) == 3 else (refs[0], refs[0], refs[1])
    for rb in range(ROWS // 8):
        rows = slice(rb * 8, rb * 8 + 8)
        for k in range(2):

            def emit(c, value):
                next_ref[2 * c + k, rows, :] = full_ref[2 * c + k, rows, :] + factor * value

            tendency(now_ref, metric_ref, rb, k, emit)


def redo_rim(place, now_ref, metric_ref, line_ref, column_ref, blocks, store):
    lat, lon = place

    def redo(rbs, tile):
        cols = slice(0, COLS) if tile is None else slice(tile * LANES, (tile + 1) * LANES)
        for rb in rbs:
            for k in range(2):

                def emit(c, value):
                    store(2 * c + k, slice(rb * 8, rb * 8 + 8), cols, value)

                tendency(now_ref, metric_ref, rb, k, emit, tile, (place, line_ref, column_ref))

    pl.when(lat == 0)(lambda: redo([0], None))
    pl.when(lat == NT // CT - 1)(lambda: redo([CT // 8 - 1], None))
    pl.when(lon == 0)(lambda: redo(range(blocks), 0))
    pl.when(lon == 7)(lambda: redo(range(blocks), LANE_TILES - 1))


def rim_kernel(
    factor, aux_ref, donor_ref, slot_ref, tile_ref, cos_ref, sin_ref, metric_ref, index_ref, weight_ref, *refs
):
    full_ref, now_ref, inner_ref, next_ref, packet_ref, line_ref, column_ref = refs if len(refs) == 7 else refs[:1] + refs
    place = place_of(aux_ref)
    keep_ghosts(place[1], pick_ghosts(donor_ref, slot_ref, tile_ref, cos_ref, sin_ref), line_ref, column_ref)
    next_ref[...] = inner_ref[...]

    def store(f, rows, cols, value):
        next_ref[f, rows, cols] = full_ref[f, rows, cols] + factor * value

    redo_rim(place, now_ref, metric_ref, line_ref, column_ref, ROWS // 8, store)

    def block_of(f, rb, t):
        return next_ref[f, rb * 8 : rb * 8 + 8, t * LANES : (t + 1) * LANES]

    packet_ref[...] = build_packet(block_of, index_ref, weight_ref)


def last_inner_kernel(metric_ref, full_ref, second_ref, third_ref, fourth_ref, base_ref, out_ref):
    for rb in range(CT // 8):
        rows = slice(rb * 8, rb * 8 + 8)
        for k in range(2):

            def emit(c, value):
                f = 2 * c + k
                base = second_ref[f, rows, :] + 2.0 * third_ref[f, rows, :] + fourth_ref[f, rows, :] - full_ref[f, rows, :]
                base = (1.0 / 3.0) * base
                base_ref[f, rows, :] = base
                out_ref[f, rows, :] = base + (time_step / 6) * value

            tendency(fourth_ref, metric_ref, rb, k, emit)


def last_rim_kernel(
    aux_ref, donor_ref, slot_ref, tile_ref, cos_ref, sin_ref, metric_ref, base_ref, inner_ref, now_ref,
    out_ref, line_ref, column_ref,
):
    place = place_of(aux_ref)
    keep_ghosts(place[1], pick_ghosts(donor_ref, slot_ref, tile_ref, cos_ref, sin_ref), line_ref, column_ref)
    for f in range(FIELDS):
        out_ref[f] = inner_ref[f, :, 0:CP]

    def store(f, rows, cols, value):
        cols = slice(cols.start, min(cols.stop, CP))
        out = base_ref[f, rows, cols] + (time_step / 6) * value[:, : cols.stop - cols.start]
        out_ref[f, rows, cols] = out

    redo_rim(place, now_ref, metric_ref, line_ref, column_ref, CT // 8, store)


def call(kernel, ins, outs, scratch=(), cost=0, left=()):
    vmem = pl.BlockSpec(memory_space=pltpu.VMEM)
    hbm = pl.BlockSpec(memory_space=pltpu.HBM)
    shapes = tuple(jax.ShapeDtypeStruct(s, d) for s, d in outs)
    ins = [pltpu.with_memory_space_constraint(a, pltpu.HBM) if i in left else a for i, a in enumerate(ins)]
    return pl.pallas_call(
        kernel,
        out_shape=shapes,
        in_specs=[hbm if i in left else vmem for i in range(len(ins))],
        out_specs=(vmem,) * len(outs),
        scratch_shapes=list(scratch),
        compiler_params=pltpu.CompilerParams(vmem_limit_bytes=VMEM_LIMIT),
        cost_estimate=pl.CostEstimate(flops=cost * 1000, bytes_accessed=cost, transcendentals=0) if cost else None,
    )(*ins)


def coordinates(axes):
    points = [()]
    for a in axes:
        points = [q + (i,) for q in points for i in range(SIZES[a])]
    return points


def permute(value, axes, move):
    points = coordinates(axes)
    place = {q: i for i, q in enumerate(points)}
    pairs = []
    for q in points:
        to = move(q)
        if to is not None:
            pairs.append((place[q], place[to]))
    return lax.ppermute(value, axes if len(axes) > 1 else axes[0], pairs)


def within(value, axes):
    return permute(value, axes, lambda q: (q[0], 1 - q[1]))


def between(value, axes):
    count = SIZES[axes[0]]
    return permute(value, axes, lambda q: ((q[0] + 1) % count, 0) if q[1] == 1 else ((q[0] - 1) % count, 1))


def swap_packets(packet):
    same = permute(packet, ("panel", "xh"), lambda q: (1 - q[0], q[1]))
    other = permute(packet, ("panel", "xh"), lambda q: (1 - q[0], 1 - q[1]))
    second = lane_of(packet.shape) >= 64
    return jnp.where(second == (lax.axis_index("xh") == 1), same, other)


def spread_packets(pair, inner):
    if inner is not None:
        pair, _ = lax.optimization_barrier((pair, inner))
    count = SIZES["z"] * SIZES["y"]
    spread = lax.all_to_all(jnp.broadcast_to(pair[None], (count,) + pair.shape), ("z", "y"), 0, 0)
    return lax.all_gather(spread, "core")


def on_device(state, pack_cell, pack_frac, ns_source, we_source, ns_turn, we_turn):
    f32 = jnp.float32
    tile = state.reshape(FIELDS, CT, CP)
    lat = lax.axis_index(LAT)
    lon = lax.axis_index(LON)
    panel = lax.axis_index("panel")
    flags = jnp.broadcast_to(jnp.stack([lat, lon, panel] + [panel] * 5).astype(jnp.int32)[:, None], (8, LANES))
    raw = [pack_cell.reshape(1, SLOTS), pack_frac.reshape(2, SLOTS), ns_source, we_source, ns_turn, we_turn]
    vreg = (8, LANES)
    packed = ((16, LANES), f32)
    whole = ((FIELDS, ROWS, COLS), f32)
    message = ((8, 8, COLS), f32)
    side = ((ROWS, LANES), f32)
    tile, aux, packet, lat_inner, lat_cross, index, weight = call(
        open_kernel,
        [flags, tile] + raw,
        [
            ((FIELDS, CT, CP), f32),
            ((8, COLS), f32),
            packed,
            message,
            message,
            ((LANE_TILES,) + vreg, jnp.int32),
            ((3 * LANE_TILES,) + vreg, f32),
        ],
        scratch=[pltpu.VMEM(a.shape, a.dtype) for a in raw] + [pltpu.SemaphoreType.DMA((len(raw) + 1,))],
        left=range(1, 8),
    )
    lat_inner = within(lat_inner, LAT)
    lat_cross = between(lat_cross, LAT)
    lon_inner, lon_cross = call(side_kernel, [aux, tile, lat_inner, lat_cross], [side, side])
    pair, _ = lax.optimization_barrier((swap_packets(packet), lon_inner))
    lon_inner = within(lon_inner, LON)
    lon_cross = between(lon_cross, LON)
    points = (LANE_TILES + 1,) + vreg
    full, slot, where, cosine, sine, metric = call(
        frame_kernel,
        [aux, tile, lat_inner, lat_cross, lon_inner, lon_cross],
        [whole, (points, jnp.int32), (points, jnp.int32), (points, f32), (points, f32), ((ROWS, LANES), f32)],
    )
    tables = [slot, where, cosine, sine, metric]
    kept = [pltpu.VMEM((16, COLS), f32), pltpu.VMEM((FIELDS, ROWS, LANES), f32)]
    states = [full]
    for factor in (time_step / 2, time_step / 2, time_step):
        if len(states) > 1:
            pair = swap_packets(packet)
        now = [states[-1]] if len(states) > 1 else []
        (inner,) = call(functools.partial(inner_kernel, factor), [metric, full] + now, [whole], cost=2_000_000 if now else 50_000_000)
        after, packet = call(
            functools.partial(rim_kernel, factor),
            [aux, spread_packets(pair, inner if now else None)] + tables + [index, weight, full] + now + [inner],
            [whole, packed],
                scratch=kept,
        )
        states.append(after)
    pair = swap_packets(packet)
    inner_shape = ((FIELDS, CT, COLS), f32)
    base, inner = call(last_inner_kernel, [metric] + states, [inner_shape, inner_shape], cost=2_000_000)
    (result,) = call(
        last_rim_kernel,
        [aux, spread_packets(pair, inner)] + tables + [base, inner, states[-1]],
        [((FIELDS, CT, CP), f32)],
        scratch=kept,
    )
    return result.reshape(state.shape)


def solution(mesh):
    fine = Mesh(mesh.devices.reshape(tuple(SIZES[a] for a in AXES)), AXES)
    return jax.shard_map(
        on_device,
        mesh=fine,
        in_specs=(
            P("panel", None, None, LAT, LON),
            P("panel", LAT, LON, None),
            P("panel", None, LAT, LON, None),
            P(None, None, LON),
            P(None, None, LAT),
            P(None, None, LON),
            P(None, None, LAT),
        ),
        out_specs=P("panel", None, None, LAT, LON),
        check_vma=False,
    )
```

time: 156 us -> 118 us (0.76)
  Pallas kernels: 32.8 us -> 15.2 us
  starting transfers between devices: 34.4 us -> 22.6 us
  blocking collectives: 68.6 us -> 63.5 us
  local copies, waits for them, and re-layouts: 3.39 us -> 0.94 us
  other arithmetic: 2.29 us -> 0.02 us
    pallas_call x7 -> x11, Pallas kernels: 32.8 us -> 15.2 us  [call(): pl.pallas_call(kernel, out_shape=shapes, in_specs=[hbm if i in left else...]
    ppermute x12, starting transfers between devices: 23 us -> 12.6 us  [permute(): return lax.ppermute(value, axes if len(axes) > 1 else axes[0], pairs)]
    all_to_all x1, waiting for transfers between devices: 0.01 us -> 8.68 us  [spread_packets(): lax.all_to_all(jnp.broadcast_to(pair[None], (count,) + pair.shape), ('z',...]
    all_to_all x3, blocking collectives: 49.7 us -> 41.4 us  [spread_packets(): lax.all_to_all(jnp.broadcast_to(pair[None], (count,) + pair.shape), ('z',...]
    ppermute x12, waiting for transfers between devices: 13.7 us -> 6.49 us  [permute(): return lax.ppermute(value, axes if len(axes) > 1 else axes[0], pairs)]
    all_gather x4, blocking collectives: 18.8 us -> 22.1 us  [spread_packets(): return lax.all_gather(spread, 'core')]
    convert_element_type x3 -> x0, other arithmetic: 2.05 us -> none  [the longest x2 1.38 us: chosen(): lax.dynamic_slice(table, (panel, side, 0), (1, 1, table.shape[2]))[0]]
  transfers between devices with their start and end apart: 13 -> 13, of which waited for: 9 -> 7; matrix products, arithmetic and copies ran while one was open for 0% -> 1% of each run, Pallas kernels for 1% -> 5%
where the time goes in v2:
time: 118 us
  blocking collectives  63.5 us (54%)
  starting transfers between devices  22.6 us (19%)
  Pallas kernels  15.2 us (13%)
  waiting for transfers between devices  15.2 us (13%)
    all_to_all x3, blocking collectives, spread_packets(): lax.all_to_all(jnp.broadcast_to(pair[None], (count,) + pair.shape), ('z',...  41.4 us
    all_gather x4, blocking collectives, spread_packets(): return lax.all_gather(spread, 'core')  22.1 us
    pallas_call x11, Pallas kernels, call(): pl.pallas_call(kernel, out_shape=shapes, in_specs=[hbm if i in left else...  15.2 us
    ppermute x12, starting transfers between devices, permute(): return lax.ppermute(value, axes if len(axes) > 1 else axes[0], pairs)  12.6 us
    all_to_all x1, starting transfers between devices, spread_packets(): lax.all_to_all(jnp.broadcast_to(pair[None], (count,) + pair.shape), ('z',...  9.99 us
    all_to_all x1, waiting for transfers between devices, spread_packets(): lax.all_to_all(jnp.broadcast_to(pair[None], (count,) + pair.shape), ('z',...  8.68 us
    ppermute x12, waiting for transfers between devices, permute(): return lax.ppermute(value, axes if len(axes) > 1 else axes[0], pairs)  6.49 us
  transfers between devices with their start and end apart: 13, of which 7 were waited for; matrix products, arithmetic and copies ran while one was open for 1% of the time, Pallas kernels for 5%

profile of v2, /device:TPU:1, one launch (start us, length us, event | category | flops | bytes accessed | tf_op | source)
XLA Modules:
  0.0 117.6 jit_solution(18174323314557230166)
XLA Ops:
  0.0 0.1 stack.20
  0.1 0.1 broadcast_in_dim.10.flags_ref
  0.2 1.8 %shard_map.73 = (f32[14,24,576]{2,1,0:T(8,128)S(1)}, f32[8,640]{1,0:T(8,128)S(1)}, f32[16,128]{1,0:T(8,128)S(1)}, f32[8,8,640]{2,1,0:T(8,128)S(1)}, f32[8,8,640]...) custom-call(s32[8,128]{1,0:T(8,128)S(1)} %broadcast_in_dim.10.flags_ref, ...), custom_call_target="tpu_custom_call" | custom-call | tf_op jit(solution)/shard_map/pallas_call | solution.py:444
  2.0 3.3 %collective-permute-start.2 = (f32[8,8,640]{2,1,0:T(8,128)S(1)}, f32[8,8,640]{2,1,0:T(8,128)S(1)}, u32[]{:S(2)}, u32[]{:S(2)}) collective-permute-start(f32[8,8,640]{2,1,0:T(8,128)S(1)} %get-tuple-element.35), channel_id=1, source_target_pairs={{0,8},{8,0},{16,24},{24,16},{32,40},{40,32},{48,56},{56,48},{64,72... | collective-permute-start | bytes 491528 | tf_op jit(solution)/shard_map/ppermute | solution.py:470
  5.3 0.0 collective-permute-start.3
  5.3 2.4 %collective-permute-start.1 = (f32[16,128]{1,0:T(8,128)S(1)}, f32[16,128]{1,0:T(8,128)S(1)}, u32[]{:S(2)}, u32[]{:S(2)}) collective-permute-start(f32[16,128]{1,0:T(8,128)S(1)} %get-tuple-element.33), channel_id=1, source_target_pairs={{0,129},{1,128},{128,1},{129,0},{2,131},{3,130},{130,3},{131,2},{4... | collective-permute-start | bytes 24584 | tf_op jit(solution)/shard_map/ppermute | solution.py:470
  7.7 0.0 collective-permute-start
  7.7 0.0 collective-permute-done.2.lat_inner_ref
  7.7 2.4 %collective-permute-done.3.lat_cross_ref = f32[8,8,640]{2,1,0:T(8,128)S(1)} collective-permute-done((f32[8,8,640]{2,1,0:T(8,128)S(1)}, f32[8,8,640]{2,1,0:T(8,128)S(1)}, u32[]{:S(2)}, u32[]{:S(2)}) %collective-permute-start.3) | collective-permute-done | bytes 163872 | tf_op jit(solution)/shard_map/ppermute | solution.py:470
  10.0 0.2 shard_map.74
  10.2 3.5 %collective-permute-start.5 = (f32[32,128]{1,0:T(8,128)S(1)}, f32[32,128]{1,0:T(8,128)S(1)}, u32[]{:S(2)}, u32[]{:S(2)}) collective-permute-start(f32[32,128]{1,0:T(8,128)S(1)} %get-tuple-element.39), channel_id=1, source_target_pairs={{0,7},{1,2},{2,1},{3,4},{4,3},{5,6},{6,5},{7,0},{8,15},{9,10},{10,... | collective-permute-start | bytes 49160 | tf_op jit(solution)/shard_map/ppermute | solution.py:470
  13.8 0.0 collective-permute-start.4
  13.8 0.0 collective-permute-done.1
  13.8 0.0 collective-permute-done
  13.8 0.7 broadcast_in_dim.11
  14.5 10.0 %all-to-all-start = ((f32[32,16,128]{2,1,0:T(8,128)}), f32[32,16,128]{2,1,0:T(8,128)S(1)}, u32[]{:S(2)}, u32[]{:S(2)}) async-start(f32[32,16,128]{2,1,0:T(8,128)} %broadcast_in_dim.11), calls=%async_computation | async-start | bytes 524288 | tf_op jit(solution)/shard_map/all_to_all | solution.py:493
  24.5 0.0 collective-permute-done.5.lon_cross_ref
  24.5 0.0 collective-permute-done.4.lon_inner_ref
  24.5 0.3 shard_map.75
  24.8 1.4 %shard_map.76.refs_1_ = f32[14,32,640]{2,1,0:T(8,128)S(1)} custom-call(f32[32,128]{1,0:T(8,128)S(1)} %get-tuple-element.44.metric_ref, f32[14,32,640]{2,1,0:T(8,128)S(1)} %get-tuple-element.47.refs_0_.full_ref), custom_call_target="tpu_custom_call" | custom-call | flops 49999998976 | bytes 50000000 | tf_op jit(solution)/shard_map/pallas_call | solution.py:444
  26.2 8.7 %all-to-all-done = f32[32,16,128]{2,1,0:T(8,128)S(1)} async-done(((f32[32,16,128]{2,1,0:T(8,128)}), f32[32,16,128]{2,1,0:T(8,128)S(1)}, u32[]{:S(2)}, u32[]{:S(2)}) %all-to-all-start) | async-done | bytes 262176 | tf_op jit(solution)/shard_map/all_to_all | solution.py:493
  34.9 5.6 %all-gather = f32[64,16,128]{2,1,0:T(8,128)S(1)} all-gather(f32[32,16,128]{2,1,0:T(8,128)S(1)} %all-to-all-done), channel_id=2, replica_groups=mesh['panel'=2,'z'=8,'core'=2,'y'=4,'xh'=2] {'core'}, dimensions={0}, use_global_device_ids=true | all-gather | bytes 786432 | tf_op jit(solution)/shard_map/all_gather | solution.py:494
  40.5 1.8 %shard_map.77 = (f32[14,32,640]{2,1,0:T(8,128)S(1)}, f32[16,128]{1,0:T(8,128)S(1)}) custom-call(f32[8,640]{1,0:T(8,128)S(1)} %get-tuple-element.32.aux_ref, f32[2,32,16,128]{3,2,1,0:T(8,128)S(1)} %bitcast.14, s32[6,8,128]{2,1,0:T(8,128)S(1)} %get-tuple-element.40.slot_ref, s32[6,8,128]{2,1,0:T(8,128)S(1)} %get-tuple-element.41.tile_ref, ...), custom_call_target="tpu_custom_call" | custom-call | tf_op jit(solution)/shard_map/pallas_call | solution.py:444
  42.2 1.4 %collective-permute-start.7 = (f32[16,128]{1,0:T(8,128)S(1)}, f32[16,128]{1,0:T(8,128)S(1)}, u32[]{:S(2)}, u32[]{:S(2)}) collective-permute-start(f32[16,128]{1,0:T(8,128)S(1)} %get-tuple-element.48), channel_id=1, source_target_pairs={{0,129},{1,128},{128,1},{129,0},{2,131},{3,130},{130,3},{131,2},{4... | collective-permute-start | bytes 24584 | tf_op jit(solution)/shard_map/ppermute | solution.py:470
  43.6 0.0 collective-permute-start.6
  43.6 1.4 %shard_map.78.refs_2_ = f32[14,32,640]{2,1,0:T(8,128)S(1)} custom-call(f32[32,128]{1,0:T(8,128)S(1)} %get-tuple-element.44.metric_ref, f32[14,32,640]{2,1,0:T(8,128)S(1)} %get-tuple-element.47.refs_0_.full_ref, f32[14,32,640]{2,1,0:T(8,128)S(1)} %get-tuple-element.49.refs_1_.second_ref), custom_call_target="tpu_custom_call" | custom-call | flops 2000000000 | bytes 2000000 | tf_op jit(solution)/shard_map/pallas_call | solution.py:444
  45.0 0.9 collective-permute-done.7
  46.0 0.1 collective-permute-done.6
  46.2 13.8 %all_to_all.20 = f32[32,16,128]{2,1,0:T(8,128)S(1)} all-to-all(f32[32,16,128]{2,1,0:T(8,128)S(1)} %broadcast_in_dim.12), channel_id=1, replica_groups=mesh['panel'=2,'z'=8,'core'=2,'y'=4,'xh'=2] {'z','y'}, dimensions={0} | all-to-all | bytes 524288 | tf_op jit(solution)/shard_map/all_to_all | solution.py:493
  59.9 5.7 %all-gather.1 = f32[64,16,128]{2,1,0:T(8,128)S(1)} all-gather(f32[32,16,128]{2,1,0:T(8,128)S(1)} %all_to_all.20), channel_id=3, replica_groups=mesh['panel'=2,'z'=8,'core'=2,'y'=4,'xh'=2] {'core'}, dimensions={0}, use_global_device_ids=true | all-gather | bytes 786432 | tf_op jit(solution)/shard_map/all_gather | solution.py:494
  65.7 1.8 %shard_map.79 = (f32[14,32,640]{2,1,0:T(8,128)S(1)}, f32[16,128]{1,0:T(8,128)S(1)}) custom-call(f32[8,640]{1,0:T(8,128)S(1)} %get-tuple-element.32.aux_ref, f32[2,32,16,128]{3,2,1,0:T(8,128)S(1)} %bitcast.13, s32[6,8,128]{2,1,0:T(8,128)S(1)} %get-tuple-element.40.slot_ref, s32[6,8,128]{2,1,0:T(8,128)S(1)} %get-tuple-element.41.tile_ref, ...), custom_call_target="tpu_custom_call" | custom-call | tf_op jit(solution)/shard_map/pallas_call | solution.py:444
  67.5 0.6 collective-permute-start.9
  68.1 0.0 collective-permute-start.8
  68.1 1.4 %shard_map.80.refs_2_ = f32[14,32,640]{2,1,0:T(8,128)S(1)} custom-call(f32[32,128]{1,0:T(8,128)S(1)} %get-tuple-element.44.metric_ref, f32[14,32,640]{2,1,0:T(8,128)S(1)} %get-tuple-element.47.refs_0_.full_ref, f32[14,32,640]{2,1,0:T(8,128)S(1)} %get-tuple-element.52.refs_1_.third_ref), custom_call_target="tpu_custom_call" | custom-call | flops 2000000000 | bytes 2000000 | tf_op jit(solution)/shard_map/pallas_call | solution.py:444
  69.5 1.7 %collective-permute-done.9 = f32[16,128]{1,0:T(8,128)S(1)} collective-permute-done((f32[16,128]{1,0:T(8,128)S(1)}, f32[16,128]{1,0:T(8,128)S(1)}, u32[]{:S(2)}, u32[]{:S(2)}) %collective-permute-start.9) | collective-permute-done | bytes 8224 | tf_op jit(solution)/shard_map/ppermute | solution.py:470
  71.2 0.0 collective-permute-done.8
  71.2 13.6 %all_to_all.21 = f32[32,16,128]{2,1,0:T(8,128)S(1)} all-to-all(f32[32,16,128]{2,1,0:T(8,128)S(1)} %broadcast_in_dim.13), channel_id=1, replica_groups=mesh['panel'=2,'z'=8,'core'=2,'y'=4,'xh'=2] {'z','y'}, dimensions={0} | all-to-all | bytes 524288 | tf_op jit(solution)/shard_map/all_to_all | solution.py:493
  84.8 5.3 %all-gather.2 = f32[64,16,128]{2,1,0:T(8,128)S(1)} all-gather(f32[32,16,128]{2,1,0:T(8,128)S(1)} %all_to_all.21), channel_id=4, replica_groups=mesh['panel'=2,'z'=8,'core'=2,'y'=4,'xh'=2] {'core'}, dimensions={0}, use_global_device_ids=true | all-gather | bytes 786432 | tf_op jit(solution)/shard_map/all_gather | solution.py:494
  90.1 1.8 %shard_map.81 = (f32[14,32,640]{2,1,0:T(8,128)S(1)}, f32[16,128]{1,0:T(8,128)S(1)}) custom-call(f32[8,640]{1,0:T(8,128)S(1)} %get-tuple-element.32.aux_ref, f32[2,32,16,128]{3,2,1,0:T(8,128)S(1)} %bitcast.12, s32[6,8,128]{2,1,0:T(8,128)S(1)} %get-tuple-element.40.slot_ref, s32[6,8,128]{2,1,0:T(8,128)S(1)} %get-tuple-element.41.tile_ref, ...), custom_call_target="tpu_custom_call" | custom-call | tf_op jit(solution)/shard_map/pallas_call | solution.py:444
  91.8 1.4 %collective-permute-start.11 = (f32[16,128]{1,0:T(8,128)S(1)}, f32[16,128]{1,0:T(8,128)S(1)}, u32[]{:S(2)}, u32[]{:S(2)}) collective-permute-start(f32[16,128]{1,0:T(8,128)S(1)} %get-tuple-element.54), channel_id=1, source_target_pairs={{0,129},{1,128},{128,1},{129,0},{2,131},{3,130},{130,3},{131,2},{4... | collective-permute-start | bytes 24584 | tf_op jit(solution)/shard_map/ppermute | solution.py:470
  93.2 0.0 collective-permute-start.10
  93.2 1.2 %shard_map.82 = (f32[14,24,640]{2,1,0:T(8,128)S(1)}, f32[14,24,640]{2,1,0:T(8,128)S(1)}) custom-call(f32[32,128]{1,0:T(8,128)S(1)} %get-tuple-element.44.metric_ref, f32[14,32,640]{2,1,0:T(8,128)S(1)} %get-tuple-element.47.refs_0_.full_ref, f32[14,32,640]{2,1,0:T(8,128)S(1)} %get-tuple-element.49.refs_1_.second_ref, ...), custom_call_target="tpu_custom_call" | custom-call | flops 2000000000 | bytes 2000000 | tf_op jit(solution)/shard_map/pallas_call | solution.py:444
  94.4 1.2 collective-permute-done.11
  95.6 0.1 collective-permute-done.10
  95.8 14.0 %all_to_all.22 = f32[32,16,128]{2,1,0:T(8,128)S(1)} all-to-all(f32[32,16,128]{2,1,0:T(8,128)S(1)} %broadcast_in_dim.14), channel_id=1, replica_groups=mesh['panel'=2,'z'=8,'core'=2,'y'=4,'xh'=2] {'z','y'}, dimensions={0} | all-to-all | bytes 524288 | tf_op jit(solution)/shard_map/all_to_all | solution.py:493
  109.8 5.6 %all-gather.3 = f32[64,16,128]{2,1,0:T(8,128)S(1)} all-gather(f32[32,16,128]{2,1,0:T(8,128)S(1)} %all_to_all.22), channel_id=5, replica_groups=mesh['panel'=2,'z'=8,'core'=2,'y'=4,'xh'=2] {'core'}, dimensions={0}, use_global_device_ids=true | all-gather | bytes 786432 | tf_op jit(solution)/shard_map/all_gather | solution.py:494
  115.4 2.2 %shard_map.83 = f32[14,24,576]{2,1,0:T(8,128)} custom-call(f32[8,640]{1,0:T(8,128)S(1)} %get-tuple-element.32.aux_ref, f32[2,32,16,128]{3,2,1,0:T(8,128)S(1)} %bitcast.11, s32[6,8,128]{2,1,0:T(8,128)S(1)} %get-tuple-element.40.slot_ref, s32[6,8,128]{2,1,0:T(8,128)S(1)} %get-tuple-element.41.tile_ref, f32[6,8,128]{2,1,0:T(8,128)S(1)} %get-tuple-element.42.cos_ref, ...), custom_call_target="tpu_custom_call" | custom-call | tf_op jit(solution)/shard_map/pallas_call | solution.py:444
  (8 shorter events, 0.1 us)
Async XLA Ops:
  2.0 5.7 %collective-permute-start.2 = (f32[8,8,640]{2,1,0:T(8,128)S(1)}, f32[8,8,640]{2,1,0:T(8,128)S(1)}, u32[]{:S(2)}, u32[]{:S(2)}) collective-permute-start(f32[8,8,640]{2,1,0:T(8,128)S(1)} %get-tuple-element.35), channel_id=1, source_target_pairs={{0,8},{8,0},{16,24},{24,16},{32,40},{40,32},{48,56},{56,48},{64,72... | collective-permute-start | bytes 491528 | tf_op jit(solution)/shard_map/ppermute | solution.py:470
  5.3 4.7 %collective-permute-start.3 = (f32[8,8,640]{2,1,0:T(8,128)S(1)}, f32[8,8,640]{2,1,0:T(8,128)S(1)}, u32[]{:S(2)}, u32[]{:S(2)}) collective-permute-start(f32[8,8,640]{2,1,0:T(8,128)S(1)} %get-tuple-element.36), channel_id=1, source_target_pairs={{0,120},{8,16},{16,8},{24,32},{32,24},{40,48},{48,40},{56,64},{64,... | collective-permute-start | bytes 491528 | tf_op jit(solution)/shard_map/ppermute | solution.py:470
  5.3 8.5 %collective-permute-start.1 = (f32[16,128]{1,0:T(8,128)S(1)}, f32[16,128]{1,0:T(8,128)S(1)}, u32[]{:S(2)}, u32[]{:S(2)}) collective-permute-start(f32[16,128]{1,0:T(8,128)S(1)} %get-tuple-element.33), channel_id=1, source_target_pairs={{0,129},{1,128},{128,1},{129,0},{2,131},{3,130},{130,3},{131,2},{4... | collective-permute-start | bytes 24584 | tf_op jit(solution)/shard_map/ppermute | solution.py:470
  7.7 6.1 %collective-permute-start = (f32[16,128]{1,0:T(8,128)S(1)}, f32[16,128]{1,0:T(8,128)S(1)}, u32[]{:S(2)}, u32[]{:S(2)}) collective-permute-start(f32[16,128]{1,0:T(8,128)S(1)} %get-tuple-element.33), channel_id=1, source_target_pairs={{0,128},{1,129},{128,0},{129,1},{2,130},{3,131},{130,2},{131,3},{4... | collective-permute-start | bytes 24584 | tf_op jit(solution)/shard_map/ppermute | solution.py:470
  10.2 14.3 %collective-permute-start.5 = (f32[32,128]{1,0:T(8,128)S(1)}, f32[32,128]{1,0:T(8,128)S(1)}, u32[]{:S(2)}, u32[]{:S(2)}) collective-permute-start(f32[32,128]{1,0:T(8,128)S(1)} %get-tuple-element.39), channel_id=1, source_target_pairs={{0,7},{1,2},{2,1},{3,4},{4,3},{5,6},{6,5},{7,0},{8,15},{9,10},{10,... | collective-permute-start | bytes 49160 | tf_op jit(solution)/shard_map/ppermute | solution.py:470
  13.8 10.8 %collective-permute-start.4 = (f32[32,128]{1,0:T(8,128)S(1)}, f32[32,128]{1,0:T(8,128)S(1)}, u32[]{:S(2)}, u32[]{:S(2)}) collective-permute-start(f32[32,128]{1,0:T(8,128)S(1)} %get-tuple-element.37), channel_id=1, source_target_pairs={{0,1},{1,0},{2,3},{3,2},{4,5},{5,4},{6,7},{7,6},{8,9},{9,8},{10,11... | collective-permute-start | bytes 49160 | tf_op jit(solution)/shard_map/ppermute | solution.py:470
  14.5 20.4 %all-to-all-start = ((f32[32,16,128]{2,1,0:T(8,128)}), f32[32,16,128]{2,1,0:T(8,128)S(1)}, u32[]{:S(2)}, u32[]{:S(2)}) async-start(f32[32,16,128]{2,1,0:T(8,128)} %broadcast_in_dim.11), calls=%async_computation | async-start | bytes 524288 | tf_op jit(solution)/shard_map/all_to_all | solution.py:493
  42.2 3.7 %collective-permute-start.7 = (f32[16,128]{1,0:T(8,128)S(1)}, f32[16,128]{1,0:T(8,128)S(1)}, u32[]{:S(2)}, u32[]{:S(2)}) collective-permute-start(f32[16,128]{1,0:T(8,128)S(1)} %get-tuple-element.48), channel_id=1, source_target_pairs={{0,129},{1,128},{128,1},{129,0},{2,131},{3,130},{130,3},{131,2},{4... | collective-permute-start | bytes 24584 | tf_op jit(solution)/shard_map/ppermute | solution.py:470
  43.6 2.5 %collective-permute-start.6 = (f32[16,128]{1,0:T(8,128)S(1)}, f32[16,128]{1,0:T(8,128)S(1)}, u32[]{:S(2)}, u32[]{:S(2)}) collective-permute-start(f32[16,128]{1,0:T(8,128)S(1)} %get-tuple-element.48), channel_id=1, source_target_pairs={{0,128},{1,129},{128,0},{129,1},{2,130},{3,131},{130,2},{131,3},{4... | collective-permute-start | bytes 24584 | tf_op jit(solution)/shard_map/ppermute | solution.py:470
  67.5 3.7 %collective-permute-start.9 = (f32[16,128]{1,0:T(8,128)S(1)}, f32[16,128]{1,0:T(8,128)S(1)}, u32[]{:S(2)}, u32[]{:S(2)}) collective-permute-start(f32[16,128]{1,0:T(8,128)S(1)} %get-tuple-element.51), channel_id=1, source_target_pairs={{0,129},{1,128},{128,1},{129,0},{2,131},{3,130},{130,3},{131,2},{4... | collective-permute-start | bytes 24584 | tf_op jit(solution)/shard_map/ppermute | solution.py:470
  68.1 3.1 %collective-permute-start.8 = (f32[16,128]{1,0:T(8,128)S(1)}, f32[16,128]{1,0:T(8,128)S(1)}, u32[]{:S(2)}, u32[]{:S(2)}) collective-permute-start(f32[16,128]{1,0:T(8,128)S(1)} %get-tuple-element.51), channel_id=1, source_target_pairs={{0,128},{1,129},{128,0},{129,1},{2,130},{3,131},{130,2},{131,3},{4... | collective-permute-start | bytes 24584 | tf_op jit(solution)/shard_map/ppermute | solution.py:470
  91.8 3.7 %collective-permute-start.11 = (f32[16,128]{1,0:T(8,128)S(1)}, f32[16,128]{1,0:T(8,128)S(1)}, u32[]{:S(2)}, u32[]{:S(2)}) collective-permute-start(f32[16,128]{1,0:T(8,128)S(1)} %get-tuple-element.54), channel_id=1, source_target_pairs={{0,129},{1,128},{128,1},{129,0},{2,131},{3,130},{130,3},{131,2},{4... | collective-permute-start | bytes 24584 | tf_op jit(solution)/shard_map/ppermute | solution.py:470
  93.2 2.5 %collective-permute-start.10 = (f32[16,128]{1,0:T(8,128)S(1)}, f32[16,128]{1,0:T(8,128)S(1)}, u32[]{:S(2)}, u32[]{:S(2)}) collective-permute-start(f32[16,128]{1,0:T(8,128)S(1)} %get-tuple-element.54), channel_id=1, source_target_pairs={{0,128},{1,129},{128,0},{129,1},{2,130},{3,131},{130,2},{131,3},{4... | collective-permute-start | bytes 24584 | tf_op jit(solution)/shard_map/ppermute | solution.py:470

commit v3 on v2

--- a/solution.py
+++ b/solution.py
@@ -87,7 +87,7 @@
     for copy in copies[:-1]:
         copy.wait()
     panel = flags_ref[2, 0]
-    far_south = flags_ref[0, 0] == NT // CT - 1
+    far_south = flags_ref[0, 0] >= NT // CT - 2
     far_east = flags_ref[1, 0] == 7
     aux_ref[...] = jnp.zeros((8, COLS), jnp.float32)
     for i, (table, far) in enumerate(
@@ -152,8 +152,24 @@
     return jnp.where(row < HALO, pltpu.roll(from_south, HALO, 0), from_north)
 
 
-def side_kernel(aux_ref, state_ref, lat_inner_ref, lat_cross_ref, inner_ref, cross_ref):
+def column_list(aux_ref, lat_inner_ref, lat_cross_ref):
+    lane = lane_of((8, LANES))
+    block = aux_ref[:, 0:LANES]
+    south, north = ordered(place_of(aux_ref)[0], lat_inner_ref[7, :, 0:LANES], lat_cross_ref[7, :, 0:LANES])
+    block = jnp.where((lane >= CT) & (lane < CT + HALO), pltpu.roll(south, CT, 1), block)
+    return jnp.where((lane >= ROWS - HALO) & (lane < ROWS), pltpu.roll(north, 8, 1), block)
+
+
+def donor_places(source):
+    whole = jnp.floor((source + 0.5) * (1.0 / SLOTS))
+    tile = whole.astype(jnp.int32)
+    return (source - whole * SLOTS).astype(jnp.int32) + 64 * (tile & 1), tile // 2
+
+
+def side_kernel(aux_ref, state_ref, lat_inner_ref, lat_cross_ref, inner_ref, cross_ref, column_ref):
     shape = (8, LANES)
+    source = jnp.broadcast_to(column_list(aux_ref, lat_inner_ref, lat_cross_ref)[2:3, :], shape)
+    column_ref[0:8, :], column_ref[8:16, :] = donor_places(source)
     lat, lon = place_of(aux_ref)
     lane = lane_of(shape)
     row = row_of(shape)
@@ -218,16 +234,10 @@
             source = jnp.broadcast_to(block[0:1, :], shape)
             angle = jnp.broadcast_to(block[1:2, :], shape)
         else:
-            block = aux_ref[:, 0:LANES]
-            south, north = ordered(lat, lat_inner_ref[7, :, 0:LANES], lat_cross_ref[7, :, 0:LANES])
-            block = jnp.where((lane >= CT) & (lane < CT + HALO), pltpu.roll(south, CT, 1), block)
-            block = jnp.where((lane >= 28) & (lane < 32), pltpu.roll(north, 8, 1), block)
+            block = column_list(aux_ref, lat_inner_ref, lat_cross_ref)
             source = jnp.broadcast_to(block[2:3, :], shape)
             angle = jnp.broadcast_to(block[3:4, :], shape)
-        whole = jnp.floor((source + 0.5) * (1.0 / SLOTS))
-        tile = whole.astype(jnp.int32)
-        slot_ref[t] = (source - whole * SLOTS).astype(jnp.int32) + 64 * (tile & 1)
-        tile_ref[t] = tile // 2
+        slot_ref[t], tile_ref[t] = donor_places(source)
         cos_ref[t] = jnp.cos(angle)
         sin_ref[t] = jnp.sin(angle)
     line = row_of((ROWS, LANES))
@@ -236,20 +246,30 @@
     metric_ref[...] = 1.0 / jnp.sin(theta)
 
 
-def pick_ghosts(donor_ref, slot_ref, tile_ref, cos_ref, sin_ref):
+def pick_kernel(aux_ref, donor_ref, slot_ref, tile_ref, other_ref, out_ref):
+    mine = 4 * (place_of(aux_ref)[0] & 1)
+    count = LANE_TILES + 1
+    tables = [(slot_ref[t], tile_ref[t]) for t in range(count)] + [(other_ref[0:8, :], other_ref[8:16, :])]
+    for t, (slots, pairs) in enumerate(tables):
+        pairs = pairs - mine
+        for half in range(2):
+            rows = slice(half * 8, half * 8 + 8)
+            total = jnp.zeros((8, LANES), jnp.float32)
+            for v in range(TILES // 4):
+                block = donor_ref[v, rows, :]
+                total = jnp.where(pairs == v // 4 * 8 + v % 4, lane_gather(block, slots), total)
+            out_ref[t, rows, :] = total
+
+
+def turned_ghosts(share_ref, other_ref, cos_ref, sin_ref):
     shape = (8, LANES)
     row = row_of(shape)
     count = LANE_TILES + 1
     low, high = [], []
     for t in range(count):
-        slots, pairs = slot_ref[t], tile_ref[t]
-        for half, out in ((0, low), (1, high)):
-            total = jnp.zeros(shape, jnp.float32)
-            for v in range(TILES // 2):
-                z, core, y = v // 8, v // 4 % 2, v % 4
-                block = donor_ref[core, z * 4 + y, half * 8 : half * 8 + 8, :]
-                total = jnp.where(pairs == v, lane_gather(block, slots), total)
-            out.append(total)
+        theirs = t if t < LANE_TILES else count
+        for out, rows in ((low, slice(0, 8)), (high, slice(8, 16))):
+            out.append(share_ref[t, rows, :] + other_ref[theirs, rows, :])
     ghosts = []
     for t in range(count):
         cosine, sine = cos_ref[t], sin_ref[t]
@@ -386,11 +406,11 @@
 
 
 def rim_kernel(
-    factor, aux_ref, donor_ref, slot_ref, tile_ref, cos_ref, sin_ref, metric_ref, index_ref, weight_ref, *refs
+    factor, aux_ref, share_ref, other_ref, cos_ref, sin_ref, metric_ref, index_ref, weight_ref, *refs
 ):
     full_ref, now_ref, inner_ref, next_ref, packet_ref, line_ref, column_ref = refs if len(refs) == 7 else refs[:1] + refs
     place = place_of(aux_ref)
-    keep_ghosts(place[1], pick_ghosts(donor_ref, slot_ref, tile_ref, cos_ref, sin_ref), line_ref, column_ref)
+    keep_ghosts(place[1], turned_ghosts(share_ref, other_ref, cos_ref, sin_ref), line_ref, column_ref)
     next_ref[...] = inner_ref[...]
 
     def store(f, rows, cols, value):
@@ -420,11 +440,11 @@
 
 
 def last_rim_kernel(
-    aux_ref, donor_ref, slot_ref, tile_ref, cos_ref, sin_ref, metric_ref, base_ref, inner_ref, now_ref,
+    aux_ref, share_ref, other_ref, cos_ref, sin_ref, metric_ref, base_ref, inner_ref, now_ref,
     out_ref, line_ref, column_ref,
 ):
     place = place_of(aux_ref)
-    keep_ghosts(place[1], pick_ghosts(donor_ref, slot_ref, tile_ref, cos_ref, sin_ref), line_ref, column_ref)
+    keep_ghosts(place[1], turned_ghosts(share_ref, other_ref, cos_ref, sin_ref), line_ref, column_ref)
     for f in range(FIELDS):
         out_ref[f] = inner_ref[f, :, 0:CP]
 
@@ -486,12 +506,13 @@
     return jnp.where(second == (lax.axis_index("xh") == 1), same, other)
 
 
-def spread_packets(pair, inner):
-    if inner is not None:
-        pair, _ = lax.optimization_barrier((pair, inner))
+def spread_packets(pair):
     count = SIZES["z"] * SIZES["y"]
-    spread = lax.all_to_all(jnp.broadcast_to(pair[None], (count,) + pair.shape), ("z", "y"), 0, 0)
-    return lax.all_gather(spread, "core")
+    return lax.all_to_all(jnp.broadcast_to(pair[None], (count,) + pair.shape), ("z", "y"), 0, 0)
+
+
+def other_core(value):
+    return permute(value, ("core",), lambda q: (1 - q[0],))
 
 
 def on_device(state, pack_cell, pack_frac, ns_source, we_source, ns_turn, we_turn):
@@ -524,37 +545,51 @@
     )
     lat_inner = within(lat_inner, LAT)
     lat_cross = between(lat_cross, LAT)
-    lon_inner, lon_cross = call(side_kernel, [aux, tile, lat_inner, lat_cross], [side, side])
-    pair, _ = lax.optimization_barrier((swap_packets(packet), lon_inner))
+    lon_inner, lon_cross, column = call(
+        side_kernel, [aux, tile, lat_inner, lat_cross], [side, side, ((16, LANES), jnp.int32)], cost=8_000_000
+    )
+    column = other_core(column)
+    pair = swap_packets(packet)
     lon_inner = within(lon_inner, LON)
     lon_cross = between(lon_cross, LON)
+    donors = spread_packets(pair)
+    donors, lon_inner, lon_cross = lax.optimization_barrier((donors, lon_inner, lon_cross))
     points = (LANE_TILES + 1,) + vreg
     full, slot, where, cosine, sine, metric = call(
         frame_kernel,
         [aux, tile, lat_inner, lat_cross, lon_inner, lon_cross],
         [whole, (points, jnp.int32), (points, jnp.int32), (points, f32), (points, f32), ((ROWS, LANES), f32)],
     )
-    tables = [slot, where, cosine, sine, metric]
+    lists = [slot, where, column]
     kept = [pltpu.VMEM((16, COLS), f32), pltpu.VMEM((FIELDS, ROWS, LANES), f32)]
+
+    def ghost_tables(donors):
+        (share,) = call(pick_kernel, [aux, donors] + lists, [((LANE_TILES + 2, 16, LANES), f32)])
+        return [aux, share, other_core(share), cosine, sine, metric]
+
     states = [full]
     for factor in (time_step / 2, time_step / 2, time_step):
-        if len(states) > 1:
+        now = [states[-1]] if len(states) > 1 else []
+        if now:
             pair = swap_packets(packet)
-        now = [states[-1]] if len(states) > 1 else []
-        (inner,) = call(functools.partial(inner_kernel, factor), [metric, full] + now, [whole], cost=2_000_000 if now else 50_000_000)
+        (inner,) = call(functools.partial(inner_kernel, factor), [metric, full] + now, [whole], cost=2_000_000)
+        if now:
+            pair, inner = lax.optimization_barrier((pair, inner))
+            donors = spread_packets(pair)
         after, packet = call(
             functools.partial(rim_kernel, factor),
-            [aux, spread_packets(pair, inner if now else None)] + tables + [index, weight, full] + now + [inner],
+            ghost_tables(donors) + [index, weight, full] + now + [inner],
             [whole, packed],
-                scratch=kept,
+            scratch=kept,
         )
         states.append(after)
     pair = swap_packets(packet)
     inner_shape = ((FIELDS, CT, COLS), f32)
     base, inner = call(last_inner_kernel, [metric] + states, [inner_shape, inner_shape], cost=2_000_000)
+    pair, inner = lax.optimization_barrier((pair, inner))
     (result,) = call(
         last_rim_kernel,
-        [aux, spread_packets(pair, inner)] + tables + [base, inner, states[-1]],
+        ghost_tables(spread_packets(pair)) + [base, inner, states[-1]],
         [((FIELDS, CT, CP), f32)],
         scratch=kept,
     )

time: 118 us -> 112 us (0.949)
  starting transfers between devices: 22.6 us -> 45.7 us
  blocking collectives: 63.5 us -> 43.9 us
  waiting for transfers between devices: 15.2 us -> 6.96 us
  Pallas kernels: 15.2 us -> 14 us
    ppermute x12 -> x17, starting transfers between devices: 12.6 us -> 35.4 us  [permute(): return lax.ppermute(value, axes if len(axes) > 1 else axes[0], pairs)]
    all_gather x4 -> x0, blocking collectives: 22.1 us -> none  [spread_packets(): return lax.all_gather(spread, 'core')]
    all_to_all x1, waiting for transfers between devices: 8.68 us -> 1.74 us  [spread_packets(): lax.all_to_all(jnp.broadcast_to(pair[None], (count,) + pair.shape), ('z',...]
    all_to_all x3, blocking collectives: 41.4 us -> 43.9 us  [spread_packets(): lax.all_to_all(jnp.broadcast_to(pair[None], (count,) + pair.shape), ('z',...]
    ppermute x12 -> x17, waiting for transfers between devices: 6.49 us -> 5.22 us  [permute(): return lax.ppermute(value, axes if len(axes) > 1 else axes[0], pairs)]
    pallas_call x11 -> x15, Pallas kernels: 15.2 us -> 14 us  [call(): pl.pallas_call(kernel, out_shape=shapes, in_specs=[hbm if i in left else...]
  transfers between devices with their start and end apart: 13 -> 18, of which waited for: 7 -> 7; matrix products, arithmetic and copies ran while one was open for 1% -> 1% of each run, Pallas kernels for 5% -> 5%
where the time goes in v3:
time: 112 us
  starting transfers between devices  45.7 us (41%)
  blocking collectives  43.9 us (39%)
  Pallas kernels  14 us (12%)
  waiting for transfers between devices  6.96 us (6%)
    all_to_all x3, blocking collectives, spread_packets(): lax.all_to_all(jnp.broadcast_to(pair[None], (count,) + pair.shape), ('z',...  43.9 us
    ppermute x17, starting transfers between devices, permute(): return lax.ppermute(value, axes if len(axes) > 1 else axes[0], pairs)  35.4 us
    pallas_call x15, Pallas kernels, call(): pl.pallas_call(kernel, out_shape=shapes, in_specs=[hbm if i in left else...  14 us
    all_to_all x1, starting transfers between devices, spread_packets(): lax.all_to_all(jnp.broadcast_to(pair[None], (count,) + pair.shape), ('z',...  10.3 us
    ppermute x17, waiting for transfers between devices, permute(): return lax.ppermute(value, axes if len(axes) > 1 else axes[0], pairs)  5.22 us
  transfers between devices with their start and end apart: 18, of which 7 were waited for; matrix products, arithmetic and copies ran while one was open for 1% of the time, Pallas kernels for 5%

profile of v3, /device:TPU:1, one launch (start us, length us, event | category | flops | bytes accessed | tf_op | source)
XLA Modules:
  0.0 111.7 jit_solution(2568821129546251439)
XLA Ops:
  0.0 0.1 stack.20
  0.1 0.1 broadcast_in_dim.10.flags_ref
  0.2 1.8 %shard_map.73 = (f32[14,24,576]{2,1,0:T(8,128)S(1)}, f32[8,640]{1,0:T(8,128)S(1)}, f32[16,128]{1,0:T(8,128)S(1)}, f32[8,8,640]{2,1,0:T(8,128)S(1)}, f32[8,8,640]...) custom-call(s32[8,128]{1,0:T(8,128)S(1)} %broadcast_in_dim.10.flags_ref, ...), custom_call_target="tpu_custom_call" | custom-call | tf_op jit(solution)/shard_map/pallas_call | solution.py:464
  2.0 2.1 %collective-permute-start = (f32[16,128]{1,0:T(8,128)S(1)}, f32[16,128]{1,0:T(8,128)S(1)}, u32[]{:S(2)}, u32[]{:S(2)}) collective-permute-start(f32[16,128]{1,0:T(8,128)S(1)} %get-tuple-element.39), channel_id=1, source_target_pairs={{0,128},{1,129},{128,0},{129,1},{2,130},{3,131},{130,2},{131,3},{4... | collective-permute-start | bytes 24584 | tf_op jit(solution)/shard_map/ppermute | solution.py:490
  4.1 1.8 %collective-permute-start.1 = (f32[16,128]{1,0:T(8,128)S(1)}, f32[16,128]{1,0:T(8,128)S(1)}, u32[]{:S(2)}, u32[]{:S(2)}) collective-permute-start(f32[16,128]{1,0:T(8,128)S(1)} %get-tuple-element.39), channel_id=1, source_target_pairs={{0,129},{1,128},{128,1},{129,0},{2,131},{3,130},{130,3},{131,2},{4... | collective-permute-start | bytes 24584 | tf_op jit(solution)/shard_map/ppermute | solution.py:490
  5.9 1.2 %collective-permute-start.2 = (f32[8,8,640]{2,1,0:T(8,128)S(1)}, f32[8,8,640]{2,1,0:T(8,128)S(1)}, u32[]{:S(2)}, u32[]{:S(2)}) collective-permute-start(f32[8,8,640]{2,1,0:T(8,128)S(1)} %get-tuple-element.41), channel_id=1, source_target_pairs={{0,8},{8,0},{16,24},{24,16},{32,40},{40,32},{48,56},{56,48},{64,72... | collective-permute-start | bytes 491528 | tf_op jit(solution)/shard_map/ppermute | solution.py:490
  7.1 1.5 %collective-permute-start.3 = (f32[8,8,640]{2,1,0:T(8,128)S(1)}, f32[8,8,640]{2,1,0:T(8,128)S(1)}, u32[]{:S(2)}, u32[]{:S(2)}) collective-permute-start(f32[8,8,640]{2,1,0:T(8,128)S(1)} %get-tuple-element.42), channel_id=1, source_target_pairs={{0,120},{8,16},{16,8},{24,32},{32,24},{40,48},{48,40},{56,64},{64,... | collective-permute-start | bytes 491528 | tf_op jit(solution)/shard_map/ppermute | solution.py:490
  8.7 0.0 collective-permute-done
  8.7 0.0 collective-permute-done.1
  8.7 0.7 broadcast_in_dim.11
  9.4 10.3 %all-to-all-start = ((f32[32,16,128]{2,1,0:T(8,128)}), f32[32,16,128]{2,1,0:T(8,128)S(1)}, u32[]{:S(2)}, u32[]{:S(2)}) async-start(f32[32,16,128]{2,1,0:T(8,128)} %broadcast_in_dim.11), calls=%async_computation | async-start | bytes 524288 | tf_op jit(solution)/shard_map/all_to_all | solution.py:511
  19.7 0.0 collective-permute-done.2.lat_inner_ref
  19.8 0.0 collective-permute-done.3.lat_cross_ref
  19.8 0.2 shard_map.74
  20.0 1.3 %collective-permute-start.4 = (f32[32,128]{1,0:T(8,128)S(1)}, f32[32,128]{1,0:T(8,128)S(1)}, u32[]{:S(2)}, u32[]{:S(2)}) collective-permute-start(f32[32,128]{1,0:T(8,128)S(1)} %get-tuple-element.43), channel_id=1, source_target_pairs={{0,1},{1,0},{2,3},{3,2},{4,5},{5,4},{6,7},{7,6},{8,9},{9,8},{10,11... | collective-permute-start | bytes 49160 | tf_op jit(solution)/shard_map/ppermute | solution.py:490
  21.3 3.9 %collective-permute-start.5 = (f32[32,128]{1,0:T(8,128)S(1)}, f32[32,128]{1,0:T(8,128)S(1)}, u32[]{:S(2)}, u32[]{:S(2)}) collective-permute-start(f32[32,128]{1,0:T(8,128)S(1)} %get-tuple-element.44), channel_id=1, source_target_pairs={{0,7},{1,2},{2,1},{3,4},{4,3},{5,6},{6,5},{7,0},{8,15},{9,10},{10,... | collective-permute-start | bytes 49160 | tf_op jit(solution)/shard_map/ppermute | solution.py:490
  25.2 3.2 %collective-permute-start.6 = (s32[16,128]{1,0:T(8,128)S(1)}, s32[16,128]{1,0:T(8,128)S(1)}, u32[]{:S(2)}, u32[]{:S(2)}) collective-permute-start(s32[16,128]{1,0:T(8,128)S(1)} %get-tuple-element.50), channel_id=1, source_target_pairs={{0,8},{8,0},{1,9},{9,1},{2,10},{10,2},{3,11},{11,3},{4,12},{12,4},... | collective-permute-start | bytes 24584 | tf_op jit(solution)/shard_map/ppermute | solution.py:490
  28.4 0.0 collective-permute-done.4.lon_inner_ref
  28.4 0.0 collective-permute-done.5.lon_cross_ref
  28.4 1.7 %all-to-all-done.donor_ref = f32[32,16,128]{2,1,0:T(8,128)S(1)} async-done(((f32[32,16,128]{2,1,0:T(8,128)}), f32[32,16,128]{2,1,0:T(8,128)S(1)}, u32[]{:S(2)}, u32[]{:S(2)}) %all-to-all-start) | async-done | bytes 262176 | tf_op jit(solution)/shard_map/all_to_all | solution.py:511
  30.2 0.3 shard_map.75
  30.4 0.0 collective-permute-done.6.other_ref
  30.4 0.6 shard_map.76.share_ref
  31.0 3.8 %collective-permute-start.7 = (f32[7,16,128]{2,1,0:T(8,128)S(1)}, f32[7,16,128]{2,1,0:T(8,128)S(1)}, u32[]{:S(2)}, u32[]{:S(2)}) collective-permute-start(f32[7,16,128]{2,1,0:T(8,128)S(1)} %shard_map.76.share_ref), channel_id=1, source_target_pairs={{0,8},{8,0},{1,9},{9,1},{2,10},{10,2},{3,11},{11,3},{4,12},{12,4},... | collective-permute-start | bytes 172040 | tf_op jit(solution)/shard_map/ppermute | solution.py:490
  34.8 1.4 %shard_map.77.refs_1_ = f32[14,32,640]{2,1,0:T(8,128)S(1)} custom-call(f32[32,128]{1,0:T(8,128)S(1)} %get-tuple-element.53.metric_ref, f32[14,32,640]{2,1,0:T(8,128)S(1)} %get-tuple-element.56.refs_0_.full_ref), custom_call_target="tpu_custom_call" | custom-call | flops 2000000000 | bytes 2000000 | tf_op jit(solution)/shard_map/pallas_call | solution.py:464
  36.2 0.0 collective-permute-done.7.other_ref
  36.2 0.9 shard_map.78
  37.1 0.1 collective-permute-start.8
  37.2 1.5 %collective-permute-start.9 = (f32[16,128]{1,0:T(8,128)S(1)}, f32[16,128]{1,0:T(8,128)S(1)}, u32[]{:S(2)}, u32[]{:S(2)}) collective-permute-start(f32[16,128]{1,0:T(8,128)S(1)} %get-tuple-element.57), channel_id=1, source_target_pairs={{0,129},{1,128},{128,1},{129,0},{2,131},{3,130},{130,3},{131,2},{4... | collective-permute-start | bytes 24584 | tf_op jit(solution)/shard_map/ppermute | solution.py:490
  38.7 1.4 %shard_map.79.refs_2_ = f32[14,32,640]{2,1,0:T(8,128)S(1)} custom-call(f32[32,128]{1,0:T(8,128)S(1)} %get-tuple-element.53.metric_ref, f32[14,32,640]{2,1,0:T(8,128)S(1)} %get-tuple-element.56.refs_0_.full_ref, f32[14,32,640]{2,1,0:T(8,128)S(1)} %get-tuple-element.58.refs_1_.second_ref), custom_call_target="tpu_custom_call" | custom-call | flops 2000000000 | bytes 2000000 | tf_op jit(solution)/shard_map/pallas_call | solution.py:464
  40.1 0.0 collective-permute-done.8
  40.1 0.9 collective-permute-done.9
  41.0 16.8 %all_to_all.20.donor_ref = f32[32,16,128]{2,1,0:T(8,128)S(1)} all-to-all(f32[32,16,128]{2,1,0:T(8,128)S(1)} %broadcast_in_dim.12), channel_id=1, replica_groups=mesh['panel'=2,'z'=8,'core'=2,'y'=4,'xh'=2] {'z','y'}, dimensions={0} | all-to-all | bytes 524288 | tf_op jit(solution)/shard_map/all_to_all | solution.py:511
  57.8 0.6 shard_map.80.share_ref
  58.4 3.8 %collective-permute-start.10 = (f32[7,16,128]{2,1,0:T(8,128)S(1)}, f32[7,16,128]{2,1,0:T(8,128)S(1)}, u32[]{:S(2)}, u32[]{:S(2)}) collective-permute-start(f32[7,16,128]{2,1,0:T(8,128)S(1)} %shard_map.80.share_ref), channel_id=1, source_target_pairs={{0,8},{8,0},{1,9},{9,1},{2,10},{10,2},{3,11},{11,3},{4,12},{12,4},... | collective-permute-start | bytes 172040 | tf_op jit(solution)/shard_map/ppermute | solution.py:490
  62.2 0.9 collective-permute-done.10.other_ref
  63.1 0.9 shard_map.81
  64.0 0.0 collective-permute-start.11
  64.0 1.9 %collective-permute-start.12 = (f32[16,128]{1,0:T(8,128)S(1)}, f32[16,128]{1,0:T(8,128)S(1)}, u32[]{:S(2)}, u32[]{:S(2)}) collective-permute-start(f32[16,128]{1,0:T(8,128)S(1)} %get-tuple-element.61), channel_id=1, source_target_pairs={{0,129},{1,128},{128,1},{129,0},{2,131},{3,130},{130,3},{131,2},{4... | collective-permute-start | bytes 24584 | tf_op jit(solution)/shard_map/ppermute | solution.py:490
  66.0 1.4 %shard_map.82.refs_2_ = f32[14,32,640]{2,1,0:T(8,128)S(1)} custom-call(f32[32,128]{1,0:T(8,128)S(1)} %get-tuple-element.53.metric_ref, f32[14,32,640]{2,1,0:T(8,128)S(1)} %get-tuple-element.56.refs_0_.full_ref, f32[14,32,640]{2,1,0:T(8,128)S(1)} %get-tuple-element.62.refs_1_.third_ref), custom_call_target="tpu_custom_call" | custom-call | flops 2000000000 | bytes 2000000 | tf_op jit(solution)/shard_map/pallas_call | solution.py:464
  67.4 0.0 collective-permute-done.11
  67.4 0.5 collective-permute-done.12
  67.9 13.6 %all_to_all.21.donor_ref = f32[32,16,128]{2,1,0:T(8,128)S(1)} all-to-all(f32[32,16,128]{2,1,0:T(8,128)S(1)} %broadcast_in_dim.13), channel_id=1, replica_groups=mesh['panel'=2,'z'=8,'core'=2,'y'=4,'xh'=2] {'z','y'}, dimensions={0} | all-to-all | bytes 524288 | tf_op jit(solution)/shard_map/all_to_all | solution.py:511
  81.4 0.6 shard_map.83.share_ref
  82.0 3.6 %collective-permute-start.13 = (f32[7,16,128]{2,1,0:T(8,128)S(1)}, f32[7,16,128]{2,1,0:T(8,128)S(1)}, u32[]{:S(2)}, u32[]{:S(2)}) collective-permute-start(f32[7,16,128]{2,1,0:T(8,128)S(1)} %shard_map.83.share_ref), channel_id=1, source_target_pairs={{0,8},{8,0},{1,9},{9,1},{2,10},{10,2},{3,11},{11,3},{4,12},{12,4},... | collective-permute-start | bytes 172040 | tf_op jit(solution)/shard_map/ppermute | solution.py:490
  85.6 0.9 collective-permute-done.13.other_ref
  86.5 0.9 shard_map.84
  87.4 0.6 collective-permute-start.14
  88.0 1.3 %collective-permute-start.15 = (f32[16,128]{1,0:T(8,128)S(1)}, f32[16,128]{1,0:T(8,128)S(1)}, u32[]{:S(2)}, u32[]{:S(2)}) collective-permute-start(f32[16,128]{1,0:T(8,128)S(1)} %get-tuple-element.65), channel_id=1, source_target_pairs={{0,129},{1,128},{128,1},{129,0},{2,131},{3,130},{130,3},{131,2},{4... | collective-permute-start | bytes 24584 | tf_op jit(solution)/shard_map/ppermute | solution.py:490
  89.3 1.2 %shard_map.85 = (f32[14,24,640]{2,1,0:T(8,128)S(1)}, f32[14,24,640]{2,1,0:T(8,128)S(1)}) custom-call(f32[32,128]{1,0:T(8,128)S(1)} %get-tuple-element.53.metric_ref, f32[14,32,640]{2,1,0:T(8,128)S(1)} %get-tuple-element.56.refs_0_.full_ref, f32[14,32,640]{2,1,0:T(8,128)S(1)} %get-tuple-element.58.refs_1_.second_ref, ...), custom_call_target="tpu_custom_call" | custom-call | flops 2000000000 | bytes 2000000 | tf_op jit(solution)/shard_map/pallas_call | solution.py:464
  90.5 0.0 collective-permute-done.14
  90.5 1.2 %collective-permute-done.15 = f32[16,128]{1,0:T(8,128)S(1)} collective-permute-done((f32[16,128]{1,0:T(8,128)S(1)}, f32[16,128]{1,0:T(8,128)S(1)}, u32[]{:S(2)}, u32[]{:S(2)}) %collective-permute-start.15) | collective-permute-done | bytes 8224 | tf_op jit(solution)/shard_map/ppermute | solution.py:490
  91.7 13.6 %all_to_all.22.donor_ref = f32[32,16,128]{2,1,0:T(8,128)S(1)} all-to-all(f32[32,16,128]{2,1,0:T(8,128)S(1)} %broadcast_in_dim.14), channel_id=1, replica_groups=mesh['panel'=2,'z'=8,'core'=2,'y'=4,'xh'=2] {'z','y'}, dimensions={0} | all-to-all | bytes 524288 | tf_op jit(solution)/shard_map/all_to_all | solution.py:511
  105.3 0.6 shard_map.86.share_ref
  105.8 3.6 %collective-permute-start.16 = (f32[7,16,128]{2,1,0:T(8,128)S(1)}, f32[7,16,128]{2,1,0:T(8,128)S(1)}, u32[]{:S(2)}, u32[]{:S(2)}) collective-permute-start(f32[7,16,128]{2,1,0:T(8,128)S(1)} %shard_map.86.share_ref), channel_id=1, source_target_pairs={{0,8},{8,0},{1,9},{9,1},{2,10},{10,2},{3,11},{11,3},{4,12},{12,4},... | collective-permute-start | bytes 172040 | tf_op jit(solution)/shard_map/ppermute | solution.py:490
  109.4 0.9 collective-permute-done.16.other_ref
  110.3 1.4 %shard_map.87 = f32[14,24,576]{2,1,0:T(8,128)} custom-call(f32[8,640]{1,0:T(8,128)S(1)} %get-tuple-element.38.aux_ref, f32[7,16,128]{2,1,0:T(8,128)S(1)} %shard_map.86.share_ref, f32[7,16,128]{2,1,0:T(8,128)S(1)} %collective-permute-done.16.other_ref, f32[6,8,128]{2,1,0:T(8,128)S(1)} %get-tuple-element.51.cos_ref, ...), custom_call_target="tpu_custom_call" | custom-call | tf_op jit(solution)/shard_map/pallas_call | solution.py:464
  (8 shorter events, 0.1 us)
Async XLA Ops:
  2.0 6.7 %collective-permute-start = (f32[16,128]{1,0:T(8,128)S(1)}, f32[16,128]{1,0:T(8,128)S(1)}, u32[]{:S(2)}, u32[]{:S(2)}) collective-permute-start(f32[16,128]{1,0:T(8,128)S(1)} %get-tuple-element.39), channel_id=1, source_target_pairs={{0,128},{1,129},{128,0},{129,1},{2,130},{3,131},{130,2},{131,3},{4... | collective-permute-start | bytes 24584 | tf_op jit(solution)/shard_map/ppermute | solution.py:490
  4.1 4.6 %collective-permute-start.1 = (f32[16,128]{1,0:T(8,128)S(1)}, f32[16,128]{1,0:T(8,128)S(1)}, u32[]{:S(2)}, u32[]{:S(2)}) collective-permute-start(f32[16,128]{1,0:T(8,128)S(1)} %get-tuple-element.39), channel_id=1, source_target_pairs={{0,129},{1,128},{128,1},{129,0},{2,131},{3,130},{130,3},{131,2},{4... | collective-permute-start | bytes 24584 | tf_op jit(solution)/shard_map/ppermute | solution.py:490
  5.9 13.8 %collective-permute-start.2 = (f32[8,8,640]{2,1,0:T(8,128)S(1)}, f32[8,8,640]{2,1,0:T(8,128)S(1)}, u32[]{:S(2)}, u32[]{:S(2)}) collective-permute-start(f32[8,8,640]{2,1,0:T(8,128)S(1)} %get-tuple-element.41), channel_id=1, source_target_pairs={{0,8},{8,0},{16,24},{24,16},{32,40},{40,32},{48,56},{56,48},{64,72... | collective-permute-start | bytes 491528 | tf_op jit(solution)/shard_map/ppermute | solution.py:490
  7.1 12.6 %collective-permute-start.3 = (f32[8,8,640]{2,1,0:T(8,128)S(1)}, f32[8,8,640]{2,1,0:T(8,128)S(1)}, u32[]{:S(2)}, u32[]{:S(2)}) collective-permute-start(f32[8,8,640]{2,1,0:T(8,128)S(1)} %get-tuple-element.42), channel_id=1, source_target_pairs={{0,120},{8,16},{16,8},{24,32},{32,24},{40,48},{48,40},{56,64},{64,... | collective-permute-start | bytes 491528 | tf_op jit(solution)/shard_map/ppermute | solution.py:490
  9.4 20.7 %all-to-all-start = ((f32[32,16,128]{2,1,0:T(8,128)}), f32[32,16,128]{2,1,0:T(8,128)S(1)}, u32[]{:S(2)}, u32[]{:S(2)}) async-start(f32[32,16,128]{2,1,0:T(8,128)} %broadcast_in_dim.11), calls=%async_computation | async-start | bytes 524288 | tf_op jit(solution)/shard_map/all_to_all | solution.py:511
  20.0 8.4 %collective-permute-start.4 = (f32[32,128]{1,0:T(8,128)S(1)}, f32[32,128]{1,0:T(8,128)S(1)}, u32[]{:S(2)}, u32[]{:S(2)}) collective-permute-start(f32[32,128]{1,0:T(8,128)S(1)} %get-tuple-element.43), channel_id=1, source_target_pairs={{0,1},{1,0},{2,3},{3,2},{4,5},{5,4},{6,7},{7,6},{8,9},{9,8},{10,11... | collective-permute-start | bytes 49160 | tf_op jit(solution)/shard_map/ppermute | solution.py:490
  21.3 7.1 %collective-permute-start.5 = (f32[32,128]{1,0:T(8,128)S(1)}, f32[32,128]{1,0:T(8,128)S(1)}, u32[]{:S(2)}, u32[]{:S(2)}) collective-permute-start(f32[32,128]{1,0:T(8,128)S(1)} %get-tuple-element.44), channel_id=1, source_target_pairs={{0,7},{1,2},{2,1},{3,4},{4,3},{5,6},{6,5},{7,0},{8,15},{9,10},{10,... | collective-permute-start | bytes 49160 | tf_op jit(solution)/shard_map/ppermute | solution.py:490
  25.2 5.3 %collective-permute-start.6 = (s32[16,128]{1,0:T(8,128)S(1)}, s32[16,128]{1,0:T(8,128)S(1)}, u32[]{:S(2)}, u32[]{:S(2)}) collective-permute-start(s32[16,128]{1,0:T(8,128)S(1)} %get-tuple-element.50), channel_id=1, source_target_pairs={{0,8},{8,0},{1,9},{9,1},{2,10},{10,2},{3,11},{11,3},{4,12},{12,4},... | collective-permute-start | bytes 24584 | tf_op jit(solution)/shard_map/ppermute | solution.py:490
  31.0 5.2 %collective-permute-start.7 = (f32[7,16,128]{2,1,0:T(8,128)S(1)}, f32[7,16,128]{2,1,0:T(8,128)S(1)}, u32[]{:S(2)}, u32[]{:S(2)}) collective-permute-start(f32[7,16,128]{2,1,0:T(8,128)S(1)} %shard_map.76.share_ref), channel_id=1, source_target_pairs={{0,8},{8,0},{1,9},{9,1},{2,10},{10,2},{3,11},{11,3},{4,12},{12,4},... | collective-permute-start | bytes 172040 | tf_op jit(solution)/shard_map/ppermute | solution.py:490
  37.1 2.9 %collective-permute-start.8 = (f32[16,128]{1,0:T(8,128)S(1)}, f32[16,128]{1,0:T(8,128)S(1)}, u32[]{:S(2)}, u32[]{:S(2)}) collective-permute-start(f32[16,128]{1,0:T(8,128)S(1)} %get-tuple-element.57), channel_id=1, source_target_pairs={{0,128},{1,129},{128,0},{129,1},{2,130},{3,131},{130,2},{131,3},{4... | collective-permute-start | bytes 24584 | tf_op jit(solution)/shard_map/ppermute | solution.py:490
  37.2 3.8 %collective-permute-start.9 = (f32[16,128]{1,0:T(8,128)S(1)}, f32[16,128]{1,0:T(8,128)S(1)}, u32[]{:S(2)}, u32[]{:S(2)}) collective-permute-start(f32[16,128]{1,0:T(8,128)S(1)} %get-tuple-element.57), channel_id=1, source_target_pairs={{0,129},{1,128},{128,1},{129,0},{2,131},{3,130},{130,3},{131,2},{4... | collective-permute-start | bytes 24584 | tf_op jit(solution)/shard_map/ppermute | solution.py:490
  58.4 4.7 %collective-permute-start.10 = (f32[7,16,128]{2,1,0:T(8,128)S(1)}, f32[7,16,128]{2,1,0:T(8,128)S(1)}, u32[]{:S(2)}, u32[]{:S(2)}) collective-permute-start(f32[7,16,128]{2,1,0:T(8,128)S(1)} %shard_map.80.share_ref), channel_id=1, source_target_pairs={{0,8},{8,0},{1,9},{9,1},{2,10},{10,2},{3,11},{11,3},{4,12},{12,4},... | collective-permute-start | bytes 172040 | tf_op jit(solution)/shard_map/ppermute | solution.py:490
  64.0 3.4 %collective-permute-start.11 = (f32[16,128]{1,0:T(8,128)S(1)}, f32[16,128]{1,0:T(8,128)S(1)}, u32[]{:S(2)}, u32[]{:S(2)}) collective-permute-start(f32[16,128]{1,0:T(8,128)S(1)} %get-tuple-element.61), channel_id=1, source_target_pairs={{0,128},{1,129},{128,0},{129,1},{2,130},{3,131},{130,2},{131,3},{4... | collective-permute-start | bytes 24584 | tf_op jit(solution)/shard_map/ppermute | solution.py:490
  64.0 3.8 %collective-permute-start.12 = (f32[16,128]{1,0:T(8,128)S(1)}, f32[16,128]{1,0:T(8,128)S(1)}, u32[]{:S(2)}, u32[]{:S(2)}) collective-permute-start(f32[16,128]{1,0:T(8,128)S(1)} %get-tuple-element.61), channel_id=1, source_target_pairs={{0,129},{1,128},{128,1},{129,0},{2,131},{3,130},{130,3},{131,2},{4... | collective-permute-start | bytes 24584 | tf_op jit(solution)/shard_map/ppermute | solution.py:490
  82.0 4.5 %collective-permute-start.13 = (f32[7,16,128]{2,1,0:T(8,128)S(1)}, f32[7,16,128]{2,1,0:T(8,128)S(1)}, u32[]{:S(2)}, u32[]{:S(2)}) collective-permute-start(f32[7,16,128]{2,1,0:T(8,128)S(1)} %shard_map.83.share_ref), channel_id=1, source_target_pairs={{0,8},{8,0},{1,9},{9,1},{2,10},{10,2},{3,11},{11,3},{4,12},{12,4},... | collective-permute-start | bytes 172040 | tf_op jit(solution)/shard_map/ppermute | solution.py:490
  87.4 3.1 %collective-permute-start.14 = (f32[16,128]{1,0:T(8,128)S(1)}, f32[16,128]{1,0:T(8,128)S(1)}, u32[]{:S(2)}, u32[]{:S(2)}) collective-permute-start(f32[16,128]{1,0:T(8,128)S(1)} %get-tuple-element.65), channel_id=1, source_target_pairs={{0,128},{1,129},{128,0},{129,1},{2,130},{3,131},{130,2},{131,3},{4... | collective-permute-start | bytes 24584 | tf_op jit(solution)/shard_map/ppermute | solution.py:490
  88.0 3.7 %collective-permute-start.15 = (f32[16,128]{1,0:T(8,128)S(1)}, f32[16,128]{1,0:T(8,128)S(1)}, u32[]{:S(2)}, u32[]{:S(2)}) collective-permute-start(f32[16,128]{1,0:T(8,128)S(1)} %get-tuple-element.65), channel_id=1, source_target_pairs={{0,129},{1,128},{128,1},{129,0},{2,131},{3,130},{130,3},{131,2},{4... | collective-permute-start | bytes 24584 | tf_op jit(solution)/shard_map/ppermute | solution.py:490
  105.8 4.5 %collective-permute-start.16 = (f32[7,16,128]{2,1,0:T(8,128)S(1)}, f32[7,16,128]{2,1,0:T(8,128)S(1)}, u32[]{:S(2)}, u32[]{:S(2)}) collective-permute-start(f32[7,16,128]{2,1,0:T(8,128)S(1)} %shard_map.86.share_ref), channel_id=1, source_target_pairs={{0,8},{8,0},{1,9},{9,1},{2,10},{10,2},{3,11},{11,3},{4,12},{12,4},... | collective-permute-start | bytes 172040 | tf_op jit(solution)/shard_map/ppermute | solution.py:490

commit v4 on v3

--- a/solution.py
+++ b/solution.py
@@ -47,19 +47,25 @@
     return jnp.take_along_axis(block, index, axis=1, mode="promise_in_bounds")
 
 
-def build_packet(block_of, index_ref, weight_ref):
-    totals = [None] * FIELDS
-    for t in range(LANE_TILES):
-        index = index_ref[t]
-        for rb in range(CT // 8):
-            weight = weight_ref[rb * LANE_TILES + t]
-            for f in range(FIELDS):
-                term = weight * lane_gather(block_of(f, rb, t), index)
-                totals[f] = term if totals[f] is None else totals[f] + term
+def add_donors(totals, block_of, index, weight, rb, t):
+    for f in range(FIELDS):
+        term = weight * lane_gather(block_of(f, rb, t), index)
+        totals[f] = term if totals[f] is None else totals[f] + term
+
+
+def packed_rows(totals):
     rows = [jnp.sum(total, axis=0, keepdims=True) for total in totals]
     rows += [jnp.zeros((1, LANES), jnp.float32)] * (16 - FIELDS)
     packet = jnp.concatenate(rows, axis=0)
     return packet + pltpu.roll(packet, 64, 1)
+
+
+def build_packet(block_of, index_ref, weight_ref):
+    totals = [None] * FIELDS
+    for t in range(LANE_TILES):
+        for rb in range(CT // 8):
+            add_donors(totals, block_of, index_ref[t], weight_ref[rb * LANE_TILES + t], rb, t)
+    return packed_rows(totals)
 
 
 def state_block(state_ref, f, rb, t):
@@ -252,13 +258,14 @@
     tables = [(slot_ref[t], tile_ref[t]) for t in range(count)] + [(other_ref[0:8, :], other_ref[8:16, :])]
     for t, (slots, pairs) in enumerate(tables):
         pairs = pairs - mine
-        for half in range(2):
-            rows = slice(half * 8, half * 8 + 8)
-            total = jnp.zeros((8, LANES), jnp.float32)
-            for v in range(TILES // 4):
-                block = donor_ref[v, rows, :]
-                total = jnp.where(pairs == v // 4 * 8 + v % 4, lane_gather(block, slots), total)
-            out_ref[t, rows, :] = total
+        low = jnp.zeros((8, LANES), jnp.float32)
+        high = jnp.zeros((8, LANES), jnp.float32)
+        for v in range(TILES // 4):
+            here = pairs == v % 8 * 8 + v // 8
+            low = jnp.where(here, lane_gather(donor_ref[v, 0:8, :], slots), low)
+            high = jnp.where(here, lane_gather(donor_ref[v, 8:16, :], slots), high)
+        out_ref[t, 0:8, :] = low
+        out_ref[t, 8:16, :] = high
 
 
 def turned_ghosts(share_ref, other_ref, cos_ref, sin_ref):
@@ -374,8 +381,7 @@
     emit(6, conduction * p[3] - along(flow_by, p) + gradient * value(0))
 
 
-def inner_kernel(factor, metric_ref, *refs):
-    full_ref, now_ref, next_ref = refs if len(refs) == 3 else (refs[0], refs[0], refs[1])
+def inner_kernel(factor, metric_ref, full_ref, now_ref, next_ref):
     for rb in range(ROWS // 8):
         rows = slice(rb * 8, rb * 8 + 8)
         for k in range(2):
@@ -384,6 +390,56 @@
                 next_ref[2 * c + k, rows, :] = full_ref[2 * c + k, rows, :] + factor * value
 
             tendency(now_ref, metric_ref, rb, k, emit)
+
+
+def first_inner_kernel(metric_ref, full_ref, next_ref):
+    inner_kernel(time_step / 2, metric_ref, full_ref, full_ref, next_ref)
+
+
+def put_rim(place, inner_ref, row_ref, column_ref, now_ref):
+    lat, lon = place
+    now_ref[...] = inner_ref[...]
+
+    def put_row(rb):
+        now_ref[:, rb * 8 : rb * 8 + 8, :] = row_ref[...]
+
+    def put_column(tile):
+        now_ref[:, :, tile * LANES : (tile + 1) * LANES] = column_ref[...]
+
+    pl.when(lat == 0)(lambda: put_row(0))
+    pl.when(lat == NT // CT - 1)(lambda: put_row(CT // 8 - 1))
+    pl.when(lon == 0)(lambda: put_column(0))
+    pl.when(lon == 7)(lambda: put_column(LANE_TILES - 1))
+
+
+def next_inner_kernel(factor, aux_ref, metric_ref, full_ref, inner_ref, row_ref, column_ref, now_ref, next_ref):
+    put_rim(place_of(aux_ref), inner_ref, row_ref, column_ref, now_ref)
+    inner_kernel(factor, metric_ref, full_ref, now_ref, next_ref)
+
+
+def on_rim(place, rb, t):
+    lat, lon = place
+    in_row = {0: lat == 0, CT // 8 - 1: lat == NT // CT - 1}.get(rb, False)
+    in_column = {0: lon == 0, LANE_TILES - 1: lon == 7}.get(t, False)
+    return in_row, in_column
+
+
+def donor_kernel(aux_ref, inner_ref, index_ref, weight_ref, total_ref):
+    place = place_of(aux_ref)
+    totals = [None] * FIELDS
+
+    def block_of(f, rb, t):
+        return inner_ref[f, rb * 8 : rb * 8 + 8, t * LANES : (t + 1) * LANES]
+
+    for t in range(LANE_TILES):
+        for rb in range(CT // 8):
+            weight = weight_ref[rb * LANE_TILES + t]
+            for here in on_rim(place, rb, t):
+                if here is not False:
+                    weight = jnp.where(here, 0.0, weight)
+            add_donors(totals, block_of, index_ref[t], weight, rb, t)
+    for f in range(FIELDS):
+        total_ref[f] = totals[f]
 
 
 def redo_rim(place, now_ref, metric_ref, line_ref, column_ref, blocks, store):
@@ -406,25 +462,52 @@
 
 
 def rim_kernel(
-    factor, aux_ref, share_ref, other_ref, cos_ref, sin_ref, metric_ref, index_ref, weight_ref, *refs
+    factor, aux_ref, share_ref, other_ref, cos_ref, sin_ref, metric_ref, index_ref, weight_ref, total_ref, full_ref, now_ref,
+    row_ref, side_ref, packet_ref, line_ref, column_ref, sum_ref,
 ):
-    full_ref, now_ref, inner_ref, next_ref, packet_ref, line_ref, column_ref = refs if len(refs) == 7 else refs[:1] + refs
     place = place_of(aux_ref)
-    keep_ghosts(place[1], turned_ghosts(share_ref, other_ref, cos_ref, sin_ref), line_ref, column_ref)
-    next_ref[...] = inner_ref[...]
+    lat, lon = place
+    keep_ghosts(lon, turned_ghosts(share_ref, other_ref, cos_ref, sin_ref), line_ref, column_ref)
+    sum_ref[...] = total_ref[...]
 
     def store(f, rows, cols, value):
-        next_ref[f, rows, cols] = full_ref[f, rows, cols] + factor * value
+        value = full_ref[f, rows, cols] + factor * value
+        if cols.stop - cols.start == COLS:
+            row_ref[f] = value
+        else:
+            side_ref[f, rows, :] = value
 
     redo_rim(place, now_ref, metric_ref, line_ref, column_ref, ROWS // 8, store)
 
-    def block_of(f, rb, t):
-        return next_ref[f, rb * 8 : rb * 8 + 8, t * LANES : (t + 1) * LANES]
-
-    packet_ref[...] = build_packet(block_of, index_ref, weight_ref)
-
-
-def last_inner_kernel(metric_ref, full_ref, second_ref, third_ref, fourth_ref, base_ref, out_ref):
+    def add(blocks, block_of, skip):
+        totals = [sum_ref[f] for f in range(FIELDS)]
+        for rb, t in blocks:
+            weight = weight_ref[rb * LANE_TILES + t]
+            if skip and on_rim(place, rb, t)[1] is not False:
+                weight = jnp.where(on_rim(place, rb, t)[1], 0.0, weight)
+            add_donors(totals, block_of, index_ref[t], weight, rb, t)
+        for f in range(FIELDS):
+            sum_ref[f] = totals[f]
+
+    def add_row(rb):
+        blocks = [(rb, t) for t in range(LANE_TILES)]
+        add(blocks, lambda f, rb, t: row_ref[f, :, t * LANES : (t + 1) * LANES], True)
+
+    def add_side(t):
+        blocks = [(rb, t) for rb in range(CT // 8)]
+        add(blocks, lambda f, rb, t: side_ref[f, rb * 8 : rb * 8 + 8, :], False)
+
+    pl.when(lat == 0)(lambda: add_row(0))
+    pl.when(lat == NT // CT - 1)(lambda: add_row(CT // 8 - 1))
+    pl.when(lon == 0)(lambda: add_side(0))
+    pl.when(lon == 7)(lambda: add_side(LANE_TILES - 1))
+    packet_ref[...] = packed_rows([sum_ref[f] for f in range(FIELDS)])
+
+
+def last_inner_kernel(
+    aux_ref, metric_ref, full_ref, second_ref, third_ref, inner_ref, row_ref, column_ref, fourth_ref, base_ref, out_ref
+):
+    put_rim(place_of(aux_ref), inner_ref, row_ref, column_ref, fourth_ref)
     for rb in range(CT // 8):
         rows = slice(rb * 8, rb * 8 + 8)
         for k in range(2):
@@ -508,7 +591,7 @@
 
 def spread_packets(pair):
     count = SIZES["z"] * SIZES["y"]
-    return lax.all_to_all(jnp.broadcast_to(pair[None], (count,) + pair.shape), ("z", "y"), 0, 0)
+    return lax.all_to_all(jnp.broadcast_to(pair[None], (count,) + pair.shape), ("y", "z"), 0, 0)
 
 
 def other_core(value):
@@ -567,25 +650,34 @@
         (share,) = call(pick_kernel, [aux, donors] + lists, [((LANE_TILES + 2, 16, LANES), f32)])
         return [aux, share, other_core(share), cosine, sine, metric]
 
+    row, side = ((FIELDS, 8, COLS), f32), ((FIELDS, ROWS, LANES), f32)
+    totals = ((FIELDS,) + vreg, f32)
     states = [full]
     for factor in (time_step / 2, time_step / 2, time_step):
-        now = [states[-1]] if len(states) > 1 else []
-        if now:
+        if len(states) == 1:
+            (inner,) = call(first_inner_kernel, [metric, full], [whole], cost=2_000_000)
+        else:
             pair = swap_packets(packet)
-        (inner,) = call(functools.partial(inner_kernel, factor), [metric, full] + now, [whole], cost=2_000_000)
-        if now:
+            now, inner = call(
+                functools.partial(next_inner_kernel, factor), [aux, metric, full, inner] + rim, [whole, whole], cost=2_000_000
+            )
+            states[-1] = now
             pair, inner = lax.optimization_barrier((pair, inner))
             donors = spread_packets(pair)
-        after, packet = call(
+        tables = ghost_tables(donors)
+        (sums,) = call(donor_kernel, [aux, inner, index, weight], [totals], cost=500_000)
+        *rim, packet = call(
             functools.partial(rim_kernel, factor),
-            ghost_tables(donors) + [index, weight, full] + now + [inner],
-            [whole, packed],
-            scratch=kept,
+            tables + [index, weight, sums, full, states[-1]],
+            [row, side, packed],
+            scratch=kept + [pltpu.VMEM(*totals)],
         )
-        states.append(after)
+        states.append(None)
     pair = swap_packets(packet)
     inner_shape = ((FIELDS, CT, COLS), f32)
-    base, inner = call(last_inner_kernel, [metric] + states, [inner_shape, inner_shape], cost=2_000_000)
+    states[-1], base, inner = call(
+        last_inner_kernel, [aux, metric] + states[:-1] + [inner] + rim, [whole, inner_shape, inner_shape], cost=2_000_000
+    )
     pair, inner = lax.optimization_barrier((pair, inner))
     (result,) = call(
         last_rim_kernel,

time: 112 us -> 111 us (level)
  waiting for transfers between devices: 6.96 us -> 5.43 us
  Pallas kernels: 14 us -> 15.2 us
    pallas_call x15 -> x18, Pallas kernels: 14 us -> 15.2 us  [call(): pl.pallas_call(kernel, out_shape=shapes, in_specs=[hbm if i in left else...]
  transfers between devices with their start and end apart: 18 -> 18, of which waited for: 7 -> 7; matrix products, arithmetic and copies ran while one was open for 1% -> 1% of each run, Pallas kernels for 5% -> 7%
where the time goes in v4:
time: 111 us
  starting transfers between devices  45.7 us (41%)
  blocking collectives  43.2 us (39%)
  Pallas kernels  15.2 us (14%)
  waiting for transfers between devices  5.43 us (5%)
    all_to_all x3, blocking collectives, spread_packets(): lax.all_to_all(jnp.broadcast_to(pair[None], (count,) + pair.shape), ('y',...  43.2 us
    ppermute x17, starting transfers between devices, permute(): return lax.ppermute(value, axes if len(axes) > 1 else axes[0], pairs)  35.4 us
    pallas_call x18, Pallas kernels, call(): pl.pallas_call(kernel, out_shape=shapes, in_specs=[hbm if i in left else...  15.2 us
    all_to_all x1, starting transfers between devices, spread_packets(): lax.all_to_all(jnp.broadcast_to(pair[None], (count,) + pair.shape), ('y',...  10.3 us
    ppermute x17, waiting for transfers between devices, permute(): return lax.ppermute(value, axes if len(axes) > 1 else axes[0], pairs)  4.48 us
  transfers between devices with their start and end apart: 18, of which 7 were waited for; matrix products, arithmetic and copies ran while one was open for 1% of the time, Pallas kernels for 7%

profile of v4, /device:TPU:1, one launch (start us, length us, event | category | flops | bytes accessed | tf_op | source)
XLA Modules:
  0.0 110.7 jit_solution(7646817369594765931)
XLA Ops:
  0.0 0.1 stack.20
  0.1 0.1 broadcast_in_dim.10.flags_ref
  0.2 1.8 %shard_map.73 = (f32[14,24,576]{2,1,0:T(8,128)S(1)}, f32[8,640]{1,0:T(8,128)S(1)}, f32[16,128]{1,0:T(8,128)S(1)}, f32[8,8,640]{2,1,0:T(8,128)S(1)}, f32[8,8,640]...) custom-call(s32[8,128]{1,0:T(8,128)S(1)} %broadcast_in_dim.10.flags_ref, ...), custom_call_target="tpu_custom_call" | custom-call | tf_op jit(solution)/shard_map/pallas_call | solution.py:547
  2.0 2.1 %collective-permute-start = (f32[16,128]{1,0:T(8,128)S(1)}, f32[16,128]{1,0:T(8,128)S(1)}, u32[]{:S(2)}, u32[]{:S(2)}) collective-permute-start(f32[16,128]{1,0:T(8,128)S(1)} %get-tuple-element.47), channel_id=1, source_target_pairs={{0,128},{1,129},{128,0},{129,1},{2,130},{3,131},{130,2},{131,3},{4... | collective-permute-start | bytes 24584 | tf_op jit(solution)/shard_map/ppermute | solution.py:573
  4.1 1.8 %collective-permute-start.1 = (f32[16,128]{1,0:T(8,128)S(1)}, f32[16,128]{1,0:T(8,128)S(1)}, u32[]{:S(2)}, u32[]{:S(2)}) collective-permute-start(f32[16,128]{1,0:T(8,128)S(1)} %get-tuple-element.47), channel_id=1, source_target_pairs={{0,129},{1,128},{128,1},{129,0},{2,131},{3,130},{130,3},{131,2},{4... | collective-permute-start | bytes 24584 | tf_op jit(solution)/shard_map/ppermute | solution.py:573
  5.9 1.2 %collective-permute-start.2 = (f32[8,8,640]{2,1,0:T(8,128)S(1)}, f32[8,8,640]{2,1,0:T(8,128)S(1)}, u32[]{:S(2)}, u32[]{:S(2)}) collective-permute-start(f32[8,8,640]{2,1,0:T(8,128)S(1)} %get-tuple-element.49), channel_id=1, source_target_pairs={{0,8},{8,0},{16,24},{24,16},{32,40},{40,32},{48,56},{56,48},{64,72... | collective-permute-start | bytes 491528 | tf_op jit(solution)/shard_map/ppermute | solution.py:573
  7.1 1.5 %collective-permute-start.3 = (f32[8,8,640]{2,1,0:T(8,128)S(1)}, f32[8,8,640]{2,1,0:T(8,128)S(1)}, u32[]{:S(2)}, u32[]{:S(2)}) collective-permute-start(f32[8,8,640]{2,1,0:T(8,128)S(1)} %get-tuple-element.50), channel_id=1, source_target_pairs={{0,120},{8,16},{16,8},{24,32},{32,24},{40,48},{48,40},{56,64},{64,... | collective-permute-start | bytes 491528 | tf_op jit(solution)/shard_map/ppermute | solution.py:573
  8.7 0.0 collective-permute-done
  8.7 0.0 collective-permute-done.1
  8.7 0.7 broadcast_in_dim.11
  9.4 10.3 %all-to-all-start = ((f32[32,16,128]{2,1,0:T(8,128)}), f32[32,16,128]{2,1,0:T(8,128)S(1)}, u32[]{:S(2)}, u32[]{:S(2)}) async-start(f32[32,16,128]{2,1,0:T(8,128)} %broadcast_in_dim.11), calls=%async_computation | async-start | bytes 524288 | tf_op jit(solution)/shard_map/all_to_all | solution.py:594
  19.7 0.0 collective-permute-done.2.lat_inner_ref
  19.8 0.0 collective-permute-done.3.lat_cross_ref
  19.8 0.2 shard_map.74
  20.0 1.3 %collective-permute-start.4 = (f32[32,128]{1,0:T(8,128)S(1)}, f32[32,128]{1,0:T(8,128)S(1)}, u32[]{:S(2)}, u32[]{:S(2)}) collective-permute-start(f32[32,128]{1,0:T(8,128)S(1)} %get-tuple-element.51), channel_id=1, source_target_pairs={{0,1},{1,0},{2,3},{3,2},{4,5},{5,4},{6,7},{7,6},{8,9},{9,8},{10,11... | collective-permute-start | bytes 49160 | tf_op jit(solution)/shard_map/ppermute | solution.py:573
  21.3 3.9 %collective-permute-start.5 = (f32[32,128]{1,0:T(8,128)S(1)}, f32[32,128]{1,0:T(8,128)S(1)}, u32[]{:S(2)}, u32[]{:S(2)}) collective-permute-start(f32[32,128]{1,0:T(8,128)S(1)} %get-tuple-element.52), channel_id=1, source_target_pairs={{0,7},{1,2},{2,1},{3,4},{4,3},{5,6},{6,5},{7,0},{8,15},{9,10},{10,... | collective-permute-start | bytes 49160 | tf_op jit(solution)/shard_map/ppermute | solution.py:573
  25.2 3.2 %collective-permute-start.6 = (s32[16,128]{1,0:T(8,128)S(1)}, s32[16,128]{1,0:T(8,128)S(1)}, u32[]{:S(2)}, u32[]{:S(2)}) collective-permute-start(s32[16,128]{1,0:T(8,128)S(1)} %get-tuple-element.58), channel_id=1, source_target_pairs={{0,8},{8,0},{1,9},{9,1},{2,10},{10,2},{3,11},{11,3},{4,12},{12,4},... | collective-permute-start | bytes 24584 | tf_op jit(solution)/shard_map/ppermute | solution.py:573
  28.5 0.0 collective-permute-done.4.lon_inner_ref
  28.5 0.0 collective-permute-done.5.lon_cross_ref
  28.5 0.9 all-to-all-done.donor_ref
  29.4 0.3 shard_map.75
  29.7 0.0 collective-permute-done.6.other_ref
  29.7 0.6 shard_map.76.share_ref
  30.3 4.2 %collective-permute-start.7 = (f32[7,16,128]{2,1,0:T(8,128)S(1)}, f32[7,16,128]{2,1,0:T(8,128)S(1)}, u32[]{:S(2)}, u32[]{:S(2)}) collective-permute-start(f32[7,16,128]{2,1,0:T(8,128)S(1)} %shard_map.76.share_ref), channel_id=1, source_target_pairs={{0,8},{8,0},{1,9},{9,1},{2,10},{10,2},{3,11},{11,3},{4,12},{12,4},... | collective-permute-start | bytes 172040 | tf_op jit(solution)/shard_map/ppermute | solution.py:573
  34.4 1.5 %shard_map.77.inner_ref = f32[14,32,640]{2,1,0:T(8,128)S(1)} custom-call(f32[32,128]{1,0:T(8,128)S(1)} %get-tuple-element.61.metric_ref, f32[14,32,640]{2,1,0:T(8,128)S(1)} %get-tuple-element.64.full_ref.now_ref), custom_call_target="tpu_custom_call" | custom-call | flops 2000000000 | bytes 2000000 | tf_op jit(solution)/shard_map/pallas_call | solution.py:547
  35.9 0.3 shard_map.78.total_ref
  36.2 0.0 collective-permute-done.7.other_ref
  36.2 0.7 shard_map.79
  36.9 0.0 collective-permute-start.8
  36.9 1.4 %collective-permute-start.9 = (f32[16,128]{1,0:T(8,128)S(1)}, f32[16,128]{1,0:T(8,128)S(1)}, u32[]{:S(2)}, u32[]{:S(2)}) collective-permute-start(f32[16,128]{1,0:T(8,128)S(1)} %get-tuple-element.65), channel_id=1, source_target_pairs={{0,129},{1,128},{128,1},{129,0},{2,131},{3,130},{130,3},{131,2},{4... | collective-permute-start | bytes 24584 | tf_op jit(solution)/shard_map/ppermute | solution.py:573
  38.3 1.8 %shard_map.80 = (f32[14,32,640]{2,1,0:T(8,128)S(1)}, f32[14,32,640]{2,1,0:T(8,128)S(1)}) custom-call(f32[8,640]{1,0:T(8,128)S(1)} %get-tuple-element.46.aux_ref, f32[32,128]{1,0:T(8,128)S(1)} %get-tuple-element.61.metric_ref, f32[14,32,640]{2,1,0:T(8,128)S(1)} %get-tuple-element.64.full_ref.now_ref, f32[14,32,640]{2,1,0:T(8,128)S(1)} %shard_map.77.inner_ref, ...), custom_call_target="tpu_custom_call" | custom-call | flops 2000000000 | bytes 2000000 | tf_op jit(solution)/shard_map/pallas_call | solution.py:547
  40.1 0.0 collective-permute-done.8
  40.1 0.6 collective-permute-done.9
  40.8 16.6 %all_to_all.20.donor_ref = f32[32,16,128]{2,1,0:T(8,128)S(1)} all-to-all(f32[32,16,128]{2,1,0:T(8,128)S(1)} %broadcast_in_dim.12), channel_id=1, replica_groups=mesh['panel'=2,'z'=8,'core'=2,'y'=4,'xh'=2] {'y','z'}, dimensions={0} | all-to-all | bytes 524288 | tf_op jit(solution)/shard_map/all_to_all | solution.py:594
  57.4 0.6 shard_map.81.share_ref
  58.0 3.7 %collective-permute-start.10 = (f32[7,16,128]{2,1,0:T(8,128)S(1)}, f32[7,16,128]{2,1,0:T(8,128)S(1)}, u32[]{:S(2)}, u32[]{:S(2)}) collective-permute-start(f32[7,16,128]{2,1,0:T(8,128)S(1)} %shard_map.81.share_ref), channel_id=1, source_target_pairs={{0,8},{8,0},{1,9},{9,1},{2,10},{10,2},{3,11},{11,3},{4,12},{12,4},... | collective-permute-start | bytes 172040 | tf_op jit(solution)/shard_map/ppermute | solution.py:573
  61.7 0.3 shard_map.82.total_ref
  62.0 0.6 collective-permute-done.10.other_ref
  62.5 0.7 shard_map.83
  63.2 0.0 collective-permute-start.11
  63.3 1.5 %collective-permute-start.12 = (f32[16,128]{1,0:T(8,128)S(1)}, f32[16,128]{1,0:T(8,128)S(1)}, u32[]{:S(2)}, u32[]{:S(2)}) collective-permute-start(f32[16,128]{1,0:T(8,128)S(1)} %get-tuple-element.72), channel_id=1, source_target_pairs={{0,129},{1,128},{128,1},{129,0},{2,131},{3,130},{130,3},{131,2},{4... | collective-permute-start | bytes 24584 | tf_op jit(solution)/shard_map/ppermute | solution.py:573
  64.8 1.6 %shard_map.84 = (f32[14,32,640]{2,1,0:T(8,128)S(1)}, f32[14,32,640]{2,1,0:T(8,128)S(1)}) custom-call(f32[8,640]{1,0:T(8,128)S(1)} %get-tuple-element.46.aux_ref, f32[32,128]{1,0:T(8,128)S(1)} %get-tuple-element.61.metric_ref, f32[14,32,640]{2,1,0:T(8,128)S(1)} %get-tuple-element.64.full_ref.now_ref, f32[14,32,640]{2,1,0:T(8,128)S(1)} %get-tuple-element.70.inner_ref, ...), custom_call_target="tpu_custom_call" | custom-call | flops 2000000000 | bytes 2000000 | tf_op jit(solution)/shard_map/pallas_call | solution.py:547
  66.4 0.0 collective-permute-done.11
  66.4 0.6 collective-permute-done.12
  67.1 13.4 %all_to_all.21.donor_ref = f32[32,16,128]{2,1,0:T(8,128)S(1)} all-to-all(f32[32,16,128]{2,1,0:T(8,128)S(1)} %broadcast_in_dim.13), channel_id=1, replica_groups=mesh['panel'=2,'z'=8,'core'=2,'y'=4,'xh'=2] {'y','z'}, dimensions={0} | all-to-all | bytes 524288 | tf_op jit(solution)/shard_map/all_to_all | solution.py:594
  80.5 0.6 shard_map.85.share_ref
  81.1 3.8 %collective-permute-start.13 = (f32[7,16,128]{2,1,0:T(8,128)S(1)}, f32[7,16,128]{2,1,0:T(8,128)S(1)}, u32[]{:S(2)}, u32[]{:S(2)}) collective-permute-start(f32[7,16,128]{2,1,0:T(8,128)S(1)} %shard_map.85.share_ref), channel_id=1, source_target_pairs={{0,8},{8,0},{1,9},{9,1},{2,10},{10,2},{3,11},{11,3},{4,12},{12,4},... | collective-permute-start | bytes 172040 | tf_op jit(solution)/shard_map/ppermute | solution.py:573
  84.8 0.3 shard_map.86.total_ref
  85.2 0.6 collective-permute-done.13.other_ref
  85.7 0.7 shard_map.87
  86.4 0.7 collective-permute-start.14
  87.2 1.1 %collective-permute-start.15 = (f32[16,128]{1,0:T(8,128)S(1)}, f32[16,128]{1,0:T(8,128)S(1)}, u32[]{:S(2)}, u32[]{:S(2)}) collective-permute-start(f32[16,128]{1,0:T(8,128)S(1)} %get-tuple-element.79), channel_id=1, source_target_pairs={{0,129},{1,128},{128,1},{129,0},{2,131},{3,130},{130,3},{131,2},{4... | collective-permute-start | bytes 24584 | tf_op jit(solution)/shard_map/ppermute | solution.py:573
  88.3 1.4 %shard_map.88 = (f32[14,32,640]{2,1,0:T(8,128)S(1)}, f32[14,24,640]{2,1,0:T(8,128)S(1)}, f32[14,24,640]{2,1,0:T(8,128)S(1)}) custom-call(f32[8,640]{1,0:T(8,128)S(1)} %get-tuple-element.46.aux_ref, f32[32,128]{1,0:T(8,128)S(1)} %get-tuple-element.61.metric_ref, f32[14,32,640]{2,1,0:T(8,128)S(1)} %get-tuple-element.64.full_ref.now_ref, ...), custom_call_target="tpu_custom_call" | custom-call | flops 2000000000 | bytes 2000000 | tf_op jit(solution)/shard_map/pallas_call | solution.py:547
  89.7 0.0 collective-permute-done.14
  89.7 1.1 %collective-permute-done.15 = f32[16,128]{1,0:T(8,128)S(1)} collective-permute-done((f32[16,128]{1,0:T(8,128)S(1)}, f32[16,128]{1,0:T(8,128)S(1)}, u32[]{:S(2)}, u32[]{:S(2)}) %collective-permute-start.15) | collective-permute-done | bytes 8224 | tf_op jit(solution)/shard_map/ppermute | solution.py:573
  90.9 13.2 %all_to_all.22.donor_ref = f32[32,16,128]{2,1,0:T(8,128)S(1)} all-to-all(f32[32,16,128]{2,1,0:T(8,128)S(1)} %broadcast_in_dim.14), channel_id=1, replica_groups=mesh['panel'=2,'z'=8,'core'=2,'y'=4,'xh'=2] {'y','z'}, dimensions={0} | all-to-all | bytes 524288 | tf_op jit(solution)/shard_map/all_to_all | solution.py:594
  104.1 0.6 shard_map.89.share_ref
  104.7 3.8 %collective-permute-start.16 = (f32[7,16,128]{2,1,0:T(8,128)S(1)}, f32[7,16,128]{2,1,0:T(8,128)S(1)}, u32[]{:S(2)}, u32[]{:S(2)}) collective-permute-start(f32[7,16,128]{2,1,0:T(8,128)S(1)} %shard_map.89.share_ref), channel_id=1, source_target_pairs={{0,8},{8,0},{1,9},{9,1},{2,10},{10,2},{3,11},{11,3},{4,12},{12,4},... | collective-permute-start | bytes 172040 | tf_op jit(solution)/shard_map/ppermute | solution.py:573
  108.4 0.9 collective-permute-done.16.other_ref
  109.3 1.4 %shard_map.90 = f32[14,24,576]{2,1,0:T(8,128)} custom-call(f32[8,640]{1,0:T(8,128)S(1)} %get-tuple-element.46.aux_ref, f32[7,16,128]{2,1,0:T(8,128)S(1)} %shard_map.89.share_ref, f32[7,16,128]{2,1,0:T(8,128)S(1)} %collective-permute-done.16.other_ref, f32[6,8,128]{2,1,0:T(8,128)S(1)} %get-tuple-element.59.cos_ref, ...), custom_call_target="tpu_custom_call" | custom-call | tf_op jit(solution)/shard_map/pallas_call | solution.py:547
  (8 shorter events, 0.1 us)
Async XLA Ops:
  2.0 6.7 %collective-permute-start = (f32[16,128]{1,0:T(8,128)S(1)}, f32[16,128]{1,0:T(8,128)S(1)}, u32[]{:S(2)}, u32[]{:S(2)}) collective-permute-start(f32[16,128]{1,0:T(8,128)S(1)} %get-tuple-element.47), channel_id=1, source_target_pairs={{0,128},{1,129},{128,0},{129,1},{2,130},{3,131},{130,2},{131,3},{4... | collective-permute-start | bytes 24584 | tf_op jit(solution)/shard_map/ppermute | solution.py:573
  4.1 4.6 %collective-permute-start.1 = (f32[16,128]{1,0:T(8,128)S(1)}, f32[16,128]{1,0:T(8,128)S(1)}, u32[]{:S(2)}, u32[]{:S(2)}) collective-permute-start(f32[16,128]{1,0:T(8,128)S(1)} %get-tuple-element.47), channel_id=1, source_target_pairs={{0,129},{1,128},{128,1},{129,0},{2,131},{3,130},{130,3},{131,2},{4... | collective-permute-start | bytes 24584 | tf_op jit(solution)/shard_map/ppermute | solution.py:573
  5.9 13.8 %collective-permute-start.2 = (f32[8,8,640]{2,1,0:T(8,128)S(1)}, f32[8,8,640]{2,1,0:T(8,128)S(1)}, u32[]{:S(2)}, u32[]{:S(2)}) collective-permute-start(f32[8,8,640]{2,1,0:T(8,128)S(1)} %get-tuple-element.49), channel_id=1, source_target_pairs={{0,8},{8,0},{16,24},{24,16},{32,40},{40,32},{48,56},{56,48},{64,72... | collective-permute-start | bytes 491528 | tf_op jit(solution)/shard_map/ppermute | solution.py:573
  7.1 12.6 %collective-permute-start.3 = (f32[8,8,640]{2,1,0:T(8,128)S(1)}, f32[8,8,640]{2,1,0:T(8,128)S(1)}, u32[]{:S(2)}, u32[]{:S(2)}) collective-permute-start(f32[8,8,640]{2,1,0:T(8,128)S(1)} %get-tuple-element.50), channel_id=1, source_target_pairs={{0,120},{8,16},{16,8},{24,32},{32,24},{40,48},{48,40},{56,64},{64,... | collective-permute-start | bytes 491528 | tf_op jit(solution)/shard_map/ppermute | solution.py:573
  9.4 20.0 %all-to-all-start = ((f32[32,16,128]{2,1,0:T(8,128)}), f32[32,16,128]{2,1,0:T(8,128)S(1)}, u32[]{:S(2)}, u32[]{:S(2)}) async-start(f32[32,16,128]{2,1,0:T(8,128)} %broadcast_in_dim.11), calls=%async_computation | async-start | bytes 524288 | tf_op jit(solution)/shard_map/all_to_all | solution.py:594
  20.0 8.5 %collective-permute-start.4 = (f32[32,128]{1,0:T(8,128)S(1)}, f32[32,128]{1,0:T(8,128)S(1)}, u32[]{:S(2)}, u32[]{:S(2)}) collective-permute-start(f32[32,128]{1,0:T(8,128)S(1)} %get-tuple-element.51), channel_id=1, source_target_pairs={{0,1},{1,0},{2,3},{3,2},{4,5},{5,4},{6,7},{7,6},{8,9},{9,8},{10,11... | collective-permute-start | bytes 49160 | tf_op jit(solution)/shard_map/ppermute | solution.py:573
  21.3 7.2 %collective-permute-start.5 = (f32[32,128]{1,0:T(8,128)S(1)}, f32[32,128]{1,0:T(8,128)S(1)}, u32[]{:S(2)}, u32[]{:S(2)}) collective-permute-start(f32[32,128]{1,0:T(8,128)S(1)} %get-tuple-element.52), channel_id=1, source_target_pairs={{0,7},{1,2},{2,1},{3,4},{4,3},{5,6},{6,5},{7,0},{8,15},{9,10},{10,... | collective-permute-start | bytes 49160 | tf_op jit(solution)/shard_map/ppermute | solution.py:573
  25.2 4.5 %collective-permute-start.6 = (s32[16,128]{1,0:T(8,128)S(1)}, s32[16,128]{1,0:T(8,128)S(1)}, u32[]{:S(2)}, u32[]{:S(2)}) collective-permute-start(s32[16,128]{1,0:T(8,128)S(1)} %get-tuple-element.58), channel_id=1, source_target_pairs={{0,8},{8,0},{1,9},{9,1},{2,10},{10,2},{3,11},{11,3},{4,12},{12,4},... | collective-permute-start | bytes 24584 | tf_op jit(solution)/shard_map/ppermute | solution.py:573
  30.3 5.9 %collective-permute-start.7 = (f32[7,16,128]{2,1,0:T(8,128)S(1)}, f32[7,16,128]{2,1,0:T(8,128)S(1)}, u32[]{:S(2)}, u32[]{:S(2)}) collective-permute-start(f32[7,16,128]{2,1,0:T(8,128)S(1)} %shard_map.76.share_ref), channel_id=1, source_target_pairs={{0,8},{8,0},{1,9},{9,1},{2,10},{10,2},{3,11},{11,3},{4,12},{12,4},... | collective-permute-start | bytes 172040 | tf_op jit(solution)/shard_map/ppermute | solution.py:573
  36.9 3.2 %collective-permute-start.8 = (f32[16,128]{1,0:T(8,128)S(1)}, f32[16,128]{1,0:T(8,128)S(1)}, u32[]{:S(2)}, u32[]{:S(2)}) collective-permute-start(f32[16,128]{1,0:T(8,128)S(1)} %get-tuple-element.65), channel_id=1, source_target_pairs={{0,128},{1,129},{128,0},{129,1},{2,130},{3,131},{130,2},{131,3},{4... | collective-permute-start | bytes 24584 | tf_op jit(solution)/shard_map/ppermute | solution.py:573
  36.9 3.8 %collective-permute-start.9 = (f32[16,128]{1,0:T(8,128)S(1)}, f32[16,128]{1,0:T(8,128)S(1)}, u32[]{:S(2)}, u32[]{:S(2)}) collective-permute-start(f32[16,128]{1,0:T(8,128)S(1)} %get-tuple-element.65), channel_id=1, source_target_pairs={{0,129},{1,128},{128,1},{129,0},{2,131},{3,130},{130,3},{131,2},{4... | collective-permute-start | bytes 24584 | tf_op jit(solution)/shard_map/ppermute | solution.py:573
  58.0 4.6 %collective-permute-start.10 = (f32[7,16,128]{2,1,0:T(8,128)S(1)}, f32[7,16,128]{2,1,0:T(8,128)S(1)}, u32[]{:S(2)}, u32[]{:S(2)}) collective-permute-start(f32[7,16,128]{2,1,0:T(8,128)S(1)} %shard_map.81.share_ref), channel_id=1, source_target_pairs={{0,8},{8,0},{1,9},{9,1},{2,10},{10,2},{3,11},{11,3},{4,12},{12,4},... | collective-permute-start | bytes 172040 | tf_op jit(solution)/shard_map/ppermute | solution.py:573
  63.2 3.2 %collective-permute-start.11 = (f32[16,128]{1,0:T(8,128)S(1)}, f32[16,128]{1,0:T(8,128)S(1)}, u32[]{:S(2)}, u32[]{:S(2)}) collective-permute-start(f32[16,128]{1,0:T(8,128)S(1)} %get-tuple-element.72), channel_id=1, source_target_pairs={{0,128},{1,129},{128,0},{129,1},{2,130},{3,131},{130,2},{131,3},{4... | collective-permute-start | bytes 24584 | tf_op jit(solution)/shard_map/ppermute | solution.py:573
  63.3 3.8 %collective-permute-start.12 = (f32[16,128]{1,0:T(8,128)S(1)}, f32[16,128]{1,0:T(8,128)S(1)}, u32[]{:S(2)}, u32[]{:S(2)}) collective-permute-start(f32[16,128]{1,0:T(8,128)S(1)} %get-tuple-element.72), channel_id=1, source_target_pairs={{0,129},{1,128},{128,1},{129,0},{2,131},{3,130},{130,3},{131,2},{4... | collective-permute-start | bytes 24584 | tf_op jit(solution)/shard_map/ppermute | solution.py:573
  81.1 4.6 %collective-permute-start.13 = (f32[7,16,128]{2,1,0:T(8,128)S(1)}, f32[7,16,128]{2,1,0:T(8,128)S(1)}, u32[]{:S(2)}, u32[]{:S(2)}) collective-permute-start(f32[7,16,128]{2,1,0:T(8,128)S(1)} %shard_map.85.share_ref), channel_id=1, source_target_pairs={{0,8},{8,0},{1,9},{9,1},{2,10},{10,2},{3,11},{11,3},{4,12},{12,4},... | collective-permute-start | bytes 172040 | tf_op jit(solution)/shard_map/ppermute | solution.py:573
  86.4 3.3 %collective-permute-start.14 = (f32[16,128]{1,0:T(8,128)S(1)}, f32[16,128]{1,0:T(8,128)S(1)}, u32[]{:S(2)}, u32[]{:S(2)}) collective-permute-start(f32[16,128]{1,0:T(8,128)S(1)} %get-tuple-element.79), channel_id=1, source_target_pairs={{0,128},{1,129},{128,0},{129,1},{2,130},{3,131},{130,2},{131,3},{4... | collective-permute-start | bytes 24584 | tf_op jit(solution)/shard_map/ppermute | solution.py:573
  87.2 3.7 %collective-permute-start.15 = (f32[16,128]{1,0:T(8,128)S(1)}, f32[16,128]{1,0:T(8,128)S(1)}, u32[]{:S(2)}, u32[]{:S(2)}) collective-permute-start(f32[16,128]{1,0:T(8,128)S(1)} %get-tuple-element.79), channel_id=1, source_target_pairs={{0,129},{1,128},{128,1},{129,0},{2,131},{3,130},{130,3},{131,2},{4... | collective-permute-start | bytes 24584 | tf_op jit(solution)/shard_map/ppermute | solution.py:573
  104.7 4.6 %collective-permute-start.16 = (f32[7,16,128]{2,1,0:T(8,128)S(1)}, f32[7,16,128]{2,1,0:T(8,128)S(1)}, u32[]{:S(2)}, u32[]{:S(2)}) collective-permute-start(f32[7,16,128]{2,1,0:T(8,128)S(1)} %shard_map.89.share_ref), channel_id=1, source_target_pairs={{0,8},{8,0},{1,9},{9,1},{2,10},{10,2},{3,11},{11,3},{4,12},{12,4},... | collective-permute-start | bytes 172040 | tf_op jit(solution)/shard_map/ppermute | solution.py:573

commit v5 on v4

--- a/solution.py
+++ b/solution.py
@@ -107,16 +107,21 @@
     lane = lane_of(shape)
     row = row_of(shape)
     copies[-1].wait()
-    first_core = (flags_ref[0, 0] & 1) == 0
-    for c in range(7):
-        for t in range(LANE_TILES):
-            cols = slice(t * LANES, (t + 1) * LANES)
-            top = [state_block(state_ref, 2 * c + k, 0, t) for k in range(2)]
-            end = [state_block(state_ref, 2 * c + k, CT // 8 - 1, t) for k in range(2)]
-            north = jnp.where(row < HALO, top[0], pltpu.roll(top[1], HALO, 0))
-            south = jnp.where(row < HALO, pltpu.roll(end[0], HALO, 0), end[1])
-            inner_ref[c, :, cols] = jnp.where(first_core, south, north)
-            cross_ref[c, :, cols] = jnp.where(first_core, north, south)
+    for rb in range(CT // 8):
+        west = jnp.zeros(shape, jnp.float32)
+        east = jnp.zeros(shape, jnp.float32)
+        for f in range(FIELDS):
+            first = state_block(state_ref, f, rb, 0)
+            last = state_block(state_ref, f, rb, LANE_TILES - 1)
+            here = (lane >= 8 * f) & (lane < 8 * f + HALO)
+            west = jnp.where(here, pltpu.roll(first, 8 * f, 1) if f else first, west)
+            east = jnp.where(here, pltpu.roll(last, (8 * f - 60) % LANES, 1), east)
+        if rb == 0:
+            here = (lane >= 112) & (lane < 112 + HALO)
+            west = jnp.where(here, pltpu.roll(aux_ref[:, 0:LANES], 112, 1), west)
+            east = jnp.where(here, pltpu.roll(aux_ref[:, LAST:COLS], 112 - 60, 1), east)
+        rows = slice(rb * 8, rb * 8 + 8)
+        inner_ref[rows, :], cross_ref[rows, :] = ordered(flags_ref[1, 0], east, west)
 
     def doubled(line):
         line = jnp.concatenate([line, jnp.zeros((1, LANES - SLOTS), jnp.float32)], axis=1)
@@ -143,9 +148,6 @@
             weight_ref[rb * LANE_TILES + t] = jnp.where(inside, down * along, 0.0)
     packet_ref[...] = build_packet(functools.partial(state_block, state_ref), index_ref, weight_ref)
 
-    inner_ref[7] = aux_ref[...]
-    cross_ref[7] = aux_ref[...]
-
 
 def ordered(flag, inner, cross):
     first = (flag & 1) == 0
@@ -172,34 +174,31 @@
     return (source - whole * SLOTS).astype(jnp.int32) + 64 * (tile & 1), tile // 2
 
 
-def side_kernel(aux_ref, state_ref, lat_inner_ref, lat_cross_ref, inner_ref, cross_ref, column_ref):
+def lat_kernel(aux_ref, state_ref, lon_inner_ref, lon_cross_ref, inner_ref, cross_ref):
     shape = (8, LANES)
-    source = jnp.broadcast_to(column_list(aux_ref, lat_inner_ref, lat_cross_ref)[2:3, :], shape)
-    column_ref[0:8, :], column_ref[8:16, :] = donor_places(source)
-    lat, lon = place_of(aux_ref)
     lane = lane_of(shape)
     row = row_of(shape)
-    for rb in range(ROWS // 8):
-        west = jnp.zeros(shape, jnp.float32)
-        east = jnp.zeros(shape, jnp.float32)
-        for f in range(FIELDS):
-            c, k = f // 2, f % 2
-            if rb < CT // 8:
-                first = state_block(state_ref, f, rb, 0)
-                last = state_block(state_ref, f, rb, LANE_TILES - 1)
-            else:
-                first = outer_rows(*ordered(lat, lat_inner_ref[c, :, 0:LANES], lat_cross_ref[c, :, 0:LANES]), k, row)
-                last = outer_rows(*ordered(lat, lat_inner_ref[c, :, LAST:COLS], lat_cross_ref[c, :, LAST:COLS]), k, row)
-            here = (lane >= 8 * f) & (lane < 8 * f + HALO)
-            west = jnp.where(here, pltpu.roll(first, 8 * f, 1) if f else first, west)
-            east = jnp.where(here, pltpu.roll(last, (8 * f - 60) % LANES, 1), east)
-        if rb == 0:
-            here = (lane >= 112) & (lane < 112 + HALO)
-            west = jnp.where(here, pltpu.roll(aux_ref[:, 0:LANES], 112, 1), west)
-            east = jnp.where(here, pltpu.roll(aux_ref[:, LAST:COLS], 112 - 60, 1), east)
-        inner, cross = ordered(lon, east, west)
-        inner_ref[rb * 8 : rb * 8 + 8, :] = inner
-        cross_ref[rb * 8 : rb * 8 + 8, :] = cross
+    lat, lon = place_of(aux_ref)
+    first_core = (lat & 1) == 0
+
+    def block(f, rb, t):
+        value = state_block(state_ref, f, rb, t)
+        if t < LANE_TILES - 1:
+            return value
+        rows = slice(rb * 8, rb * 8 + 8)
+        return with_columns(value, *ordered(lon, lon_inner_ref[rows, :], lon_cross_ref[rows, :]), f, lane)
+
+    for c in range(7):
+        for t in range(LANE_TILES):
+            cols = slice(t * LANES, (t + 1) * LANES)
+            top = [block(2 * c + k, 0, t) for k in range(2)]
+            end = [block(2 * c + k, CT // 8 - 1, t) for k in range(2)]
+            north = jnp.where(row < HALO, top[0], pltpu.roll(top[1], HALO, 0))
+            south = jnp.where(row < HALO, pltpu.roll(end[0], HALO, 0), end[1])
+            inner_ref[c, :, cols] = jnp.where(first_core, south, north)
+            cross_ref[c, :, cols] = jnp.where(first_core, north, south)
+    inner_ref[7] = aux_ref[...]
+    cross_ref[7] = aux_ref[...]
 
 
 def with_columns(block, from_east, from_west, f, lane):
@@ -209,7 +208,7 @@
 
 def frame_kernel(
     aux_ref, state_ref, lat_inner_ref, lat_cross_ref, lon_inner_ref, lon_cross_ref,
-    full_ref, slot_ref, tile_ref, cos_ref, sin_ref, metric_ref,
+    full_ref, slot_ref, tile_ref, cos_ref, sin_ref, metric_ref, column_ref,
 ):
     shape = (8, LANES)
     lat, lon = place_of(aux_ref)
@@ -217,18 +216,18 @@
     row = row_of(shape)
     for rb in range(ROWS // 8):
         rows = slice(rb * 8, rb * 8 + 8)
-        east, west = ordered(lon, lon_inner_ref[rows, :], lon_cross_ref[rows, :])
         for f in range(FIELDS):
             c, k = f // 2, f % 2
             for t in range(LANE_TILES):
                 cols = slice(t * LANES, (t + 1) * LANES)
                 if rb < CT // 8:
                     block = state_block(state_ref, f, rb, t)
+                    if t == LANE_TILES - 1:
+                        sides = ordered(lon, lon_inner_ref[rows, :], lon_cross_ref[rows, :])
+                        block = with_columns(block, *sides, f, lane)
                 else:
                     south, north = ordered(lat, lat_inner_ref[c, :, cols], lat_cross_ref[c, :, cols])
                     block = outer_rows(south, north, k, row)
-                if t == LANE_TILES - 1:
-                    block = with_columns(block, east, west, f, lane)
                 full_ref[f, rows, cols] = block
     for t in range(LANE_TILES + 1):
         if t < LANE_TILES:
@@ -244,6 +243,8 @@
             source = jnp.broadcast_to(block[2:3, :], shape)
             angle = jnp.broadcast_to(block[3:4, :], shape)
         slot_ref[t], tile_ref[t] = donor_places(source)
+        if t == LANE_TILES:
+            column_ref[0:8, :], column_ref[8:16, :] = donor_places(source)
         cos_ref[t] = jnp.cos(angle)
         sin_ref[t] = jnp.sin(angle)
     line = row_of((ROWS, LANES))
@@ -609,41 +610,38 @@
     vreg = (8, LANES)
     packed = ((16, LANES), f32)
     whole = ((FIELDS, ROWS, COLS), f32)
-    message = ((8, 8, COLS), f32)
-    side = ((ROWS, LANES), f32)
-    tile, aux, packet, lat_inner, lat_cross, index, weight = call(
+    lat_message = ((8, 8, COLS), f32)
+    lon_message = ((CT, LANES), f32)
+    tile, aux, packet, lon_inner, lon_cross, index, weight = call(
         open_kernel,
         [flags, tile] + raw,
         [
             ((FIELDS, CT, CP), f32),
             ((8, COLS), f32),
             packed,
-            message,
-            message,
+            lon_message,
+            lon_message,
             ((LANE_TILES,) + vreg, jnp.int32),
             ((3 * LANE_TILES,) + vreg, f32),
         ],
         scratch=[pltpu.VMEM(a.shape, a.dtype) for a in raw] + [pltpu.SemaphoreType.DMA((len(raw) + 1,))],
         left=range(1, 8),
     )
+    lon_inner = within(lon_inner, LON)
+    lon_cross = between(lon_cross, LON)
+    pair = swap_packets(packet)
+    lat_inner, lat_cross = call(lat_kernel, [aux, tile, lon_inner, lon_cross], [lat_message] * 2, cost=8_000_000)
     lat_inner = within(lat_inner, LAT)
     lat_cross = between(lat_cross, LAT)
-    lon_inner, lon_cross, column = call(
-        side_kernel, [aux, tile, lat_inner, lat_cross], [side, side, ((16, LANES), jnp.int32)], cost=8_000_000
-    )
-    column = other_core(column)
-    pair = swap_packets(packet)
-    lon_inner = within(lon_inner, LON)
-    lon_cross = between(lon_cross, LON)
     donors = spread_packets(pair)
-    donors, lon_inner, lon_cross = lax.optimization_barrier((donors, lon_inner, lon_cross))
+    donors, lat_inner, lat_cross = lax.optimization_barrier((donors, lat_inner, lat_cross))
     points = (LANE_TILES + 1,) + vreg
-    full, slot, where, cosine, sine, metric = call(
+    full, slot, where, cosine, sine, metric, column = call(
         frame_kernel,
         [aux, tile, lat_inner, lat_cross, lon_inner, lon_cross],
-        [whole, (points, jnp.int32), (points, jnp.int32), (points, f32), (points, f32), ((ROWS, LANES), f32)],
+        [whole, (points, jnp.int32), (points, jnp.int32), (points, f32), (points, f32), ((ROWS, LANES), f32), ((16, LANES), jnp.int32)],
     )
-    lists = [slot, where, column]
+    lists = [slot, where, other_core(column)]
     kept = [pltpu.VMEM((16, COLS), f32), pltpu.VMEM((FIELDS, ROWS, LANES), f32)]
 
     def ghost_tables(donors):
@@ -656,6 +654,7 @@
     for factor in (time_step / 2, time_step / 2, time_step):
         if len(states) == 1:
             (inner,) = call(first_inner_kernel, [metric, full], [whole], cost=2_000_000)
+            donors, inner = lax.optimization_barrier((donors, inner))
         else:
             pair = swap_packets(packet)
             now, inner = call(

time: 111 us -> 111 us (level)
  waiting for transfers between devices: 5.43 us -> 12.5 us
  starting transfers between devices: 45.7 us -> 41.9 us
  blocking collectives: 43.2 us -> 39.5 us
    ppermute x17, waiting for transfers between devices: 4.48 us -> 12.5 us  [permute(): return lax.ppermute(value, axes if len(axes) > 1 else axes[0], pairs)]
    all_to_all x3, blocking collectives: 43.2 us -> 39.5 us  [spread_packets(): lax.all_to_all(jnp.broadcast_to(pair[None], (count,) + pair.shape), ('y',...]
    ppermute x17, starting transfers between devices: 35.4 us -> 33.1 us  [permute(): return lax.ppermute(value, axes if len(axes) > 1 else axes[0], pairs)]
    all_to_all x1, starting transfers between devices: 10.3 us -> 8.76 us  [spread_packets(): lax.all_to_all(jnp.broadcast_to(pair[None], (count,) + pair.shape), ('y',...]
  transfers between devices with their start and end apart: 18 -> 18, of which waited for: 7 -> 8; matrix products, arithmetic and copies ran while one was open for 1% -> 1% of each run, Pallas kernels for 7% -> 7%
where the time goes in v5:
time: 111 us; the launch traced here: 110 us
  starting transfers between devices  41.9 us (38%)
  blocking collectives  39.5 us (36%)
  Pallas kernels  15.2 us (14%)
  waiting for transfers between devices  12.5 us (11%)
    all_to_all x3, blocking collectives, spread_packets(): lax.all_to_all(jnp.broadcast_to(pair[None], (count,) + pair.shape), ('y',...  39.5 us
    ppermute x17, starting transfers between devices, permute(): return lax.ppermute(value, axes if len(axes) > 1 else axes[0], pairs)  33.1 us
    pallas_call x18, Pallas kernels, call(): pl.pallas_call(kernel, out_shape=shapes, in_specs=[hbm if i in left else...  15.2 us
    ppermute x17, waiting for transfers between devices, permute(): return lax.ppermute(value, axes if len(axes) > 1 else axes[0], pairs)  12.5 us
    all_to_all x1, starting transfers between devices, spread_packets(): lax.all_to_all(jnp.broadcast_to(pair[None], (count,) + pair.shape), ('y',...  8.76 us
  transfers between devices with their start and end apart: 18, of which 8 were waited for; matrix products, arithmetic and copies ran while one was open for 1% of the time, Pallas kernels for 7%

profile of v5, /device:TPU:1, one launch (start us, length us, event | category | flops | bytes accessed | tf_op | source)
XLA Modules:
  0.0 110.2 jit_solution(16273034221058774944)
XLA Ops:
  0.0 0.1 stack.20
  0.1 0.1 broadcast_in_dim.10.flags_ref
  0.2 1.9 %shard_map.73 = (f32[14,24,576]{2,1,0:T(8,128)S(1)}, f32[8,640]{1,0:T(8,128)S(1)}, f32[16,128]{1,0:T(8,128)S(1)}, f32[24,128]{1,0:T(8,128)S(1)}, f32[24,128]{1,0...) custom-call(s32[8,128]{1,0:T(8,128)S(1)} %broadcast_in_dim.10.flags_ref, f32[14,24,576]{2,1,0:T(8,128)} %bitcast.7, ...), custom_call_target="tpu_custom_call" | custom-call | tf_op jit(solution)/shard_map/pallas_call | solution.py:548
  2.0 2.1 %collective-permute-start = (f32[16,128]{1,0:T(8,128)S(1)}, f32[16,128]{1,0:T(8,128)S(1)}, u32[]{:S(2)}, u32[]{:S(2)}) collective-permute-start(f32[16,128]{1,0:T(8,128)S(1)} %get-tuple-element.49), channel_id=1, source_target_pairs={{0,128},{1,129},{128,0},{129,1},{2,130},{3,131},{130,2},{131,3},{4... | collective-permute-start | bytes 24584 | tf_op jit(solution)/shard_map/ppermute | solution.py:574
  4.2 1.8 %collective-permute-start.1 = (f32[16,128]{1,0:T(8,128)S(1)}, f32[16,128]{1,0:T(8,128)S(1)}, u32[]{:S(2)}, u32[]{:S(2)}) collective-permute-start(f32[16,128]{1,0:T(8,128)S(1)} %get-tuple-element.49), channel_id=1, source_target_pairs={{0,129},{1,128},{128,1},{129,0},{2,131},{3,130},{130,3},{131,2},{4... | collective-permute-start | bytes 24584 | tf_op jit(solution)/shard_map/ppermute | solution.py:574
  6.0 0.6 collective-permute-start.2
  6.6 4.8 %collective-permute-start.3 = (f32[24,128]{1,0:T(8,128)S(1)}, f32[24,128]{1,0:T(8,128)S(1)}, u32[]{:S(2)}, u32[]{:S(2)}) collective-permute-start(f32[24,128]{1,0:T(8,128)S(1)} %get-tuple-element.52), channel_id=1, source_target_pairs={{0,7},{1,2},{2,1},{3,4},{4,3},{5,6},{6,5},{7,0},{8,15},{9,10},{10,... | collective-permute-start | bytes 36872 | tf_op jit(solution)/shard_map/ppermute | solution.py:574
  11.4 0.0 collective-permute-done
  11.4 0.0 collective-permute-done.1
  11.4 0.7 broadcast_in_dim.11
  12.2 8.8 %all-to-all-start = ((f32[32,16,128]{2,1,0:T(8,128)}), f32[32,16,128]{2,1,0:T(8,128)S(1)}, u32[]{:S(2)}, u32[]{:S(2)}) async-start(f32[32,16,128]{2,1,0:T(8,128)} %broadcast_in_dim.11), calls=%async_computation | async-start | bytes 524288 | tf_op jit(solution)/shard_map/all_to_all | solution.py:595
  20.9 0.0 collective-permute-done.2.lon_inner_ref
  20.9 0.0 collective-permute-done.3.lon_cross_ref
  20.9 0.2 shard_map.74
  21.1 2.2 %collective-permute-start.4 = (f32[8,8,640]{2,1,0:T(8,128)S(1)}, f32[8,8,640]{2,1,0:T(8,128)S(1)}, u32[]{:S(2)}, u32[]{:S(2)}) collective-permute-start(f32[8,8,640]{2,1,0:T(8,128)S(1)} %get-tuple-element.53), channel_id=1, source_target_pairs={{0,8},{8,0},{16,24},{24,16},{32,40},{40,32},{48,56},{56,48},{64,72... | collective-permute-start | bytes 491528 | tf_op jit(solution)/shard_map/ppermute | solution.py:574
  23.3 1.5 %collective-permute-start.5 = (f32[8,8,640]{2,1,0:T(8,128)S(1)}, f32[8,8,640]{2,1,0:T(8,128)S(1)}, u32[]{:S(2)}, u32[]{:S(2)}) collective-permute-start(f32[8,8,640]{2,1,0:T(8,128)S(1)} %get-tuple-element.54), channel_id=1, source_target_pairs={{0,120},{8,16},{16,8},{24,32},{32,24},{40,48},{48,40},{56,64},{64,... | collective-permute-start | bytes 491528 | tf_op jit(solution)/shard_map/ppermute | solution.py:574
  24.8 0.0 collective-permute-done.4.lat_inner_ref
  24.8 6.3 %collective-permute-done.5.lat_cross_ref = f32[8,8,640]{2,1,0:T(8,128)S(1)} collective-permute-done((f32[8,8,640]{2,1,0:T(8,128)S(1)}, f32[8,8,640]{2,1,0:T(8,128)S(1)}, u32[]{:S(2)}, u32[]{:S(2)}) %collective-permute-start.5) | collective-permute-done | bytes 163872 | tf_op jit(solution)/shard_map/ppermute | solution.py:574
  31.1 0.0 all-to-all-done.donor_ref
  31.1 0.3 shard_map.75
  31.4 4.5 %collective-permute-start.6 = (s32[16,128]{1,0:T(8,128)S(1)}, s32[16,128]{1,0:T(8,128)S(1)}, u32[]{:S(2)}, u32[]{:S(2)}) collective-permute-start(s32[16,128]{1,0:T(8,128)S(1)} %get-tuple-element.63), channel_id=1, source_target_pairs={{0,8},{8,0},{1,9},{9,1},{2,10},{10,2},{3,11},{11,3},{4,12},{12,4},... | collective-permute-start | bytes 24584 | tf_op jit(solution)/shard_map/ppermute | solution.py:574
  35.8 1.5 %shard_map.76.inner_ref = f32[14,32,640]{2,1,0:T(8,128)S(1)} custom-call(f32[32,128]{1,0:T(8,128)S(1)} %get-tuple-element.58.metric_ref, f32[14,32,640]{2,1,0:T(8,128)S(1)} %get-tuple-element.59.full_ref.now_ref), custom_call_target="tpu_custom_call" | custom-call | flops 2000000000 | bytes 2000000 | tf_op jit(solution)/shard_map/pallas_call | solution.py:548
  37.3 0.0 collective-permute-done.6.other_ref
  37.3 0.6 shard_map.77.share_ref
  37.9 0.1 collective-permute-start.7
  38.0 0.3 shard_map.78.total_ref
  38.3 0.9 collective-permute-done.7.other_ref
  39.2 0.7 shard_map.79
  39.9 0.3 collective-permute-start.8
  40.2 1.1 %collective-permute-start.9 = (f32[16,128]{1,0:T(8,128)S(1)}, f32[16,128]{1,0:T(8,128)S(1)}, u32[]{:S(2)}, u32[]{:S(2)}) collective-permute-start(f32[16,128]{1,0:T(8,128)S(1)} %get-tuple-element.69), channel_id=1, source_target_pairs={{0,129},{1,128},{128,1},{129,0},{2,131},{3,130},{130,3},{131,2},{4... | collective-permute-start | bytes 24584 | tf_op jit(solution)/shard_map/ppermute | solution.py:574
  41.4 1.8 %shard_map.80 = (f32[14,32,640]{2,1,0:T(8,128)S(1)}, f32[14,32,640]{2,1,0:T(8,128)S(1)}) custom-call(f32[8,640]{1,0:T(8,128)S(1)} %get-tuple-element.48.aux_ref, f32[32,128]{1,0:T(8,128)S(1)} %get-tuple-element.58.metric_ref, f32[14,32,640]{2,1,0:T(8,128)S(1)} %get-tuple-element.59.full_ref.now_ref, f32[14,32,640]{2,1,0:T(8,128)S(1)} %shard_map.76.inner_ref, ...), custom_call_target="tpu_custom_call" | custom-call | flops 2000000000 | bytes 2000000 | tf_op jit(solution)/shard_map/pallas_call | solution.py:548
  43.1 0.0 collective-permute-done.8
  43.2 0.8 collective-permute-done.9
  44.0 13.2 %all_to_all.20.donor_ref = f32[32,16,128]{2,1,0:T(8,128)S(1)} all-to-all(f32[32,16,128]{2,1,0:T(8,128)S(1)} %broadcast_in_dim.12), channel_id=1, replica_groups=mesh['panel'=2,'z'=8,'core'=2,'y'=4,'xh'=2] {'y','z'}, dimensions={0} | all-to-all | bytes 524288 | tf_op jit(solution)/shard_map/all_to_all | solution.py:595
  57.2 0.6 shard_map.81.share_ref
  57.7 3.7 %collective-permute-start.10 = (f32[7,16,128]{2,1,0:T(8,128)S(1)}, f32[7,16,128]{2,1,0:T(8,128)S(1)}, u32[]{:S(2)}, u32[]{:S(2)}) collective-permute-start(f32[7,16,128]{2,1,0:T(8,128)S(1)} %shard_map.81.share_ref), channel_id=1, source_target_pairs={{0,8},{8,0},{1,9},{9,1},{2,10},{10,2},{3,11},{11,3},{4,12},{12,4},... | collective-permute-start | bytes 172040 | tf_op jit(solution)/shard_map/ppermute | solution.py:574
  61.4 0.3 shard_map.82.total_ref
  61.7 0.6 collective-permute-done.10.other_ref
  62.3 0.7 shard_map.83
  63.0 0.6 collective-permute-start.11
  63.6 0.8 collective-permute-start.12
  64.4 1.6 %shard_map.84 = (f32[14,32,640]{2,1,0:T(8,128)S(1)}, f32[14,32,640]{2,1,0:T(8,128)S(1)}) custom-call(f32[8,640]{1,0:T(8,128)S(1)} %get-tuple-element.48.aux_ref, f32[32,128]{1,0:T(8,128)S(1)} %get-tuple-element.58.metric_ref, f32[14,32,640]{2,1,0:T(8,128)S(1)} %get-tuple-element.59.full_ref.now_ref, f32[14,32,640]{2,1,0:T(8,128)S(1)} %get-tuple-element.74.inner_ref, ...), custom_call_target="tpu_custom_call" | custom-call | flops 2000000000 | bytes 2000000 | tf_op jit(solution)/shard_map/pallas_call | solution.py:548
  66.0 0.0 collective-permute-done.11
  66.0 1.3 %collective-permute-done.12 = f32[16,128]{1,0:T(8,128)S(1)} collective-permute-done((f32[16,128]{1,0:T(8,128)S(1)}, f32[16,128]{1,0:T(8,128)S(1)}, u32[]{:S(2)}, u32[]{:S(2)}) %collective-permute-start.12) | collective-permute-done | bytes 8224 | tf_op jit(solution)/shard_map/ppermute | solution.py:574
  67.3 13.2 %all_to_all.21.donor_ref = f32[32,16,128]{2,1,0:T(8,128)S(1)} all-to-all(f32[32,16,128]{2,1,0:T(8,128)S(1)} %broadcast_in_dim.13), channel_id=1, replica_groups=mesh['panel'=2,'z'=8,'core'=2,'y'=4,'xh'=2] {'y','z'}, dimensions={0} | all-to-all | bytes 524288 | tf_op jit(solution)/shard_map/all_to_all | solution.py:595
  80.5 0.6 shard_map.85.share_ref
  81.1 3.8 %collective-permute-start.13 = (f32[7,16,128]{2,1,0:T(8,128)S(1)}, f32[7,16,128]{2,1,0:T(8,128)S(1)}, u32[]{:S(2)}, u32[]{:S(2)}) collective-permute-start(f32[7,16,128]{2,1,0:T(8,128)S(1)} %shard_map.85.share_ref), channel_id=1, source_target_pairs={{0,8},{8,0},{1,9},{9,1},{2,10},{10,2},{3,11},{11,3},{4,12},{12,4},... | collective-permute-start | bytes 172040 | tf_op jit(solution)/shard_map/ppermute | solution.py:574
  84.8 0.3 shard_map.86.total_ref
  85.1 0.6 collective-permute-done.13.other_ref
  85.7 0.7 shard_map.87
  86.4 0.3 collective-permute-start.14
  86.7 1.2 %collective-permute-start.15 = (f32[16,128]{1,0:T(8,128)S(1)}, f32[16,128]{1,0:T(8,128)S(1)}, u32[]{:S(2)}, u32[]{:S(2)}) collective-permute-start(f32[16,128]{1,0:T(8,128)S(1)} %get-tuple-element.83), channel_id=1, source_target_pairs={{0,129},{1,128},{128,1},{129,0},{2,131},{3,130},{130,3},{131,2},{4... | collective-permute-start | bytes 24584 | tf_op jit(solution)/shard_map/ppermute | solution.py:574
  87.9 1.4 %shard_map.88 = (f32[14,32,640]{2,1,0:T(8,128)S(1)}, f32[14,24,640]{2,1,0:T(8,128)S(1)}, f32[14,24,640]{2,1,0:T(8,128)S(1)}) custom-call(f32[8,640]{1,0:T(8,128)S(1)} %get-tuple-element.48.aux_ref, f32[32,128]{1,0:T(8,128)S(1)} %get-tuple-element.58.metric_ref, f32[14,32,640]{2,1,0:T(8,128)S(1)} %get-tuple-element.59.full_ref.now_ref, ...), custom_call_target="tpu_custom_call" | custom-call | flops 2000000000 | bytes 2000000 | tf_op jit(solution)/shard_map/pallas_call | solution.py:548
  89.3 0.0 collective-permute-done.14
  89.3 1.2 %collective-permute-done.15 = f32[16,128]{1,0:T(8,128)S(1)} collective-permute-done((f32[16,128]{1,0:T(8,128)S(1)}, f32[16,128]{1,0:T(8,128)S(1)}, u32[]{:S(2)}, u32[]{:S(2)}) %collective-permute-start.15) | collective-permute-done | bytes 8224 | tf_op jit(solution)/shard_map/ppermute | solution.py:574
  90.5 13.1 %all_to_all.22.donor_ref = f32[32,16,128]{2,1,0:T(8,128)S(1)} all-to-all(f32[32,16,128]{2,1,0:T(8,128)S(1)} %broadcast_in_dim.14), channel_id=1, replica_groups=mesh['panel'=2,'z'=8,'core'=2,'y'=4,'xh'=2] {'y','z'}, dimensions={0} | all-to-all | bytes 524288 | tf_op jit(solution)/shard_map/all_to_all | solution.py:595
  103.6 0.6 shard_map.89.share_ref
  104.2 3.8 %collective-permute-start.16 = (f32[7,16,128]{2,1,0:T(8,128)S(1)}, f32[7,16,128]{2,1,0:T(8,128)S(1)}, u32[]{:S(2)}, u32[]{:S(2)}) collective-permute-start(f32[7,16,128]{2,1,0:T(8,128)S(1)} %shard_map.89.share_ref), channel_id=1, source_target_pairs={{0,8},{8,0},{1,9},{9,1},{2,10},{10,2},{3,11},{11,3},{4,12},{12,4},... | collective-permute-start | bytes 172040 | tf_op jit(solution)/shard_map/ppermute | solution.py:574
  108.0 0.9 collective-permute-done.16.other_ref
  108.8 1.4 %shard_map.90 = f32[14,24,576]{2,1,0:T(8,128)} custom-call(f32[8,640]{1,0:T(8,128)S(1)} %get-tuple-element.48.aux_ref, f32[7,16,128]{2,1,0:T(8,128)S(1)} %shard_map.89.share_ref, f32[7,16,128]{2,1,0:T(8,128)S(1)} %collective-permute-done.16.other_ref, f32[6,8,128]{2,1,0:T(8,128)S(1)} %get-tuple-element.64.cos_ref, ...), custom_call_target="tpu_custom_call" | custom-call | tf_op jit(solution)/shard_map/pallas_call | solution.py:548
  (8 shorter events, 0.1 us)
Async XLA Ops:
  2.0 9.4 %collective-permute-start = (f32[16,128]{1,0:T(8,128)S(1)}, f32[16,128]{1,0:T(8,128)S(1)}, u32[]{:S(2)}, u32[]{:S(2)}) collective-permute-start(f32[16,128]{1,0:T(8,128)S(1)} %get-tuple-element.49), channel_id=1, source_target_pairs={{0,128},{1,129},{128,0},{129,1},{2,130},{3,131},{130,2},{131,3},{4... | collective-permute-start | bytes 24584 | tf_op jit(solution)/shard_map/ppermute | solution.py:574
  4.2 7.3 %collective-permute-start.1 = (f32[16,128]{1,0:T(8,128)S(1)}, f32[16,128]{1,0:T(8,128)S(1)}, u32[]{:S(2)}, u32[]{:S(2)}) collective-permute-start(f32[16,128]{1,0:T(8,128)S(1)} %get-tuple-element.49), channel_id=1, source_target_pairs={{0,129},{1,128},{128,1},{129,0},{2,131},{3,130},{130,3},{131,2},{4... | collective-permute-start | bytes 24584 | tf_op jit(solution)/shard_map/ppermute | solution.py:574
  6.0 14.9 %collective-permute-start.2 = (f32[24,128]{1,0:T(8,128)S(1)}, f32[24,128]{1,0:T(8,128)S(1)}, u32[]{:S(2)}, u32[]{:S(2)}) collective-permute-start(f32[24,128]{1,0:T(8,128)S(1)} %get-tuple-element.51), channel_id=1, source_target_pairs={{0,1},{1,0},{2,3},{3,2},{4,5},{5,4},{6,7},{7,6},{8,9},{9,8},{10,11... | collective-permute-start | bytes 36872 | tf_op jit(solution)/shard_map/ppermute | solution.py:574
  6.6 14.3 %collective-permute-start.3 = (f32[24,128]{1,0:T(8,128)S(1)}, f32[24,128]{1,0:T(8,128)S(1)}, u32[]{:S(2)}, u32[]{:S(2)}) collective-permute-start(f32[24,128]{1,0:T(8,128)S(1)} %get-tuple-element.52), channel_id=1, source_target_pairs={{0,7},{1,2},{2,1},{3,4},{4,3},{5,6},{6,5},{7,0},{8,15},{9,10},{10,... | collective-permute-start | bytes 36872 | tf_op jit(solution)/shard_map/ppermute | solution.py:574
  12.2 18.9 %all-to-all-start = ((f32[32,16,128]{2,1,0:T(8,128)}), f32[32,16,128]{2,1,0:T(8,128)S(1)}, u32[]{:S(2)}, u32[]{:S(2)}) async-start(f32[32,16,128]{2,1,0:T(8,128)} %broadcast_in_dim.11), calls=%async_computation | async-start | bytes 524288 | tf_op jit(solution)/shard_map/all_to_all | solution.py:595
  21.1 3.7 %collective-permute-start.4 = (f32[8,8,640]{2,1,0:T(8,128)S(1)}, f32[8,8,640]{2,1,0:T(8,128)S(1)}, u32[]{:S(2)}, u32[]{:S(2)}) collective-permute-start(f32[8,8,640]{2,1,0:T(8,128)S(1)} %get-tuple-element.53), channel_id=1, source_target_pairs={{0,8},{8,0},{16,24},{24,16},{32,40},{40,32},{48,56},{56,48},{64,72... | collective-permute-start | bytes 491528 | tf_op jit(solution)/shard_map/ppermute | solution.py:574
  23.3 7.8 %collective-permute-start.5 = (f32[8,8,640]{2,1,0:T(8,128)S(1)}, f32[8,8,640]{2,1,0:T(8,128)S(1)}, u32[]{:S(2)}, u32[]{:S(2)}) collective-permute-start(f32[8,8,640]{2,1,0:T(8,128)S(1)} %get-tuple-element.54), channel_id=1, source_target_pairs={{0,120},{8,16},{16,8},{24,32},{32,24},{40,48},{48,40},{56,64},{64,... | collective-permute-start | bytes 491528 | tf_op jit(solution)/shard_map/ppermute | solution.py:574
  31.4 5.9 %collective-permute-start.6 = (s32[16,128]{1,0:T(8,128)S(1)}, s32[16,128]{1,0:T(8,128)S(1)}, u32[]{:S(2)}, u32[]{:S(2)}) collective-permute-start(s32[16,128]{1,0:T(8,128)S(1)} %get-tuple-element.63), channel_id=1, source_target_pairs={{0,8},{8,0},{1,9},{9,1},{2,10},{10,2},{3,11},{11,3},{4,12},{12,4},... | collective-permute-start | bytes 24584 | tf_op jit(solution)/shard_map/ppermute | solution.py:574
  37.9 1.3 %collective-permute-start.7 = (f32[7,16,128]{2,1,0:T(8,128)S(1)}, f32[7,16,128]{2,1,0:T(8,128)S(1)}, u32[]{:S(2)}, u32[]{:S(2)}) collective-permute-start(f32[7,16,128]{2,1,0:T(8,128)S(1)} %shard_map.77.share_ref), channel_id=1, source_target_pairs={{0,8},{8,0},{1,9},{9,1},{2,10},{10,2},{3,11},{11,3},{4,12},{12,4},... | collective-permute-start | bytes 172040 | tf_op jit(solution)/shard_map/ppermute | solution.py:574
  39.9 3.3 %collective-permute-start.8 = (f32[16,128]{1,0:T(8,128)S(1)}, f32[16,128]{1,0:T(8,128)S(1)}, u32[]{:S(2)}, u32[]{:S(2)}) collective-permute-start(f32[16,128]{1,0:T(8,128)S(1)} %get-tuple-element.69), channel_id=1, source_target_pairs={{0,128},{1,129},{128,0},{129,1},{2,130},{3,131},{130,2},{131,3},{4... | collective-permute-start | bytes 24584 | tf_op jit(solution)/shard_map/ppermute | solution.py:574
  40.2 3.7 %collective-permute-start.9 = (f32[16,128]{1,0:T(8,128)S(1)}, f32[16,128]{1,0:T(8,128)S(1)}, u32[]{:S(2)}, u32[]{:S(2)}) collective-permute-start(f32[16,128]{1,0:T(8,128)S(1)} %get-tuple-element.69), channel_id=1, source_target_pairs={{0,129},{1,128},{128,1},{129,0},{2,131},{3,130},{130,3},{131,2},{4... | collective-permute-start | bytes 24584 | tf_op jit(solution)/shard_map/ppermute | solution.py:574
  57.7 4.6 %collective-permute-start.10 = (f32[7,16,128]{2,1,0:T(8,128)S(1)}, f32[7,16,128]{2,1,0:T(8,128)S(1)}, u32[]{:S(2)}, u32[]{:S(2)}) collective-permute-start(f32[7,16,128]{2,1,0:T(8,128)S(1)} %shard_map.81.share_ref), channel_id=1, source_target_pairs={{0,8},{8,0},{1,9},{9,1},{2,10},{10,2},{3,11},{11,3},{4,12},{12,4},... | collective-permute-start | bytes 172040 | tf_op jit(solution)/shard_map/ppermute | solution.py:574
  63.0 3.0 %collective-permute-start.11 = (f32[16,128]{1,0:T(8,128)S(1)}, f32[16,128]{1,0:T(8,128)S(1)}, u32[]{:S(2)}, u32[]{:S(2)}) collective-permute-start(f32[16,128]{1,0:T(8,128)S(1)} %get-tuple-element.76), channel_id=1, source_target_pairs={{0,128},{1,129},{128,0},{129,1},{2,130},{3,131},{130,2},{131,3},{4... | collective-permute-start | bytes 24584 | tf_op jit(solution)/shard_map/ppermute | solution.py:574
  63.6 3.7 %collective-permute-start.12 = (f32[16,128]{1,0:T(8,128)S(1)}, f32[16,128]{1,0:T(8,128)S(1)}, u32[]{:S(2)}, u32[]{:S(2)}) collective-permute-start(f32[16,128]{1,0:T(8,128)S(1)} %get-tuple-element.76), channel_id=1, source_target_pairs={{0,129},{1,128},{128,1},{129,0},{2,131},{3,130},{130,3},{131,2},{4... | collective-permute-start | bytes 24584 | tf_op jit(solution)/shard_map/ppermute | solution.py:574
  81.1 4.6 %collective-permute-start.13 = (f32[7,16,128]{2,1,0:T(8,128)S(1)}, f32[7,16,128]{2,1,0:T(8,128)S(1)}, u32[]{:S(2)}, u32[]{:S(2)}) collective-permute-start(f32[7,16,128]{2,1,0:T(8,128)S(1)} %shard_map.85.share_ref), channel_id=1, source_target_pairs={{0,8},{8,0},{1,9},{9,1},{2,10},{10,2},{3,11},{11,3},{4,12},{12,4},... | collective-permute-start | bytes 172040 | tf_op jit(solution)/shard_map/ppermute | solution.py:574
  86.4 2.9 %collective-permute-start.14 = (f32[16,128]{1,0:T(8,128)S(1)}, f32[16,128]{1,0:T(8,128)S(1)}, u32[]{:S(2)}, u32[]{:S(2)}) collective-permute-start(f32[16,128]{1,0:T(8,128)S(1)} %get-tuple-element.83), channel_id=1, source_target_pairs={{0,128},{1,129},{128,0},{129,1},{2,130},{3,131},{130,2},{131,3},{4... | collective-permute-start | bytes 24584 | tf_op jit(solution)/shard_map/ppermute | solution.py:574
  86.7 3.8 %collective-permute-start.15 = (f32[16,128]{1,0:T(8,128)S(1)}, f32[16,128]{1,0:T(8,128)S(1)}, u32[]{:S(2)}, u32[]{:S(2)}) collective-permute-start(f32[16,128]{1,0:T(8,128)S(1)} %get-tuple-element.83), channel_id=1, source_target_pairs={{0,129},{1,128},{128,1},{129,0},{2,131},{3,130},{130,3},{131,2},{4... | collective-permute-start | bytes 24584 | tf_op jit(solution)/shard_map/ppermute | solution.py:574
  104.2 4.6 %collective-permute-start.16 = (f32[7,16,128]{2,1,0:T(8,128)S(1)}, f32[7,16,128]{2,1,0:T(8,128)S(1)}, u32[]{:S(2)}, u32[]{:S(2)}) collective-permute-start(f32[7,16,128]{2,1,0:T(8,128)S(1)} %shard_map.89.share_ref), channel_id=1, source_target_pairs={{0,8},{8,0},{1,9},{9,1},{2,10},{10,2},{3,11},{11,3},{4,12},{12,4},... | collective-permute-start | bytes 172040 | tf_op jit(solution)/shard_map/ppermute | solution.py:574

commit v6 on v5

--- a/solution.py
+++ b/solution.py
@@ -32,6 +32,7 @@
 TILES = 128
 LANE_TILES = COLS // LANES
 LAST = COLS - LANES
+SPARE = 68
 VMEM_LIMIT = 24 * 1024 * 1024
 
 
@@ -163,9 +164,9 @@
 def column_list(aux_ref, lat_inner_ref, lat_cross_ref):
     lane = lane_of((8, LANES))
     block = aux_ref[:, 0:LANES]
-    south, north = ordered(place_of(aux_ref)[0], lat_inner_ref[7, :, 0:LANES], lat_cross_ref[7, :, 0:LANES])
-    block = jnp.where((lane >= CT) & (lane < CT + HALO), pltpu.roll(south, CT, 1), block)
-    return jnp.where((lane >= ROWS - HALO) & (lane < ROWS), pltpu.roll(north, 8, 1), block)
+    south, north = ordered(place_of(aux_ref)[0], lat_inner_ref[0, :, LAST:COLS], lat_cross_ref[0, :, LAST:COLS])
+    block = jnp.where((lane >= CT) & (lane < CT + HALO), pltpu.roll(south, (CT - SPARE) % LANES, 1), block)
+    return jnp.where((lane >= ROWS - HALO) & (lane < ROWS), pltpu.roll(north, (8 - SPARE) % LANES, 1), block)
 
 
 def donor_places(source):
@@ -195,10 +196,14 @@
             end = [block(2 * c + k, CT // 8 - 1, t) for k in range(2)]
             north = jnp.where(row < HALO, top[0], pltpu.roll(top[1], HALO, 0))
             south = jnp.where(row < HALO, pltpu.roll(end[0], HALO, 0), end[1])
-            inner_ref[c, :, cols] = jnp.where(first_core, south, north)
-            cross_ref[c, :, cols] = jnp.where(first_core, north, south)
-    inner_ref[7] = aux_ref[...]
-    cross_ref[7] = aux_ref[...]
+            inner = jnp.where(first_core, south, north)
+            cross = jnp.where(first_core, north, south)
+            if c == 0 and t == LANE_TILES - 1:
+                here = (lane >= SPARE) & (lane < SPARE + CT)
+                lists = pltpu.roll(aux_ref[:, 0:LANES], SPARE, 1)
+                inner, cross = jnp.where(here, lists, inner), jnp.where(here, lists, cross)
+            inner_ref[c, :, cols] = inner
+            cross_ref[c, :, cols] = cross
 
 
 def with_columns(block, from_east, from_west, f, lane):
@@ -228,6 +233,8 @@
                 else:
                     south, north = ordered(lat, lat_inner_ref[c, :, cols], lat_cross_ref[c, :, cols])
                     block = outer_rows(south, north, k, row)
+                    if t == LANE_TILES - 1:
+                        block = jnp.where((lane >= SPARE) & (lane < LANES - HALO), 0.0, block)
                 full_ref[f, rows, cols] = block
     for t in range(LANE_TILES + 1):
         if t < LANE_TILES:
@@ -610,7 +617,7 @@
     vreg = (8, LANES)
     packed = ((16, LANES), f32)
     whole = ((FIELDS, ROWS, COLS), f32)
-    lat_message = ((8, 8, COLS), f32)
+    lat_message = ((7, 8, COLS), f32)
     lon_message = ((CT, LANES), f32)
     tile, aux, packet, lon_inner, lon_cross, index, weight = call(
         open_kernel,

time: 111 us -> 110 us (level)
  no operation moved by 1% of the time
where the time goes in v6:
time: 110 us
  starting transfers between devices  42.1 us (38%)
  blocking collectives  39.4 us (36%)
  Pallas kernels  15.2 us (14%)
  waiting for transfers between devices  12.3 us (11%)
    all_to_all x3, blocking collectives, spread_packets(): lax.all_to_all(jnp.broadcast_to(pair[None], (count,) + pair.shape), ('y',...  39.4 us
    ppermute x17, starting transfers between devices, permute(): return lax.ppermute(value, axes if len(axes) > 1 else axes[0], pairs)  33.3 us
    pallas_call x18, Pallas kernels, call(): pl.pallas_call(kernel, out_shape=shapes, in_specs=[hbm if i in left else...  15.2 us
    ppermute x17, waiting for transfers between devices, permute(): return lax.ppermute(value, axes if len(axes) > 1 else axes[0], pairs)  12.3 us
    all_to_all x1, starting transfers between devices, spread_packets(): lax.all_to_all(jnp.broadcast_to(pair[None], (count,) + pair.shape), ('y',...  8.76 us
  transfers between devices with their start and end apart: 18, of which 8 were waited for; matrix products, arithmetic and copies ran while one was open for 1% of the time, Pallas kernels for 7%

profile of v6, /device:TPU:1, one launch (start us, length us, event | category | flops | bytes accessed | tf_op | source)
XLA Modules:
  0.0 110.1 jit_solution(9379380504475555516)
XLA Ops:
  0.0 0.1 stack.20
  0.1 0.1 broadcast_in_dim.10.flags_ref
  0.2 1.9 %shard_map.73 = (f32[14,24,576]{2,1,0:T(8,128)S(1)}, f32[8,640]{1,0:T(8,128)S(1)}, f32[16,128]{1,0:T(8,128)S(1)}, f32[24,128]{1,0:T(8,128)S(1)}, f32[24,128]{1,0...) custom-call(s32[8,128]{1,0:T(8,128)S(1)} %broadcast_in_dim.10.flags_ref, f32[14,24,576]{2,1,0:T(8,128)} %bitcast.7, ...), custom_call_target="tpu_custom_call" | custom-call | tf_op jit(solution)/shard_map/pallas_call | solution.py:555
  2.0 2.1 %collective-permute-start = (f32[16,128]{1,0:T(8,128)S(1)}, f32[16,128]{1,0:T(8,128)S(1)}, u32[]{:S(2)}, u32[]{:S(2)}) collective-permute-start(f32[16,128]{1,0:T(8,128)S(1)} %get-tuple-element.49), channel_id=1, source_target_pairs={{0,128},{1,129},{128,0},{129,1},{2,130},{3,131},{130,2},{131,3},{4... | collective-permute-start | bytes 24584 | tf_op jit(solution)/shard_map/ppermute | solution.py:581
  4.2 1.8 %collective-permute-start.1 = (f32[16,128]{1,0:T(8,128)S(1)}, f32[16,128]{1,0:T(8,128)S(1)}, u32[]{:S(2)}, u32[]{:S(2)}) collective-permute-start(f32[16,128]{1,0:T(8,128)S(1)} %get-tuple-element.49), channel_id=1, source_target_pairs={{0,129},{1,128},{128,1},{129,0},{2,131},{3,130},{130,3},{131,2},{4... | collective-permute-start | bytes 24584 | tf_op jit(solution)/shard_map/ppermute | solution.py:581
  6.0 0.6 collective-permute-start.2
  6.6 4.8 %collective-permute-start.3 = (f32[24,128]{1,0:T(8,128)S(1)}, f32[24,128]{1,0:T(8,128)S(1)}, u32[]{:S(2)}, u32[]{:S(2)}) collective-permute-start(f32[24,128]{1,0:T(8,128)S(1)} %get-tuple-element.52), channel_id=1, source_target_pairs={{0,7},{1,2},{2,1},{3,4},{4,3},{5,6},{6,5},{7,0},{8,15},{9,10},{10,... | collective-permute-start | bytes 36872 | tf_op jit(solution)/shard_map/ppermute | solution.py:581
  11.4 0.0 collective-permute-done
  11.4 0.0 collective-permute-done.1
  11.4 0.7 broadcast_in_dim.11
  12.2 8.8 %all-to-all-start = ((f32[32,16,128]{2,1,0:T(8,128)}), f32[32,16,128]{2,1,0:T(8,128)S(1)}, u32[]{:S(2)}, u32[]{:S(2)}) async-start(f32[32,16,128]{2,1,0:T(8,128)} %broadcast_in_dim.11), calls=%async_computation | async-start | bytes 524288 | tf_op jit(solution)/shard_map/all_to_all | solution.py:602
  20.9 0.0 collective-permute-done.2.lon_inner_ref
  20.9 0.0 collective-permute-done.3.lon_cross_ref
  20.9 0.2 shard_map.74
  21.1 2.2 %collective-permute-start.4 = (f32[7,8,640]{2,1,0:T(8,128)S(1)}, f32[7,8,640]{2,1,0:T(8,128)S(1)}, u32[]{:S(2)}, u32[]{:S(2)}) collective-permute-start(f32[7,8,640]{2,1,0:T(8,128)S(1)} %get-tuple-element.53), channel_id=1, source_target_pairs={{0,8},{8,0},{16,24},{24,16},{32,40},{40,32},{48,56},{56,48},{64,72... | collective-permute-start | bytes 430088 | tf_op jit(solution)/shard_map/ppermute | solution.py:581
  23.3 1.5 %collective-permute-start.5 = (f32[7,8,640]{2,1,0:T(8,128)S(1)}, f32[7,8,640]{2,1,0:T(8,128)S(1)}, u32[]{:S(2)}, u32[]{:S(2)}) collective-permute-start(f32[7,8,640]{2,1,0:T(8,128)S(1)} %get-tuple-element.54), channel_id=1, source_target_pairs={{0,120},{8,16},{16,8},{24,32},{32,24},{40,48},{48,40},{56,64},{64,... | collective-permute-start | bytes 430088 | tf_op jit(solution)/shard_map/ppermute | solution.py:581
  24.8 0.0 collective-permute-done.4.lat_inner_ref
  24.8 6.1 %collective-permute-done.5.lat_cross_ref = f32[7,8,640]{2,1,0:T(8,128)S(1)} collective-permute-done((f32[7,8,640]{2,1,0:T(8,128)S(1)}, f32[7,8,640]{2,1,0:T(8,128)S(1)}, u32[]{:S(2)}, u32[]{:S(2)}) %collective-permute-start.5) | collective-permute-done | bytes 143392 | tf_op jit(solution)/shard_map/ppermute | solution.py:581
  30.8 0.0 all-to-all-done.donor_ref
  30.8 0.3 shard_map.75
  31.2 4.7 %collective-permute-start.6 = (s32[16,128]{1,0:T(8,128)S(1)}, s32[16,128]{1,0:T(8,128)S(1)}, u32[]{:S(2)}, u32[]{:S(2)}) collective-permute-start(s32[16,128]{1,0:T(8,128)S(1)} %get-tuple-element.63), channel_id=1, source_target_pairs={{0,8},{8,0},{1,9},{9,1},{2,10},{10,2},{3,11},{11,3},{4,12},{12,4},... | collective-permute-start | bytes 24584 | tf_op jit(solution)/shard_map/ppermute | solution.py:581
  35.8 1.5 %shard_map.76.inner_ref = f32[14,32,640]{2,1,0:T(8,128)S(1)} custom-call(f32[32,128]{1,0:T(8,128)S(1)} %get-tuple-element.58.metric_ref, f32[14,32,640]{2,1,0:T(8,128)S(1)} %get-tuple-element.59.full_ref.now_ref), custom_call_target="tpu_custom_call" | custom-call | flops 2000000000 | bytes 2000000 | tf_op jit(solution)/shard_map/pallas_call | solution.py:555
  37.3 0.0 collective-permute-done.6.other_ref
  37.3 0.6 shard_map.77.share_ref
  37.9 0.1 collective-permute-start.7
  38.0 0.3 shard_map.78.total_ref
  38.3 0.9 collective-permute-done.7.other_ref
  39.2 0.7 shard_map.79
  39.9 0.3 collective-permute-start.8
  40.2 1.1 %collective-permute-start.9 = (f32[16,128]{1,0:T(8,128)S(1)}, f32[16,128]{1,0:T(8,128)S(1)}, u32[]{:S(2)}, u32[]{:S(2)}) collective-permute-start(f32[16,128]{1,0:T(8,128)S(1)} %get-tuple-element.69), channel_id=1, source_target_pairs={{0,129},{1,128},{128,1},{129,0},{2,131},{3,130},{130,3},{131,2},{4... | collective-permute-start | bytes 24584 | tf_op jit(solution)/shard_map/ppermute | solution.py:581
  41.4 1.8 %shard_map.80 = (f32[14,32,640]{2,1,0:T(8,128)S(1)}, f32[14,32,640]{2,1,0:T(8,128)S(1)}) custom-call(f32[8,640]{1,0:T(8,128)S(1)} %get-tuple-element.48.aux_ref, f32[32,128]{1,0:T(8,128)S(1)} %get-tuple-element.58.metric_ref, f32[14,32,640]{2,1,0:T(8,128)S(1)} %get-tuple-element.59.full_ref.now_ref, f32[14,32,640]{2,1,0:T(8,128)S(1)} %shard_map.76.inner_ref, ...), custom_call_target="tpu_custom_call" | custom-call | flops 2000000000 | bytes 2000000 | tf_op jit(solution)/shard_map/pallas_call | solution.py:555
  43.2 0.0 collective-permute-done.8
  43.2 0.8 collective-permute-done.9
  44.0 13.1 %all_to_all.20.donor_ref = f32[32,16,128]{2,1,0:T(8,128)S(1)} all-to-all(f32[32,16,128]{2,1,0:T(8,128)S(1)} %broadcast_in_dim.12), channel_id=1, replica_groups=mesh['panel'=2,'z'=8,'core'=2,'y'=4,'xh'=2] {'y','z'}, dimensions={0} | all-to-all | bytes 524288 | tf_op jit(solution)/shard_map/all_to_all | solution.py:602
  57.1 0.6 shard_map.81.share_ref
  57.6 3.7 %collective-permute-start.10 = (f32[7,16,128]{2,1,0:T(8,128)S(1)}, f32[7,16,128]{2,1,0:T(8,128)S(1)}, u32[]{:S(2)}, u32[]{:S(2)}) collective-permute-start(f32[7,16,128]{2,1,0:T(8,128)S(1)} %shard_map.81.share_ref), channel_id=1, source_target_pairs={{0,8},{8,0},{1,9},{9,1},{2,10},{10,2},{3,11},{11,3},{4,12},{12,4},... | collective-permute-start | bytes 172040 | tf_op jit(solution)/shard_map/ppermute | solution.py:581
  61.3 0.3 shard_map.82.total_ref
  61.6 0.6 collective-permute-done.10.other_ref
  62.2 0.7 shard_map.83
  62.9 0.6 collective-permute-start.11
  63.5 0.8 collective-permute-start.12
  64.3 1.6 %shard_map.84 = (f32[14,32,640]{2,1,0:T(8,128)S(1)}, f32[14,32,640]{2,1,0:T(8,128)S(1)}) custom-call(f32[8,640]{1,0:T(8,128)S(1)} %get-tuple-element.48.aux_ref, f32[32,128]{1,0:T(8,128)S(1)} %get-tuple-element.58.metric_ref, f32[14,32,640]{2,1,0:T(8,128)S(1)} %get-tuple-element.59.full_ref.now_ref, f32[14,32,640]{2,1,0:T(8,128)S(1)} %get-tuple-element.74.inner_ref, ...), custom_call_target="tpu_custom_call" | custom-call | flops 2000000000 | bytes 2000000 | tf_op jit(solution)/shard_map/pallas_call | solution.py:555
  65.9 0.0 collective-permute-done.11
  65.9 1.3 %collective-permute-done.12 = f32[16,128]{1,0:T(8,128)S(1)} collective-permute-done((f32[16,128]{1,0:T(8,128)S(1)}, f32[16,128]{1,0:T(8,128)S(1)}, u32[]{:S(2)}, u32[]{:S(2)}) %collective-permute-start.12) | collective-permute-done | bytes 8224 | tf_op jit(solution)/shard_map/ppermute | solution.py:581
  67.2 13.2 %all_to_all.21.donor_ref = f32[32,16,128]{2,1,0:T(8,128)S(1)} all-to-all(f32[32,16,128]{2,1,0:T(8,128)S(1)} %broadcast_in_dim.13), channel_id=1, replica_groups=mesh['panel'=2,'z'=8,'core'=2,'y'=4,'xh'=2] {'y','z'}, dimensions={0} | all-to-all | bytes 524288 | tf_op jit(solution)/shard_map/all_to_all | solution.py:602
  80.4 0.6 shard_map.85.share_ref
  81.0 3.8 %collective-permute-start.13 = (f32[7,16,128]{2,1,0:T(8,128)S(1)}, f32[7,16,128]{2,1,0:T(8,128)S(1)}, u32[]{:S(2)}, u32[]{:S(2)}) collective-permute-start(f32[7,16,128]{2,1,0:T(8,128)S(1)} %shard_map.85.share_ref), channel_id=1, source_target_pairs={{0,8},{8,0},{1,9},{9,1},{2,10},{10,2},{3,11},{11,3},{4,12},{12,4},... | collective-permute-start | bytes 172040 | tf_op jit(solution)/shard_map/ppermute | solution.py:581
  84.8 0.3 shard_map.86.total_ref
  85.1 0.6 collective-permute-done.13.other_ref
  85.6 0.7 shard_map.87
  86.3 0.3 collective-permute-start.14
  86.6 1.2 %collective-permute-start.15 = (f32[16,128]{1,0:T(8,128)S(1)}, f32[16,128]{1,0:T(8,128)S(1)}, u32[]{:S(2)}, u32[]{:S(2)}) collective-permute-start(f32[16,128]{1,0:T(8,128)S(1)} %get-tuple-element.83), channel_id=1, source_target_pairs={{0,129},{1,128},{128,1},{129,0},{2,131},{3,130},{130,3},{131,2},{4... | collective-permute-start | bytes 24584 | tf_op jit(solution)/shard_map/ppermute | solution.py:581
  87.8 1.4 %shard_map.88 = (f32[14,32,640]{2,1,0:T(8,128)S(1)}, f32[14,24,640]{2,1,0:T(8,128)S(1)}, f32[14,24,640]{2,1,0:T(8,128)S(1)}) custom-call(f32[8,640]{1,0:T(8,128)S(1)} %get-tuple-element.48.aux_ref, f32[32,128]{1,0:T(8,128)S(1)} %get-tuple-element.58.metric_ref, f32[14,32,640]{2,1,0:T(8,128)S(1)} %get-tuple-element.59.full_ref.now_ref, ...), custom_call_target="tpu_custom_call" | custom-call | flops 2000000000 | bytes 2000000 | tf_op jit(solution)/shard_map/pallas_call | solution.py:555
  89.2 0.0 collective-permute-done.14
  89.2 1.2 %collective-permute-done.15 = f32[16,128]{1,0:T(8,128)S(1)} collective-permute-done((f32[16,128]{1,0:T(8,128)S(1)}, f32[16,128]{1,0:T(8,128)S(1)}, u32[]{:S(2)}, u32[]{:S(2)}) %collective-permute-start.15) | collective-permute-done | bytes 8224 | tf_op jit(solution)/shard_map/ppermute | solution.py:581
  90.4 13.1 %all_to_all.22.donor_ref = f32[32,16,128]{2,1,0:T(8,128)S(1)} all-to-all(f32[32,16,128]{2,1,0:T(8,128)S(1)} %broadcast_in_dim.14), channel_id=1, replica_groups=mesh['panel'=2,'z'=8,'core'=2,'y'=4,'xh'=2] {'y','z'}, dimensions={0} | all-to-all | bytes 524288 | tf_op jit(solution)/shard_map/all_to_all | solution.py:602
  103.6 0.6 shard_map.89.share_ref
  104.1 3.8 %collective-permute-start.16 = (f32[7,16,128]{2,1,0:T(8,128)S(1)}, f32[7,16,128]{2,1,0:T(8,128)S(1)}, u32[]{:S(2)}, u32[]{:S(2)}) collective-permute-start(f32[7,16,128]{2,1,0:T(8,128)S(1)} %shard_map.89.share_ref), channel_id=1, source_target_pairs={{0,8},{8,0},{1,9},{9,1},{2,10},{10,2},{3,11},{11,3},{4,12},{12,4},... | collective-permute-start | bytes 172040 | tf_op jit(solution)/shard_map/ppermute | solution.py:581
  107.9 0.9 collective-permute-done.16.other_ref
  108.8 1.4 %shard_map.90 = f32[14,24,576]{2,1,0:T(8,128)} custom-call(f32[8,640]{1,0:T(8,128)S(1)} %get-tuple-element.48.aux_ref, f32[7,16,128]{2,1,0:T(8,128)S(1)} %shard_map.89.share_ref, f32[7,16,128]{2,1,0:T(8,128)S(1)} %collective-permute-done.16.other_ref, f32[6,8,128]{2,1,0:T(8,128)S(1)} %get-tuple-element.64.cos_ref, ...), custom_call_target="tpu_custom_call" | custom-call | tf_op jit(solution)/shard_map/pallas_call | solution.py:555
  (8 shorter events, 0.1 us)
Async XLA Ops:
  2.0 9.4 %collective-permute-start = (f32[16,128]{1,0:T(8,128)S(1)}, f32[16,128]{1,0:T(8,128)S(1)}, u32[]{:S(2)}, u32[]{:S(2)}) collective-permute-start(f32[16,128]{1,0:T(8,128)S(1)} %get-tuple-element.49), channel_id=1, source_target_pairs={{0,128},{1,129},{128,0},{129,1},{2,130},{3,131},{130,2},{131,3},{4... | collective-permute-start | bytes 24584 | tf_op jit(solution)/shard_map/ppermute | solution.py:581
  4.2 7.3 %collective-permute-start.1 = (f32[16,128]{1,0:T(8,128)S(1)}, f32[16,128]{1,0:T(8,128)S(1)}, u32[]{:S(2)}, u32[]{:S(2)}) collective-permute-start(f32[16,128]{1,0:T(8,128)S(1)} %get-tuple-element.49), channel_id=1, source_target_pairs={{0,129},{1,128},{128,1},{129,0},{2,131},{3,130},{130,3},{131,2},{4... | collective-permute-start | bytes 24584 | tf_op jit(solution)/shard_map/ppermute | solution.py:581
  6.0 14.9 %collective-permute-start.2 = (f32[24,128]{1,0:T(8,128)S(1)}, f32[24,128]{1,0:T(8,128)S(1)}, u32[]{:S(2)}, u32[]{:S(2)}) collective-permute-start(f32[24,128]{1,0:T(8,128)S(1)} %get-tuple-element.51), channel_id=1, source_target_pairs={{0,1},{1,0},{2,3},{3,2},{4,5},{5,4},{6,7},{7,6},{8,9},{9,8},{10,11... | collective-permute-start | bytes 36872 | tf_op jit(solution)/shard_map/ppermute | solution.py:581
  6.6 14.3 %collective-permute-start.3 = (f32[24,128]{1,0:T(8,128)S(1)}, f32[24,128]{1,0:T(8,128)S(1)}, u32[]{:S(2)}, u32[]{:S(2)}) collective-permute-start(f32[24,128]{1,0:T(8,128)S(1)} %get-tuple-element.52), channel_id=1, source_target_pairs={{0,7},{1,2},{2,1},{3,4},{4,3},{5,6},{6,5},{7,0},{8,15},{9,10},{10,... | collective-permute-start | bytes 36872 | tf_op jit(solution)/shard_map/ppermute | solution.py:581
  12.2 18.7 %all-to-all-start = ((f32[32,16,128]{2,1,0:T(8,128)}), f32[32,16,128]{2,1,0:T(8,128)S(1)}, u32[]{:S(2)}, u32[]{:S(2)}) async-start(f32[32,16,128]{2,1,0:T(8,128)} %broadcast_in_dim.11), calls=%async_computation | async-start | bytes 524288 | tf_op jit(solution)/shard_map/all_to_all | solution.py:602
  21.1 3.7 %collective-permute-start.4 = (f32[7,8,640]{2,1,0:T(8,128)S(1)}, f32[7,8,640]{2,1,0:T(8,128)S(1)}, u32[]{:S(2)}, u32[]{:S(2)}) collective-permute-start(f32[7,8,640]{2,1,0:T(8,128)S(1)} %get-tuple-element.53), channel_id=1, source_target_pairs={{0,8},{8,0},{16,24},{24,16},{32,40},{40,32},{48,56},{56,48},{64,72... | collective-permute-start | bytes 430088 | tf_op jit(solution)/shard_map/ppermute | solution.py:581
  23.3 7.6 %collective-permute-start.5 = (f32[7,8,640]{2,1,0:T(8,128)S(1)}, f32[7,8,640]{2,1,0:T(8,128)S(1)}, u32[]{:S(2)}, u32[]{:S(2)}) collective-permute-start(f32[7,8,640]{2,1,0:T(8,128)S(1)} %get-tuple-element.54), channel_id=1, source_target_pairs={{0,120},{8,16},{16,8},{24,32},{32,24},{40,48},{48,40},{56,64},{64,... | collective-permute-start | bytes 430088 | tf_op jit(solution)/shard_map/ppermute | solution.py:581
  31.2 6.1 %collective-permute-start.6 = (s32[16,128]{1,0:T(8,128)S(1)}, s32[16,128]{1,0:T(8,128)S(1)}, u32[]{:S(2)}, u32[]{:S(2)}) collective-permute-start(s32[16,128]{1,0:T(8,128)S(1)} %get-tuple-element.63), channel_id=1, source_target_pairs={{0,8},{8,0},{1,9},{9,1},{2,10},{10,2},{3,11},{11,3},{4,12},{12,4},... | collective-permute-start | bytes 24584 | tf_op jit(solution)/shard_map/ppermute | solution.py:581
  37.9 1.3 %collective-permute-start.7 = (f32[7,16,128]{2,1,0:T(8,128)S(1)}, f32[7,16,128]{2,1,0:T(8,128)S(1)}, u32[]{:S(2)}, u32[]{:S(2)}) collective-permute-start(f32[7,16,128]{2,1,0:T(8,128)S(1)} %shard_map.77.share_ref), channel_id=1, source_target_pairs={{0,8},{8,0},{1,9},{9,1},{2,10},{10,2},{3,11},{11,3},{4,12},{12,4},... | collective-permute-start | bytes 172040 | tf_op jit(solution)/shard_map/ppermute | solution.py:581
  39.9 3.3 %collective-permute-start.8 = (f32[16,128]{1,0:T(8,128)S(1)}, f32[16,128]{1,0:T(8,128)S(1)}, u32[]{:S(2)}, u32[]{:S(2)}) collective-permute-start(f32[16,128]{1,0:T(8,128)S(1)} %get-tuple-element.69), channel_id=1, source_target_pairs={{0,128},{1,129},{128,0},{129,1},{2,130},{3,131},{130,2},{131,3},{4... | collective-permute-start | bytes 24584 | tf_op jit(solution)/shard_map/ppermute | solution.py:581
  40.2 3.7 %collective-permute-start.9 = (f32[16,128]{1,0:T(8,128)S(1)}, f32[16,128]{1,0:T(8,128)S(1)}, u32[]{:S(2)}, u32[]{:S(2)}) collective-permute-start(f32[16,128]{1,0:T(8,128)S(1)} %get-tuple-element.69), channel_id=1, source_target_pairs={{0,129},{1,128},{128,1},{129,0},{2,131},{3,130},{130,3},{131,2},{4... | collective-permute-start | bytes 24584 | tf_op jit(solution)/shard_map/ppermute | solution.py:581
  57.6 4.6 %collective-permute-start.10 = (f32[7,16,128]{2,1,0:T(8,128)S(1)}, f32[7,16,128]{2,1,0:T(8,128)S(1)}, u32[]{:S(2)}, u32[]{:S(2)}) collective-permute-start(f32[7,16,128]{2,1,0:T(8,128)S(1)} %shard_map.81.share_ref), channel_id=1, source_target_pairs={{0,8},{8,0},{1,9},{9,1},{2,10},{10,2},{3,11},{11,3},{4,12},{12,4},... | collective-permute-start | bytes 172040 | tf_op jit(solution)/shard_map/ppermute | solution.py:581
  62.9 3.0 %collective-permute-start.11 = (f32[16,128]{1,0:T(8,128)S(1)}, f32[16,128]{1,0:T(8,128)S(1)}, u32[]{:S(2)}, u32[]{:S(2)}) collective-permute-start(f32[16,128]{1,0:T(8,128)S(1)} %get-tuple-element.76), channel_id=1, source_target_pairs={{0,128},{1,129},{128,0},{129,1},{2,130},{3,131},{130,2},{131,3},{4... | collective-permute-start | bytes 24584 | tf_op jit(solution)/shard_map/ppermute | solution.py:581
  63.5 3.7 %collective-permute-start.12 = (f32[16,128]{1,0:T(8,128)S(1)}, f32[16,128]{1,0:T(8,128)S(1)}, u32[]{:S(2)}, u32[]{:S(2)}) collective-permute-start(f32[16,128]{1,0:T(8,128)S(1)} %get-tuple-element.76), channel_id=1, source_target_pairs={{0,129},{1,128},{128,1},{129,0},{2,131},{3,130},{130,3},{131,2},{4... | collective-permute-start | bytes 24584 | tf_op jit(solution)/shard_map/ppermute | solution.py:581
  81.0 4.6 %collective-permute-start.13 = (f32[7,16,128]{2,1,0:T(8,128)S(1)}, f32[7,16,128]{2,1,0:T(8,128)S(1)}, u32[]{:S(2)}, u32[]{:S(2)}) collective-permute-start(f32[7,16,128]{2,1,0:T(8,128)S(1)} %shard_map.85.share_ref), channel_id=1, source_target_pairs={{0,8},{8,0},{1,9},{9,1},{2,10},{10,2},{3,11},{11,3},{4,12},{12,4},... | collective-permute-start | bytes 172040 | tf_op jit(solution)/shard_map/ppermute | solution.py:581
  86.3 2.9 %collective-permute-start.14 = (f32[16,128]{1,0:T(8,128)S(1)}, f32[16,128]{1,0:T(8,128)S(1)}, u32[]{:S(2)}, u32[]{:S(2)}) collective-permute-start(f32[16,128]{1,0:T(8,128)S(1)} %get-tuple-element.83), channel_id=1, source_target_pairs={{0,128},{1,129},{128,0},{129,1},{2,130},{3,131},{130,2},{131,3},{4... | collective-permute-start | bytes 24584 | tf_op jit(solution)/shard_map/ppermute | solution.py:581
  86.6 3.8 %collective-permute-start.15 = (f32[16,128]{1,0:T(8,128)S(1)}, f32[16,128]{1,0:T(8,128)S(1)}, u32[]{:S(2)}, u32[]{:S(2)}) collective-permute-start(f32[16,128]{1,0:T(8,128)S(1)} %get-tuple-element.83), channel_id=1, source_target_pairs={{0,129},{1,128},{128,1},{129,0},{2,131},{3,130},{130,3},{131,2},{4... | collective-permute-start | bytes 24584 | tf_op jit(solution)/shard_map/ppermute | solution.py:581
  104.1 4.6 %collective-permute-start.16 = (f32[7,16,128]{2,1,0:T(8,128)S(1)}, f32[7,16,128]{2,1,0:T(8,128)S(1)}, u32[]{:S(2)}, u32[]{:S(2)}) collective-permute-start(f32[7,16,128]{2,1,0:T(8,128)S(1)} %shard_map.89.share_ref), channel_id=1, source_target_pairs={{0,8},{8,0},{1,9},{9,1},{2,10},{10,2},{3,11},{11,3},{4,12},{12,4},... | collective-permute-start | bytes 172040 | tf_op jit(solution)/shard_map/ppermute | solution.py:581
